TPU v7x, 32 devices: a whole 2x2x4 slice. The times are simulated.
32 devices in a mesh: lat: 4 (over y, x), lon: 8 (over z, core).
Axes of the slice: x: 2, y: 2, z: 4, core: 2. Of those that a mesh axis runs over, the one named last changes fastest.
Arguments:
- innovations: float32 [25, 16384], P(None, ('lat', 'lon')), may hold values from -6 to 6
- owners: int32 [16384, 1], P(('lat', 'lon')), may hold values from 0 to 31, as said below
- prof_row: int32 [16384], P(('lat', 'lon')), may hold values from 0 to 254
- prof_col: int32 [16384], P(('lat', 'lon')), may hold values from 0 to 126
- interp_weights: float32 [4, 16384], P(None, ('lat', 'lon')), may hold values from 0.1 to 1
- model_tiles: float32 [25, 1024, 8, 128], P(None, ('lat', 'lon')), may hold values from -6 to 6
- model_ids: int32 [1, 1024], P(None, ('lat', 'lon')), may hold values from 0 to 31, as said below
- face_x: float32 [1024, 1024], P('lat', 'lon'), may hold values from 0.02 to 0.12
- face_y: float32 [1024, 1024], P('lat', 'lon'), may hold values from 0.02 to 0.12
- cross_term: float32 [1024, 1024], P('lat', 'lon'), may hold values from -0.08 to 0.08
- wet_mask: int32 [1024, 1024], P('lat', 'lon'), may hold values 0 or 1
- norm_factor: float32 [25, 1024, 1024], P(None, 'lat', 'lon'), may hold values from 0.4 to 2.5
Outputs:
- smoothed: float32 [25, 1024, 1024], P(None, 'lat', 'lon')
- profile_values: float32 [25, 16384], P(None, ('lat', 'lon'))
Inputs may be any that keep to these rules, and one draw needn't show every extreme that they name: `owners`: among the 512 profiles of one device no owner appears more than 32 times; in every draw one owner appears exactly 32 times among every device's profiles. Owners count analysis blocks in lat-major order. `model_ids`: the 32 slots of the model device at lat index i and lon index g form as many equal groups as the lon axis has devices; group j holds tiles of the analysis block at lat index i and lon index j, and every analysis block's 32 tiles appear exactly once over its lat row.
All inputs are finite; a program needn't handle non-finite values. No bound on the sum of `wet_mask` on one device may be relied on, other than what follows from the above.
Results may differ from a plain program's by a relative error of at most 0.00002.
Values sent between devices are 32-bit elements; how exact they have to be, the bound alone decides.
No kernel may reach another device: no remote copies, remote signals or barrier semaphores. Data moves between devices by JAX's collectives and lax.ppermute only.
A program may use at most 128 MiB of HBM per device.

v0:
```python
import functools
import jax
import jax.numpy as jnp
from jax import lax
from jax.experimental import pallas as pl
from jax.experimental.pallas import tpu as pltpu
from jax.sharding import PartitionSpec as P

STEPS = 10
SUB = 8
LANES = 128
FEATS = 32
PER_ROW = LANES // FEATS
GROUPS = (5, 4, 8, 8)
CHUNKS = (2, 2)
WEIGHT_ROWS = (5, 6, 12, 13)
LOC_ROW = 7
ID_ROW = 15
SMALL = 20 * 1024 * 1024
LARGE = 60 * 1024 * 1024


def group_starts():
    starts = []
    total = 0
    for count in GROUPS:
        starts.append(total)
        total += count
    return starts


def params(grant):
    return pltpu.CompilerParams(vmem_limit_bytes=grant)


def cost(micros):
    return pl.CostEstimate(flops=0, bytes_accessed=int(micros * 3.6e6), transcendentals=0)


def iota(shape, dim):
    return lax.broadcasted_iota(jnp.int32, shape, dim)


def split3(values):
    high = values.astype(jnp.bfloat16)
    rest = values - high.astype(jnp.float32)
    middle = rest.astype(jnp.bfloat16)
    low = (rest - middle.astype(jnp.float32)).astype(jnp.bfloat16)
    return high, middle, low


def route_kernel(cap, group, copies, starts, innov, weights, own_row, prow, pcol, ids, send, slot_out, pay):
    count = innov.shape[1]
    tiles = ids.shape[1]
    extra = tiles * copies
    owner = own_row[...]
    column = jnp.broadcast_to(owner.astype(jnp.float32), (SUB, count)).T[:, :1].astype(jnp.int32)
    same = column == owner
    before = iota((count, count), 0) < iota((count, count), 1)
    ones = jnp.where(same & before, 1.0, 0.0)
    rank = jnp.sum(ones, axis=0, keepdims=True).astype(jnp.int32)
    slot = owner * cap + rank
    slot_out[...] = slot
    number = iota((1, extra), 1)
    id_slot = (number // group) * cap + number % group
    pay[...] = jnp.zeros_like(pay)
    for index, count_in in enumerate(GROUPS):
        pay[index * SUB : index * SUB + count_in, :count] = innov[starts[index] : starts[index] + count_in, :]
    for corner, row in enumerate(WEIGHT_ROWS):
        pay[row : row + 1, :count] = weights[corner : corner + 1, :]
    pay[LOC_ROW : LOC_ROW + 1, :count] = (prow[...] * LANES + pcol[...]).astype(jnp.float32)
    for i in range(copies):
        at = count + i * tiles
        pay[ID_ROW : ID_ROW + 1, at : at + tiles] = ids[...].astype(jnp.float32)
    slots = jnp.concatenate([slot, id_slot], axis=1)
    values = pay[...]
    part = slots % PER_ROW
    spread = jnp.concatenate([jnp.where(part == k, values, 0.0) for k in range(PER_ROW)], axis=0)
    rows = send.shape[0]
    hot = jnp.where(iota((rows, count + extra), 0) == slots // PER_ROW, 1.0, 0.0).astype(jnp.bfloat16)
    total = None
    for piece in split3(spread):
        term = lax.dot_general(hot, piece, (((1,), (1,)), ((), ())), preferred_element_type=jnp.float32)
        total = term if total is None else total + term
    send[...] = total


def unpack_kernel(starts, recv, slot, out):
    slots = slot[...]
    rows = recv.shape[0]
    hot = jnp.where(iota((rows, slots.shape[1]), 0) == slots // PER_ROW, 1.0, 0.0).astype(jnp.bfloat16)
    total = None
    for piece in split3(recv[...]):
        term = lax.dot_general(piece, hot, (((0,), (0,)), ((), ())), preferred_element_type=jnp.float32)
        total = term if total is None else total + term
    part = slots % PER_ROW
    picked = jnp.zeros((FEATS, slots.shape[1]), jnp.float32)
    for k in range(PER_ROW):
        picked = jnp.where(part == k, total[k * FEATS : (k + 1) * FEATS], picked)
    for index, count_in in enumerate(GROUPS):
        out[starts[index] : starts[index] + count_in, :] = picked[index * SUB : index * SUB + count_in]


def turn_slots(recv, turned):
    for h in range(recv.shape[0] // LANES):
        turned[h] = recv[h * LANES : (h + 1) * LANES, :].T


def place_kernel(recv, low, high, loc_out, turned):
    rows = recv.shape[0]
    turn_slots(recv, turned)
    for k in range(PER_ROW):
        for h in range(rows // LANES):
            at = k * FEATS
            cut = slice(h * LANES, (h + 1) * LANES)
            cells = turned[h, at + LOC_ROW : at + LOC_ROW + 1, :].astype(jnp.int32)
            loc_out[k : k + 1, cut] = cells // LANES * SUB
            loc_out[PER_ROW + k : PER_ROW + k + 1, cut] = turned[h, at + ID_ROW : at + ID_ROW + 1, :].astype(jnp.int32)
    lane = iota((rows, LANES), 1)
    for k in range(PER_ROW):
        at = k * FEATS
        col = recv[:, at + LOC_ROW : at + LOC_ROW + 1].astype(jnp.int32) % LANES
        w = [recv[:, at + row : at + row + 1] for row in WEIGHT_ROWS]
        here = lane == col
        after = lane == col + 1
        low[k * rows : (k + 1) * rows, :] = jnp.where(here, w[0], jnp.where(after, w[1], 0.0))
        high[k * rows : (k + 1) * rows, :] = jnp.where(here, w[2], jnp.where(after, w[3], 0.0))


def scatter_kernel(first, loc, recv, low, high, obs, turned, odd):
    rows = recv.shape[0]
    groups = range(obs.shape[0])
    turn_slots(recv, turned)

    def clear(i, carry):
        for g in groups:
            at = pl.ds(pl.multiple_of(i * 64, 64), 64)
            obs[g, at, :] = jnp.zeros((64, LANES), jnp.float32)
            odd[g, at, :] = jnp.zeros((64, LANES), jnp.float32)
        return carry

    lax.fori_loop(0, obs.shape[1] // 64, clear, 0)

    def body(i, carry):
        h = i // PER_ROW
        k = i % PER_ROW
        size = len(groups) * SUB
        block = turned[h, pl.ds(pl.multiple_of(k * FEATS + first * SUB, SUB), size), :]
        for seat in range(0, LANES, 2):
            found = []
            for n, total in enumerate((obs, odd)):
                at = pl.multiple_of(loc[k, h * LANES + seat + n], SUB)
                lo = low[pl.ds(k * rows + h * LANES + seat + n, 1), :]
                hi = high[pl.ds(k * rows + h * LANES + seat + n, 1), :]
                for g in groups:
                    value = block[g * SUB : (g + 1) * SUB, seat + n : seat + n + 1]
                    here = total[g, pl.ds(at, SUB), :] + value * lo
                    north = total[g, pl.ds(at + SUB, SUB), :] + value * hi
                    found.append((total, g, at, here, north))
            for total, g, at, here, north in found:
                total[g, pl.ds(at, SUB), :] = here
                total[g, pl.ds(at + SUB, SUB), :] = north
        return carry

    lax.fori_loop(0, (rows // LANES) * PER_ROW, body, 0)

    def join(i, carry):
        for g in groups:
            at = pl.ds(pl.multiple_of(i * 64, 64), 64)
            obs[g, at, :] = obs[g, at, :] + odd[g, at, :]
        return carry

    lax.fori_loop(0, obs.shape[1] // 64, join, 0)


def row_at(index):
    return pl.ds(pl.multiple_of(index * SUB, SUB), SUB)


def rows_at(index, count):
    return pl.ds(pl.multiple_of(index * SUB, SUB), count * SUB)


def send_rows(field, up, down):
    edge = up.shape[1]
    total = field.shape[1]
    for g in range(field.shape[0]):
        up[g] = field[g, total - edge :, :]
        down[g] = field[g, :edge, :]


def field_kernel(begin, sizes, n_lon, group, cap, loc, lat, tiles, obs, norm_h, field, up, down, norm, sem):
    copy = pltpu.make_async_copy(norm_h.at[pl.ds(begin, sum(sizes))], norm, sem)
    copy.start()
    field[...] = jnp.zeros_like(field)
    copy.wait()

    def body(j, carry):
        done = []
        for c in range(group):
            slot = (lat[0] * n_lon + j) * cap + c
            t = loc[PER_ROW + slot % PER_ROW, slot // PER_ROW]
            own = pl.ds(pl.multiple_of(t * SUB, SUB), SUB)
            level = 0
            for g, size in enumerate(sizes):
                for l in range(size):
                    at = pl.ds(t * (SUB * SUB) + l, SUB, stride=SUB)
                    done.append((g, at, norm[level, own, :] * (obs[g, at, :] + tiles[j, level, c])))
                    level += 1
        for g, at, value in done:
            field[g, at, :] = value
        return carry

    lax.fori_loop(0, n_lon, body, 0)
    send_rows(field, up, down)


def stack_kernel(face_x, face_y, cross, wet, field, up, down):
    field[...] = jnp.zeros_like(field)
    sources = (face_x, face_y, cross, wet)

    def body(i, carry):
        values = []
        for n in range(4):
            t = i * 4 + n
            own = pl.ds(pl.multiple_of(t * SUB, SUB), SUB)
            values += [(t, l, source[own, :].astype(jnp.float32)) for l, source in enumerate(sources)]
        for t, l, value in values:
            field[0, pl.ds(t * (SUB * SUB) + l, SUB, stride=SUB), :] = value
        return carry

    lax.fori_loop(0, face_x.shape[0] // SUB // 4, body, 0)
    send_rows(field, up, down)


STRIP = 32
HALF = 2 * STRIP
SEAT = 16
SEATS = HALF // SEAT
TURNS = 10


def span_of(rows):
    return -(-(rows + 2 * STEPS) // (SEATS * TURNS)) * TURNS


def extend(ext, field, above, below):
    groups, total, _ = field.shape
    halo = STEPS * SUB
    for g in range(groups):
        ext[g, :halo, :] = above[g]
        ext[g, halo : halo + total, :] = field[g]
        ext[g, halo + total : 2 * halo + total, :] = below[g]
        ext[g, 2 * halo + total :, :] = jnp.zeros((ext.shape[1] - 2 * halo - total, LANES), jnp.float32)


def edges_kernel(field, above, below, strips, east, west, ext):
    groups = field.shape[0]
    extend(ext, field, above, below)
    span = east.shape[0] // SUB
    lane = iota((SUB, LANES), 1)
    place = lane % HALF

    def body(i, carry):
        for n in range(TURNS):
            m = i * TURNS + n
            to_east = None
            to_west = None
            for q in range(SEATS):
                first = ext[0, row_at(q * span + m), :]
                second = pltpu.roll(ext[groups - 1, row_at(q * span + m), :], HALF, 1)
                left = jnp.where(lane < HALF, first, second)
                right = jnp.where(lane < HALF, second, first)
                row = jnp.where(place < STRIP, pltpu.roll(left, STEPS, 1), pltpu.roll(right, HALF - STEPS, 1))
                strips[row_at(q * span + m), :] = row
                right = pltpu.roll(right, SEAT * q + SEAT, 1)
                if q:
                    left = pltpu.roll(left, SEAT * q, 1)
                mine = place // SEAT == q
                to_east = right if q == 0 else jnp.where(mine, right, to_east)
                to_west = left if q == 0 else jnp.where(mine, left, to_west)
            east[row_at(m), :] = to_east
            west[row_at(m), :] = to_west
        return carry

    lax.fori_loop(0, span // TURNS, body, 0)


def build_strips(win, strips, from_west, from_east):
    span = from_west.shape[0] // SUB
    place = iota((SUB, LANES), 1) % HALF

    def body(i, carry):
        for n in range(TURNS):
            m = i * TURNS + n
            west = from_west[row_at(m), :]
            east = from_east[row_at(m), :]
            for q in range(SEATS):
                a = pltpu.roll(west, (STEPS - SEAT - SEAT * q) % LANES, 1)
                b = pltpu.roll(east, (HALF - STEPS - SEAT * q) % LANES, 1)
                row = strips[row_at(q * span + m), :]
                row = jnp.where(place < STEPS, a, jnp.where(place < HALF - STEPS, row, b))
                win[row_at(q * span + m), :] = row
        return carry

    lax.fori_loop(0, span // TURNS, body, 0)
    first = SEATS * span * SUB
    win[first:, :] = jnp.zeros((win.shape[0] - first, LANES), jnp.float32)


def fill_coef(coef, win):
    rows = coef.shape[1]

    def body(i, carry):
        done = []
        for n in range(12):
            b = i * 12 + n
            base = b * (SUB * SUB)
            at = pl.ds(pl.multiple_of(b * SUB, SUB), SUB)
            fx, fy, ct, wet = (win[pl.ds(base + s, SUB, stride=SUB), :] for s in range(4))
            wet_n = win[pl.ds(base + SUB + 3, SUB, stride=SUB), :]
            x = fx * wet * pltpu.roll(wet, LANES - 1, 1)
            xw = pltpu.roll(x, 1, 1)
            y = fy * wet * wet_n
            twist = 0.25 * ct * wet
            for c, value in enumerate((1.0 - x - xw, x, xw, y, twist)):
                done.append((c, at, value))
        for c, at, value in done:
            coef[c, at, :] = value
        return carry

    lax.fori_loop(0, rows // (12 * SUB), body, 0)


def own_coef_kernel(field, above, below, coef, ext):
    extend(ext, field, above, below)
    fill_coef(coef, ext.at[0])


def strip_coef_kernel(strips, from_west, from_east, coef, win):
    build_strips(win, strips, from_west, from_east)
    fill_coef(coef, win)


BY_MATMUL = 0.25


def fill_shift(shift):
    row = iota(shift.shape, 0) % LANES
    col = iota(shift.shape, 1)
    near = jnp.where(col < LANES, col + 1, col + LANES - 1) % LANES
    shift[...] = jnp.where(row == near, 1.0, 0.0).astype(jnp.bfloat16)


def advance(source, target, planes, weight, shift, rows):
    last = rows + 2 * STEPS + 4
    unroll = last // planes
    blocks = last // unroll
    split = int(unroll * BY_MATMUL)

    def rolled(w, index):
        cells = source[w, row_at(index), :]
        east = pltpu.roll(cells, LANES - 1, 1)
        west = pltpu.roll(cells, 1, 1)
        return cells, east, west, east - west

    def shifted_rows(w, first):
        cells = source[w, rows_at(first, split), :]
        high = cells.astype(jnp.bfloat16)
        low = (cells - high.astype(jnp.float32)).astype(jnp.bfloat16)
        both = jnp.concatenate([high, low], axis=1)
        return jnp.dot(both, shift[...], preferred_element_type=jnp.float32)

    y_first = weight(3, 0)
    state = []
    for w in range(planes):
        before = rolled(w, 0)
        now = rolled(w, 1)
        state.append((now, before[3], y_first * (now[0] - before[0])))

    def block(b, state):
        base = 1 + b * unroll
        state = list(state)
        sides = [shifted_rows(w, base + 1) for w in range(planes)]
        for u in range(unroll):
            weights = [weight(c, base + u) for c in range(5)]
            for w in range(planes):
                (cells, east, west, slope), slope_s, flux_s = state[w]
                if u < split:
                    cells_n = source[w, row_at(base + u + 1), :]
                    east_n = sides[w][u * SUB : (u + 1) * SUB, :LANES]
                    west_n = sides[w][u * SUB : (u + 1) * SUB, LANES:]
                    ahead = (cells_n, east_n, west_n, east_n - west_n)
                else:
                    ahead = rolled(w, base + u + 1)
                flux = weights[3] * (ahead[0] - cells)
                target[w, row_at(base + u), :] = (
                    (weights[0] * cells + weights[1] * east)
                    + (weights[2] * west + (flux - flux_s))
                    + weights[4] * (ahead[3] - slope_s)
                )
                state[w] = (ahead, slope, flux)
        return tuple(state)

    lax.fori_loop(0, blocks, block, tuple(state))


def diffuse(win, other, planes, coef, shift, rows):
    fill_shift(shift)

    def weight(c, index):
        return coef[c, pl.ds(index, 1), :]

    def two(t, carry):
        advance(win, other, planes, weight, shift, rows)
        advance(other, win, planes, weight, shift, rows)
        return carry

    for w in range(planes):
        other[w, :SUB, :] = jnp.zeros((SUB, LANES), jnp.float32)
        other[w, other.shape[1] - SUB * SUB :, :] = jnp.zeros((SUB * SUB, LANES), jnp.float32)
    lax.fori_loop(0, STEPS // 2, two, 0)


def own_kernel(field, above, below, coef, mid, win, other, shift):
    groups = field.shape[0]
    rows = mid.shape[1] // SUB
    halo = STEPS * SUB
    extend(win, field, above, below)
    diffuse(win, other, groups, coef, shift, rows)
    for g in range(groups):
        mid[g] = win[g, halo : halo + rows * SUB, :]


MERGE = 32


def strip_kernel(sizes, begin, aliased, earlier, *refs):
    loc, strips, from_west, from_east, coef, mid, low, high, norm_h = refs[:9]
    parts = refs[9 + aliased : 9 + aliased + earlier]
    refs = refs[9 + aliased + earlier :]
    if earlier:
        out_h, packed, sampled, turned = refs[:4]
    else:
        out_h, sampled = refs[:2]
    win, other, shift, smooth, norm, out, sems = refs[-7:]
    groups = mid.shape[0]
    rows = mid.shape[1] // SUB
    levels = pl.ds(begin, sum(sizes))
    copy = pltpu.make_async_copy(norm_h.at[levels], norm, sems.at[0])
    copy.start()
    build_strips(win.at[0], strips, from_west, from_east)
    diffuse(win, other, 1, coef, shift, rows)
    copy.wait()
    lane = iota((SUB, LANES), 1)
    outer = LANES - STEPS

    def merge(b, carry):
        for u in range(MERGE):
            at = row_at(b * MERGE + u)
            strip = win[0, row_at(b * MERGE + u + STEPS), :]
            west = pltpu.roll(strip, outer, 1)
            east = pltpu.roll(strip, HALF + STEPS, 1)
            cells = mid[0, at, :]
            smooth[0, at, :] = jnp.where(lane < STEPS, west, jnp.where(lane < outer, cells, east))
            if groups == 2:
                both = pltpu.roll(jnp.where(lane < HALF, east, west), HALF, 1)
                cells = mid[1, at, :]
                smooth[1, at, :] = jnp.where((lane < STEPS) | (lane >= outer), both, cells)
        return carry

    lax.fori_loop(0, rows // MERGE, merge, 0)

    def scale(i, carry):
        done = []
        for n in range(4):
            b = i * 4 + n
            own = pl.ds(pl.multiple_of(b * SUB, SUB), SUB)
            level = 0
            for g, size in enumerate(sizes):
                for l in range(size):
                    at = pl.ds(b * (SUB * SUB) + l, SUB, stride=SUB)
                    done.append((g, at, level, own, smooth[g, at, :] * norm[level, own, :]))
                    level += 1
        for g, at, level, own, value in done:
            out[level, own, :] = value
            smooth[g, at, :] = value
        return carry

    lax.fori_loop(0, rows // (4 * SUB), scale, 0)
    back = pltpu.make_async_copy(out, out_h.at[levels], sems.at[1])
    back.start()
    count = low.shape[0] // PER_ROW
    halves = count // LANES

    def samples(i, carry):
        h = i // PER_ROW
        k = i % PER_ROW
        kept = [[jnp.zeros((SUB, LANES), jnp.float32)] * 4 for _ in range(groups)]
        for seat in range(LANES):
            at = pl.multiple_of(loc[k, h * LANES + seat], SUB)
            lo = low[pl.ds(k * count + h * LANES + seat, 1), :]
            hi = high[pl.ds(k * count + h * LANES + seat, 1), :]
            for g in range(groups):
                value = smooth[g, pl.ds(at, SUB), :] * lo + smooth[g, pl.ds(at + SUB, SUB), :] * hi
                total = jnp.sum(value, axis=1, keepdims=True)
                kept[g][seat % 4] = jnp.where(lane == seat, total, kept[g][seat % 4])
        for g in range(groups):
            a, b, c, d = kept[g]
            sampled[h, g, row_at(k), :] = (a + b) + (c + d)
        return carry

    lax.fori_loop(0, halves * PER_ROW, samples, 0)
    if earlier:
        pack_samples(parts + (sampled,), packed, turned)
    back.wait()


def pack_samples(parts, out, turned):
    for h in range(turned.shape[0]):
        index = 0
        for part in parts:
            for g in range(part.shape[1]):
                for k in range(PER_ROW):
                    at = k * FEATS + index * SUB
                    turned[h, at : at + SUB, :] = part[h, g, k * SUB : (k + 1) * SUB, :]
                index += 1
        out[h * LANES : (h + 1) * LANES, :] = turned[h].T


def exchange_rows(up, down, n_lat):
    pairs = [(i, i + 1) for i in range(n_lat - 1)]
    back = [(i + 1, i) for i in range(n_lat - 1)]
    return lax.ppermute(up, "lat", pairs), lax.ppermute(down, "lat", back)


def exchange_columns(east, west, n_lon):
    pairs = [(i, (i + 1) % n_lon) for i in range(n_lon)]
    back = [((i + 1) % n_lon, i) for i in range(n_lon)]
    return lax.ppermute(east, "lon", pairs), lax.ppermute(west, "lon", back)


def on_device(
    innovations,
    owners,
    prof_row,
    prof_col,
    interp_weights,
    model_tiles,
    model_ids,
    face_x,
    face_y,
    cross_term,
    wet_mask,
    norm_factor,
):
    n_lat = lax.axis_size("lat")
    n_lon = lax.axis_size("lon")
    devices = n_lat * n_lon
    levels, lat_cells, lon_cells = norm_factor.shape
    tiles = model_tiles.shape[1]
    group = tiles // n_lon
    count = innovations.shape[1]
    cap = 2 * count // devices
    slots = devices * cap
    rows = slots // PER_ROW
    starts = group_starts()
    f32 = jnp.float32
    lat = lax.axis_index("lat").reshape(1)
    both = ("lat", "lon")
    span = span_of(lat_cells)
    ext_rows = SEATS * span
    win_rows = ext_rows + SUB

    def arrays(*shapes):
        return tuple(jax.ShapeDtypeStruct(shape, f32) for shape in shapes)

    def call(kernel, out_shape, micros, name, grant=SMALL, **kwargs):
        return pl.pallas_call(
            kernel,
            out_shape=out_shape,
            compiler_params=params(grant),
            cost_estimate=cost(micros),
            name=name,
            **kwargs,
        )

    def after(value, *others):
        return lax.optimization_barrier((value,) + others)[0]

    def tile_exchange(chunk, *others):
        first = sum(CHUNKS[:chunk])
        begin = starts[first]
        size = sum(GROUPS[first : first + CHUNKS[chunk]])
        piece = model_tiles[begin : begin + size].reshape(size, n_lon, group, SUB, LANES)
        piece = jnp.transpose(piece, (1, 0, 2, 3, 4))
        if others:
            piece = after(piece, *others)
        return lax.all_to_all(piece, "lon", split_axis=0, concat_axis=0, tiled=True)

    def halo(field, up, down, groups):
        above, below = exchange_rows(up, down, n_lat)
        strips, east, west = call(
            edges_kernel,
            arrays((ext_rows * SUB, LANES), (span * SUB, LANES), (span * SUB, LANES)),
            3,
            "edges",
            scratch_shapes=[pltpu.VMEM((groups, ext_rows * SUB, LANES), f32)],
        )(field, above, below)
        return (field, above, below, strips) + exchange_columns(east, west, n_lon)

    def field_shapes(groups):
        return arrays(
            (groups, lat_cells * SUB, LANES),
            (groups, STEPS * SUB, LANES),
            (groups, STEPS * SUB, LANES),
        )

    send, slot = call(
        functools.partial(route_kernel, cap, group, n_lat, starts),
        (jax.ShapeDtypeStruct((rows, LANES), f32), jax.ShapeDtypeStruct((1, count), jnp.int32)),
        3,
        "route",
        LARGE,
        scratch_shapes=[pltpu.VMEM((FEATS, count + devices * group), f32)],
    )(
        innovations,
        interp_weights,
        owners.reshape(1, count),
        prof_row.reshape(1, count),
        prof_col.reshape(1, count),
        model_ids,
    )
    stacked = call(stack_kernel, field_shapes(1), 3, "stack")(face_x, face_y, cross_term, wet_mask)
    stack, above, below, coef_strips, coef_west, coef_east = halo(*stacked, 1)
    own_coef = call(
        own_coef_kernel,
        arrays((5, win_rows, LANES))[0],
        3,
        "own_coef",
        scratch_shapes=[pltpu.VMEM((1, (win_rows + SUB) * SUB, LANES), f32)],
    )(stack, above, below)
    recv = lax.all_to_all(
        send.reshape(devices, rows // devices, LANES), both, split_axis=0, concat_axis=0, tiled=True
    ).reshape(rows, LANES)
    pieces = [tile_exchange(0, recv, stacked[0])]

    smem = pl.BlockSpec(memory_space=pltpu.SMEM)
    vmem = pl.BlockSpec(memory_space=pltpu.VMEM)
    hbm = pl.BlockSpec(memory_space=pltpu.HBM)
    turned = pltpu.VMEM((rows // LANES, LANES, LANES), f32)
    low, high, loc = call(
        place_kernel,
        arrays((slots, LANES), (slots, LANES)) + (jax.ShapeDtypeStruct((2 * PER_ROW, rows), jnp.int32),),
        2,
        "place",
        LARGE,
        scratch_shapes=[turned],
    )(recv)

    def scatter(chunk, grant):
        first = sum(CHUNKS[:chunk])
        return call(
            functools.partial(scatter_kernel, first),
            arrays((CHUNKS[chunk], lat_cells * SUB, LANES))[0],
            9,
            "scatter",
            grant,
            in_specs=[smem, vmem, vmem, vmem],
            scratch_shapes=[turned, pltpu.VMEM((CHUNKS[chunk], lat_cells * SUB, LANES), f32)],
        )(loc, recv, low, high)

    observed = [scatter(0, LARGE), scatter(1, SMALL)]
    pieces.append(tile_exchange(1, pieces[0], observed[0], own_coef, coef_strips))
    shift_space = pltpu.VMEM((2 * LANES, 2 * LANES), jnp.bfloat16)
    smoothed = None
    sampled = []
    first = 0
    for chunk, groups in enumerate(CHUNKS):
        sizes = GROUPS[first : first + groups]
        begin = starts[first]
        own_levels = (sum(sizes), lat_cells, LANES)
        field = call(
            functools.partial(field_kernel, begin, sizes, n_lon, group, cap),
            field_shapes(groups),
            4,
            "field",
            in_specs=[smem, smem, vmem, vmem, hbm],
            scratch_shapes=[pltpu.VMEM(own_levels, f32), pltpu.SemaphoreType.DMA],
        )(loc, lat, pieces[chunk], observed[chunk], norm_factor)
        field, above, below, strips, from_west, from_east = halo(*field, groups)
        mid_shape = (groups, lat_cells * SUB, LANES)
        win_shape = (groups, win_rows * SUB, LANES)
        mid = call(
            own_kernel,
            arrays(mid_shape)[0],
            6 * groups,
            "own",
            scratch_shapes=[pltpu.VMEM(win_shape, f32), pltpu.VMEM(win_shape, f32), shift_space],
        )(after(field, strips), above, below, own_coef)
        if chunk == 0:
            strip_coef = call(
                strip_coef_kernel,
                arrays((5, win_rows, LANES))[0],
                3,
                "strip_coef",
                scratch_shapes=[pltpu.VMEM(((win_rows + SUB) * SUB, LANES), f32)],
            )(after(coef_strips, mid, *observed[1:]), coef_west, coef_east)
        operands = [loc, strips, from_west, from_east, strip_coef, mid, low, high, norm_factor]
        specs = [smem] + [vmem] * 7 + [hbm]
        aliases = {}
        if smoothed is not None:
            aliases = {len(operands): 0}
            operands.append(smoothed)
            specs.append(hbm)
        last = chunk + 1 == len(CHUNKS)
        earlier = sampled if last else []
        part_shape = (rows // LANES, groups, PER_ROW * SUB, LANES)
        gathered = [pltpu.VMEM(part_shape, f32), pltpu.VMEM((rows // LANES, LANES, LANES), f32)]
        smoothed, part = call(
            functools.partial(strip_kernel, sizes, begin, len(aliases), len(earlier)),
            arrays(norm_factor.shape, (rows, LANES) if earlier else part_shape),
            12,
            "strips",
            in_specs=specs + [vmem] * len(earlier),
            out_specs=(hbm, vmem),
            scratch_shapes=(gathered if earlier else [])
            + [
                pltpu.VMEM((1,) + win_shape[1:], f32),
                pltpu.VMEM((1,) + win_shape[1:], f32),
                shift_space,
                pltpu.VMEM(mid_shape, f32),
                pltpu.VMEM(own_levels, f32),
                pltpu.VMEM(own_levels, f32),
                pltpu.SemaphoreType.DMA((2,)),
            ],
            input_output_aliases=aliases,
        )(*operands, *earlier)
        sampled.append(part)
        first += groups
        if not last:
            pieces[chunk + 1] = after(pieces[chunk + 1], part)

    back = sampled[-1]
    returned = lax.all_to_all(
        back.reshape(devices, rows // devices, LANES), both, split_axis=0, concat_axis=0, tiled=True
    ).reshape(rows, LANES)
    profile_values = call(
        functools.partial(unpack_kernel, starts),
        arrays((levels, count))[0],
        1,
        "unpack",
    )(returned, slot)
    return (smoothed, profile_values)


def solution(mesh):
    in_specs = (
        P(None, ("lat", "lon")),
        P(("lat", "lon"), None),
        P(("lat", "lon")),
        P(("lat", "lon")),
        P(None, ("lat", "lon")),
        P(None, ("lat", "lon"), None, None),
        P(None, ("lat", "lon")),
        P("lat", "lon"),
        P("lat", "lon"),
        P("lat", "lon"),
        P("lat", "lon"),
        P(None, "lat", "lon"),
    )
    out_specs = (P(None, "lat", "lon"), P(None, ("lat", "lon")))
    return jax.shard_map(
        on_device, mesh=mesh, in_specs=in_specs, out_specs=out_specs, check_vma=False
    )
```

profile of v0, /device:TPU:0, one launch (start us, length us, event | category | flops | bytes accessed | tf_op | source)
XLA Modules:
  0.0 198.0 jit_solution(263202568393259139)
XLA Ops:
  3.1 7.3 %all-to-all-start = ((f32[32,8,128]{2,1,0:T(8,128)}), f32[32,8,128]{2,1,0:T(8,128)S(1)}, u32[]{:S(2)}, u32[]{:S(2)}) async-start(f32[32,8,128]{2,1,0:T(8,128)} %bitcast.25), calls=%async_computation | async-start | bytes 262144 | tf_op jit(solution)/shard_map/all_to_all | solution.py:643
  11.9 6.7 %all-to-all-done = f32[32,8,128]{2,1,0:T(8,128)S(1)} async-done(((f32[32,8,128]{2,1,0:T(8,128)}), f32[32,8,128]{2,1,0:T(8,128)S(1)}, u32[]{:S(2)}, u32[]{:S(2)}) %all-to-all-start) | async-done | bytes 131104 | tf_op jit(solution)/shard_map/all_to_all | solution.py:643
  18.6 3.6 %all-to-all-start.1 = ((f32[8,9,4,8,128]{4,3,2,1,0:T(8,128)}), f32[8,9,4,8,128]{4,3,2,1,0:T(8,128)S(1)}, u32[]{:S(2)}, u32[]{:S(2)}) async-start(f32[8,9,4,8,128]{4,3,2,1,0:T(8,128)} %bitcast.24), calls=%async_computation.1 | async-start | bytes 2359296 | tf_op jit(solution)/shard_map/all_to_all | solution.py:599
  22.1 2.8 %collective-permute-start = (f32[1,80,128]{2,1,0:T(8,128)S(1)}, f32[1,80,128]{2,1,0:T(8,128)S(1)}, u32[]{:S(2)}, u32[]{:S(2)}) collective-permute-start(f32[1,80,128]{2,1,0:T(8,128)S(1)} %get-tuple-element.41), channel_id=1, source_target_pairs={{0,8},{8,16},{16,24},{1,9},{9,17},{17,25},{2,10},{10,18},{18,26},{... | collective-permute-start | bytes 122888 | tf_op jit(solution)/shard_map/ppermute | solution.py:534
  28.1 2.9 %collective-permute-done.1.below = f32[1,80,128]{2,1,0:T(8,128)S(1)} collective-permute-done((f32[1,80,128]{2,1,0:T(8,128)S(1)}, f32[1,80,128]{2,1,0:T(8,128)S(1)}, u32[]{:S(2)}, u32[]{:S(2)}) %collective-permute-start.1) | collective-permute-done | bytes 40992 | tf_op jit(solution)/shard_map/ppermute | solution.py:534
  32.4 7.9 %edges.3 = (f32[2240,128]{1,0:T(8,128)S(1)}, f32[560,128]{1,0:T(8,128)S(1)}, f32[560,128]{1,0:T(8,128)S(1)}) custom-call(f32[1,2048,128]{2,1,0:T(8,128)S(1)} %get-tuple-element.37.field, f32[1,80,128]{2,1,0:T(8,128)S(1)} %collective-permute-done.above, f32[1,80,128]{2,1,0:T(8,128)S(1)} %collective-permute-done.1.below), custom_call_target="tpu_custom_call" | custom-call | bytes 10800000 | tf_op jit(solution)/shard_map/edges/pallas_call | solution.py:603
  42.8 2.8 %place.1 = (f32[1024,128]{1,0:T(8,128)}, f32[1024,128]{1,0:T(8,128)}, s32[8,256]{1,0:T(8,128)}) custom-call(f32[256,128]{1,0:T(8,128)} %bitcast.16), custom_call_target="tpu_custom_call" | custom-call | bytes 7200000 | tf_op jit(solution)/shard_map/place/pallas_call | solution.py:652
  45.5 7.6 %scatter.2.obs = f32[2,2048,128]{2,1,0:T(8,128)} custom-call(s32[8,256]{1,0:T(8,128)} %get-tuple-element.36.loc.refs_0_, f32[256,128]{1,0:T(8,128)} %bitcast.17, f32[1024,128]{1,0:T(8,128)} %get-tuple-element.39.low.refs_6_, f32[1024,128]{1,0:T(8,128)} %get-tuple-element.40.high.refs_7_), custom_call_target="tpu_custom_call" | custom-call | bytes 32400000 | tf_op jit(solution)/shard_map/scatter/pallas_call | solution.py:663
  54.2 5.3 %all-to-all-start.2 = ((f32[8,16,4,8,128]{4,3,2,1,0:T(8,128)}), f32[8,16,4,8,128]{4,3,2,1,0:T(8,128)}, u32[]{:S(2)}, u32[]{:S(2)}) async-start(f32[8,16,4,8,128]{4,3,2,1,0:T(8,128)} %bitcast.21), calls=%async_computation.2 | async-start | bytes 4194304 | tf_op jit(solution)/shard_map/all_to_all | solution.py:599
  64.1 4.4 %collective-permute-start.2 = (f32[2,80,128]{2,1,0:T(8,128)S(1)}, f32[2,80,128]{2,1,0:T(8,128)S(1)}, u32[]{:S(2)}, u32[]{:S(2)}) collective-permute-start(f32[2,80,128]{2,1,0:T(8,128)S(1)} %get-tuple-element.46), channel_id=1, source_target_pairs={{0,8},{8,16},{16,24},{1,9},{9,17},{17,25},{2,10},{10,18},{18,26},{... | collective-permute-start | bytes 245768 | tf_op jit(solution)/shard_map/ppermute | solution.py:534
  70.1 3.3 %collective-permute-start.7 = (f32[560,128]{1,0:T(8,128)S(1)}, f32[560,128]{1,0:T(8,128)S(1)}, u32[]{:S(2)}, u32[]{:S(2)}) collective-permute-start(f32[560,128]{1,0:T(8,128)S(1)} %copy-done.26), channel_id=1, source_target_pairs={{1,0},{2,1},{3,2},{4,3},{5,4},{6,5},{7,6},{0,7},{9,8},{10,9},{11,1... | collective-permute-start | bytes 860168 | tf_op jit(solution)/shard_map/ppermute | solution.py:540
  75.0 7.9 %edges.4 = (f32[2240,128]{1,0:T(8,128)S(1)}, f32[560,128]{1,0:T(8,128)S(1)}, f32[560,128]{1,0:T(8,128)S(1)}) custom-call(f32[2,2048,128]{2,1,0:T(8,128)S(1)} %get-tuple-element.51.field, f32[2,80,128]{2,1,0:T(8,128)S(1)} %collective-permute-done.2.above, f32[2,80,128]{2,1,0:T(8,128)S(1)} %collective-permute-done.3.below), custom_call_target="tpu_custom_call" | custom-call | bytes 10800000 | tf_op jit(solution)/shard_map/edges/pallas_call | solution.py:603
  83.0 3.5 %collective-permute-start.5 = (f32[560,128]{1,0:T(8,128)S(1)}, f32[560,128]{1,0:T(8,128)S(1)}, u32[]{:S(2)}, u32[]{:S(2)}) collective-permute-start(f32[560,128]{1,0:T(8,128)S(1)} %get-tuple-element.50), channel_id=1, source_target_pairs={{1,0},{2,1},{3,2},{4,3},{5,4},{6,5},{7,6},{0,7},{9,8},{10,9},{11,1... | collective-permute-start | bytes 860168 | tf_op jit(solution)/shard_map/ppermute | solution.py:540
  86.5 5.7 %scatter.3.obs = f32[2,2048,128]{2,1,0:T(8,128)S(1)} custom-call(s32[8,256]{1,0:T(8,128)S(1)} %copy-done.19, f32[256,128]{1,0:T(8,128)S(1)} %bitcast.18, f32[1024,128]{1,0:T(8,128)S(1)} %copy-done.4, f32[1024,128]{1,0:T(8,128)S(1)} %copy-done.6), custom_call_target="tpu_custom_call" | custom-call | bytes 32400000 | tf_op jit(solution)/shard_map/scatter/pallas_call | solution.py:663
  93.6 13.7 %own.2.refs_5_ = f32[2,2048,128]{2,1,0:T(8,128)S(1)} custom-call(f32[2,2048,128]{2,1,0:T(8,128)S(1)} %get-tuple-element.51.field, f32[2,80,128]{2,1,0:T(8,128)S(1)} %collective-permute-done.2.above, f32[2,80,128]{2,1,0:T(8,128)S(1)} %collective-permute-done.3.below, f32[5,288,128]{2,1,0:T(8,128)S(1)} %copy-done.9), custom_call_target="tpu_custom_call" | custom-call | bytes 43200000 | tf_op jit(solution)/shard_map/own/pallas_call | solution.py:694
  110.1 13.6 %strips.2 = (f32[25,256,128]{2,1,0:T(8,128)}, f32[2,2,32,128]{3,2,1,0:T(8,128)S(1)}) custom-call(s32[8,256]{1,0:T(8,128)S(1)} %copy-done.19, f32[2240,128]{1,0:T(8,128)S(1)} %get-tuple-element.48.refs_1_, f32[560,128]{1,0:T(8,128)S(1)} %collective-permute-done.4.refs_2_, f32[560,128]{1,0:T(8,128)S(1)} %collective-permute-done.5.refs_3_, ...), custom_call_target="tpu_custom_call" | custom-call | bytes 43200000 | tf_op jit(solution)/shard_map/strips/pallas_call | solution.py:720
  126.1 2.8 %field.3 = (f32[2,2048,128]{2,1,0:T(8,128)S(1)}, f32[2,80,128]{2,1,0:T(8,128)S(1)}, f32[2,80,128]{2,1,0:T(8,128)S(1)}) custom-call(s32[8,256]{1,0:T(8,128)S(1)} %copy-done.19, s32[1]{0:T(128)} %bitcast.5.lat, f32[8,16,4,8,128]{4,3,2,1,0:T(8,128)} %all-to-all-done.2.tiles, f32[2,2048,128]{2,1,0:T(8,128)S(1)} %copy-done.2, f32[25,256,128]{2,1,0:T(8,128)S(1)} %copy-done), custom_call_target="tpu_custom_call" | custom-call | bytes 14400000 | tf_op jit(solution)/shard_map/field/pallas_call | solution.py:683
  129.0 4.4 %collective-permute-start.8 = (f32[2,80,128]{2,1,0:T(8,128)S(1)}, f32[2,80,128]{2,1,0:T(8,128)S(1)}, u32[]{:S(2)}, u32[]{:S(2)}) collective-permute-start(f32[2,80,128]{2,1,0:T(8,128)S(1)} %get-tuple-element.58), channel_id=1, source_target_pairs={{0,8},{8,16},{16,24},{1,9},{9,17},{17,25},{2,10},{10,18},{18,26},{... | collective-permute-start | bytes 245768 | tf_op jit(solution)/shard_map/ppermute | solution.py:534
  135.5 4.3 %collective-permute-done.9.below = f32[2,80,128]{2,1,0:T(8,128)S(1)} collective-permute-done((f32[2,80,128]{2,1,0:T(8,128)S(1)}, f32[2,80,128]{2,1,0:T(8,128)S(1)}, u32[]{:S(2)}, u32[]{:S(2)}) %collective-permute-start.9) | collective-permute-done | bytes 81952 | tf_op jit(solution)/shard_map/ppermute | solution.py:534
  139.8 7.9 %edges.5 = (f32[2240,128]{1,0:T(8,128)S(1)}, f32[560,128]{1,0:T(8,128)S(1)}, f32[560,128]{1,0:T(8,128)S(1)}) custom-call(f32[2,2048,128]{2,1,0:T(8,128)S(1)} %get-tuple-element.63.field, f32[2,80,128]{2,1,0:T(8,128)S(1)} %collective-permute-done.8.above, f32[2,80,128]{2,1,0:T(8,128)S(1)} %collective-permute-done.9.below), custom_call_target="tpu_custom_call" | custom-call | bytes 10800000 | tf_op jit(solution)/shard_map/edges/pallas_call | solution.py:603
  147.8 3.5 %collective-permute-start.11 = (f32[560,128]{1,0:T(8,128)S(1)}, f32[560,128]{1,0:T(8,128)S(1)}, u32[]{:S(2)}, u32[]{:S(2)}) collective-permute-start(f32[560,128]{1,0:T(8,128)S(1)} %get-tuple-element.62), channel_id=1, source_target_pairs={{1,0},{2,1},{3,2},{4,3},{5,4},{6,5},{7,6},{0,7},{9,8},{10,9},{11,1... | collective-permute-start | bytes 860168 | tf_op jit(solution)/shard_map/ppermute | solution.py:540
  151.3 13.7 %own.3.refs_5_ = f32[2,2048,128]{2,1,0:T(8,128)S(1)} custom-call(f32[2,2048,128]{2,1,0:T(8,128)S(1)} %get-tuple-element.63.field, f32[2,80,128]{2,1,0:T(8,128)S(1)} %collective-permute-done.8.above, f32[2,80,128]{2,1,0:T(8,128)S(1)} %collective-permute-done.9.below, f32[5,288,128]{2,1,0:T(8,128)S(1)} %copy-done.10), custom_call_target="tpu_custom_call" | custom-call | bytes 43200000 | tf_op jit(solution)/shard_map/own/pallas_call | solution.py:694
  165.1 13.9 %strips.3 = (f32[25,256,128]{2,1,0:T(8,128)}, f32[256,128]{1,0:T(8,128)S(1)}) custom-call(s32[8,256]{1,0:T(8,128)S(1)} %copy-done.19, f32[2240,128]{1,0:T(8,128)S(1)} %get-tuple-element.60.refs_1_, f32[560,128]{1,0:T(8,128)S(1)} %collective-permute-done.10.refs_2_, f32[560,128]{1,0:T(8,128)S(1)} %collective-permute-done.11.refs_3_, ...), custom_call_target="tpu_custom_call", output_to_operand_aliasing={{0}: (9, {})} | custom-call | bytes 43200000 | tf_op jit(solution)/shard_map/strips/pallas_call | solution.py:720
  179.0 18.0 %all_to_all.20 = f32[32,8,128]{2,1,0:T(8,128)S(1)} all-to-all(f32[32,8,128]{2,1,0:T(8,128)S(1)} %bitcast.20), channel_id=1, replica_groups=mesh['lat'=4,'lon'=8] {'lat','lon'}, dimensions={0} | all-to-all | bytes 262144 | tf_op jit(solution)/shard_map/all_to_all | solution.py:745
  (88 shorter events, 29.4 us)
Async XLA Ops:
  3.1 15.5 %all-to-all-start = ((f32[32,8,128]{2,1,0:T(8,128)}), f32[32,8,128]{2,1,0:T(8,128)S(1)}, u32[]{:S(2)}, u32[]{:S(2)}) async-start(f32[32,8,128]{2,1,0:T(8,128)} %bitcast.25), calls=%async_computation | async-start | bytes 262144 | tf_op jit(solution)/shard_map/all_to_all | solution.py:643
  18.6 34.6 %all-to-all-start.1 = ((f32[8,9,4,8,128]{4,3,2,1,0:T(8,128)}), f32[8,9,4,8,128]{4,3,2,1,0:T(8,128)S(1)}, u32[]{:S(2)}, u32[]{:S(2)}) async-start(f32[8,9,4,8,128]{4,3,2,1,0:T(8,128)} %bitcast.24), calls=%async_computation.1 | async-start | bytes 2359296 | tf_op jit(solution)/shard_map/all_to_all | solution.py:599
  22.1 6.0 %collective-permute-start = (f32[1,80,128]{2,1,0:T(8,128)S(1)}, f32[1,80,128]{2,1,0:T(8,128)S(1)}, u32[]{:S(2)}, u32[]{:S(2)}) collective-permute-start(f32[1,80,128]{2,1,0:T(8,128)S(1)} %get-tuple-element.41), channel_id=1, source_target_pairs={{0,8},{8,16},{16,24},{1,9},{9,17},{17,25},{2,10},{10,18},{18,26},{... | collective-permute-start | bytes 122888 | tf_op jit(solution)/shard_map/ppermute | solution.py:534
  24.9 6.0 %collective-permute-start.1 = (f32[1,80,128]{2,1,0:T(8,128)S(1)}, f32[1,80,128]{2,1,0:T(8,128)S(1)}, u32[]{:S(2)}, u32[]{:S(2)}) collective-permute-start(f32[1,80,128]{2,1,0:T(8,128)S(1)} %get-tuple-element.42), channel_id=1, source_target_pairs={{8,0},{16,8},{24,16},{9,1},{17,9},{25,17},{10,2},{18,10},{26,18},{... | collective-permute-start | bytes 122888 | tf_op jit(solution)/shard_map/ppermute | solution.py:534
  54.2 70.3 %all-to-all-start.2 = ((f32[8,16,4,8,128]{4,3,2,1,0:T(8,128)}), f32[8,16,4,8,128]{4,3,2,1,0:T(8,128)}, u32[]{:S(2)}, u32[]{:S(2)}) async-start(f32[8,16,4,8,128]{4,3,2,1,0:T(8,128)} %bitcast.21), calls=%async_computation.2 | async-start | bytes 4194304 | tf_op jit(solution)/shard_map/all_to_all | solution.py:599
  64.0 22.5 %copy-start.4 = (f32[1024,128]{1,0:T(8,128)S(1)}, f32[1024,128]{1,0:T(8,128)}, u32[]{:S(2)}) copy-start(f32[1024,128]{1,0:T(8,128)} %get-tuple-element.39.low.refs_6_) | copy-start | bytes 1572868
  64.0 22.5 %copy-start.6 = (f32[1024,128]{1,0:T(8,128)S(1)}, f32[1024,128]{1,0:T(8,128)}, u32[]{:S(2)}) copy-start(f32[1024,128]{1,0:T(8,128)} %get-tuple-element.40.high.refs_7_) | copy-start | bytes 1572868
  64.1 22.4 %copy-start.16 = (f32[32,8,128]{2,1,0:T(8,128)S(1)}, f32[32,8,128]{2,1,0:T(8,128)}, u32[]{:S(2)}) copy-start(f32[32,8,128]{2,1,0:T(8,128)} %copy-done.15) | copy-start | bytes 393220
  64.1 9.3 %collective-permute-start.2 = (f32[2,80,128]{2,1,0:T(8,128)S(1)}, f32[2,80,128]{2,1,0:T(8,128)S(1)}, u32[]{:S(2)}, u32[]{:S(2)}) collective-permute-start(f32[2,80,128]{2,1,0:T(8,128)S(1)} %get-tuple-element.46), channel_id=1, source_target_pairs={{0,8},{8,16},{16,24},{1,9},{9,17},{17,25},{2,10},{10,18},{18,26},{... | collective-permute-start | bytes 245768 | tf_op jit(solution)/shard_map/ppermute | solution.py:534
  68.5 6.5 %collective-permute-start.3 = (f32[2,80,128]{2,1,0:T(8,128)S(1)}, f32[2,80,128]{2,1,0:T(8,128)S(1)}, u32[]{:S(2)}, u32[]{:S(2)}) collective-permute-start(f32[2,80,128]{2,1,0:T(8,128)S(1)} %get-tuple-element.47), channel_id=1, source_target_pairs={{8,0},{16,8},{24,16},{9,1},{17,9},{25,17},{10,2},{18,10},{26,18},{... | collective-permute-start | bytes 245768 | tf_op jit(solution)/shard_map/ppermute | solution.py:534
  69.8 37.5 %collective-permute-start.6 = (f32[560,128]{1,0:T(8,128)S(1)}, f32[560,128]{1,0:T(8,128)S(1)}, u32[]{:S(2)}, u32[]{:S(2)}) collective-permute-start(f32[560,128]{1,0:T(8,128)S(1)} %copy-done.28), channel_id=1, source_target_pairs={{0,1},{1,2},{2,3},{3,4},{4,5},{5,6},{6,7},{7,0},{8,9},{9,10},{10,1... | collective-permute-start | bytes 860168 | tf_op jit(solution)/shard_map/ppermute | solution.py:540
  70.1 37.3 %collective-permute-start.7 = (f32[560,128]{1,0:T(8,128)S(1)}, f32[560,128]{1,0:T(8,128)S(1)}, u32[]{:S(2)}, u32[]{:S(2)}) collective-permute-start(f32[560,128]{1,0:T(8,128)S(1)} %copy-done.26), channel_id=1, source_target_pairs={{1,0},{2,1},{3,2},{4,3},{5,4},{6,5},{7,6},{0,7},{9,8},{10,9},{11,1... | collective-permute-start | bytes 860168 | tf_op jit(solution)/shard_map/ppermute | solution.py:540
  82.9 27.2 %collective-permute-start.4 = (f32[560,128]{1,0:T(8,128)S(1)}, f32[560,128]{1,0:T(8,128)S(1)}, u32[]{:S(2)}, u32[]{:S(2)}) collective-permute-start(f32[560,128]{1,0:T(8,128)S(1)} %get-tuple-element.49), channel_id=1, source_target_pairs={{0,1},{1,2},{2,3},{3,4},{4,5},{5,6},{6,7},{7,0},{8,9},{9,10},{10,1... | collective-permute-start | bytes 860168 | tf_op jit(solution)/shard_map/ppermute | solution.py:540
  83.0 27.1 %collective-permute-start.5 = (f32[560,128]{1,0:T(8,128)S(1)}, f32[560,128]{1,0:T(8,128)S(1)}, u32[]{:S(2)}, u32[]{:S(2)}) collective-permute-start(f32[560,128]{1,0:T(8,128)S(1)} %get-tuple-element.50), channel_id=1, source_target_pairs={{1,0},{2,1},{3,2},{4,3},{5,4},{6,5},{7,6},{0,7},{9,8},{10,9},{11,1... | collective-permute-start | bytes 860168 | tf_op jit(solution)/shard_map/ppermute | solution.py:540
  93.6 13.8 %copy-start.18 = (f32[2240,128]{1,0:T(8,128)S(1)}, f32[2240,128]{1,0:T(8,128)}, u32[]{:S(2)}) copy-start(f32[2240,128]{1,0:T(8,128)} %copy-done.17) | copy-start | bytes 3440644
  129.0 22.3 %copy-start.10 = (f32[5,288,128]{2,1,0:T(8,128)S(1)}, f32[5,288,128]{2,1,0:T(8,128)}, u32[]{:S(2)}) copy-start(f32[5,288,128]{2,1,0:T(8,128)} %copy-done.8) | copy-start | bytes 2211844
  129.0 6.5 %collective-permute-start.8 = (f32[2,80,128]{2,1,0:T(8,128)S(1)}, f32[2,80,128]{2,1,0:T(8,128)S(1)}, u32[]{:S(2)}, u32[]{:S(2)}) collective-permute-start(f32[2,80,128]{2,1,0:T(8,128)S(1)} %get-tuple-element.58), channel_id=1, source_target_pairs={{0,8},{8,16},{16,24},{1,9},{9,17},{17,25},{2,10},{10,18},{18,26},{... | collective-permute-start | bytes 245768 | tf_op jit(solution)/shard_map/ppermute | solution.py:534
  133.4 6.3 %collective-permute-start.9 = (f32[2,80,128]{2,1,0:T(8,128)S(1)}, f32[2,80,128]{2,1,0:T(8,128)S(1)}, u32[]{:S(2)}, u32[]{:S(2)}) collective-permute-start(f32[2,80,128]{2,1,0:T(8,128)S(1)} %get-tuple-element.59), channel_id=1, source_target_pairs={{8,0},{16,8},{24,16},{9,1},{17,9},{25,17},{10,2},{18,10},{26,18},{... | collective-permute-start | bytes 245768 | tf_op jit(solution)/shard_map/ppermute | solution.py:534
  147.7 17.4 %collective-permute-start.10 = (f32[560,128]{1,0:T(8,128)S(1)}, f32[560,128]{1,0:T(8,128)S(1)}, u32[]{:S(2)}, u32[]{:S(2)}) collective-permute-start(f32[560,128]{1,0:T(8,128)S(1)} %get-tuple-element.61), channel_id=1, source_target_pairs={{0,1},{1,2},{2,3},{3,4},{4,5},{5,6},{6,7},{7,0},{8,9},{9,10},{10,1... | collective-permute-start | bytes 860168 | tf_op jit(solution)/shard_map/ppermute | solution.py:540
  147.8 17.3 %collective-permute-start.11 = (f32[560,128]{1,0:T(8,128)S(1)}, f32[560,128]{1,0:T(8,128)S(1)}, u32[]{:S(2)}, u32[]{:S(2)}) collective-permute-start(f32[560,128]{1,0:T(8,128)S(1)} %get-tuple-element.62), channel_id=1, source_target_pairs={{1,0},{2,1},{3,2},{4,3},{5,4},{6,5},{7,6},{0,7},{9,8},{10,9},{11,1... | collective-permute-start | bytes 860168 | tf_op jit(solution)/shard_map/ppermute | solution.py:540
  151.3 13.8 %copy-start.5 = (f32[1024,128]{1,0:T(8,128)S(1)}, f32[1024,128]{1,0:T(8,128)}, u32[]{:S(2)}) copy-start(f32[1024,128]{1,0:T(8,128)} %get-tuple-element.39.low.refs_6_) | copy-start | bytes 1572868
  151.3 13.8 %copy-start.7 = (f32[1024,128]{1,0:T(8,128)S(1)}, f32[1024,128]{1,0:T(8,128)}, u32[]{:S(2)}) copy-start(f32[1024,128]{1,0:T(8,128)} %get-tuple-element.40.high.refs_7_) | copy-start | bytes 1572868
  151.3 13.8 %copy-start.12 = (f32[5,288,128]{2,1,0:T(8,128)S(1)}, f32[5,288,128]{2,1,0:T(8,128)}, u32[]{:S(2)}) copy-start(f32[5,288,128]{2,1,0:T(8,128)} %copy-done.11) | copy-start | bytes 2211844
  165.1 31.9 %copy-start.24 = (s32[1,512]{1,0:T(1,128)S(1)}, s32[1,512]{1,0:T(1,128)}, u32[]{:S(2)}) copy-start(s32[1,512]{1,0:T(1,128)} %get-tuple-element.67.slot) | copy-start | bytes 6148
  (22 other events, 71.5 us)
where the time goes:
time: 199 us; the launch traced here: 198 us
  Pallas kernels  105 us (53%)
  starting transfers between devices  42.5 us (21%)
  blocking collectives  18 us (9%)
  waiting for transfers between devices  17.3 us (9%)
  local copies, waits for them, and re-layouts  14.1 us (7%)
    pallas_call x2, Pallas kernels, on_device(): call(own_kernel, arrays(mid_shape)[0], 6 * groups, 'own', scratch_shapes=...  27.5 us
    pallas_call x2, Pallas kernels, on_device(): call(functools.partial(strip_kernel, sizes, begin, len(aliases), len(earl...  27.5 us
    pallas_call x3, Pallas kernels, halo(): call(edges_kernel, arrays((ext_rows * SUB, LANES), (span * SUB, LANES), (...  23.7 us
    all_to_all x1, blocking collectives, on_device(): lax.all_to_all(back.reshape(devices, rows // devices, LANES), both, split...  18 us
    ppermute x6, starting transfers between devices, exchange_rows(): return (lax.ppermute(up, 'lat', pairs), lax.ppermute(down, 'lat', back))  15.6 us
    pallas_call x2, Pallas kernels, scatter(): call(functools.partial(scatter_kernel, first), arrays((CHUNKS[chunk], lat...  13.3 us
    unnamed x58, local copies, waits for them, and re-layouts  11.3 us
    ppermute x6, starting transfers between devices, exchange_columns(): return (lax.ppermute(east, 'lon', pairs), lax.ppermute(west, 'lon', back))  10.8 us
  transfers between devices with their start and end apart: 15, of which 6 were waited for; matrix products, arithmetic and copies ran while one was open for 1% of the time, Pallas kernels for 39%

commit v1 on v0

--- a/solution.py
+++ b/solution.py
@@ -262,8 +262,9 @@
     place = lane % HALF
 
     def body(i, carry):
-        for n in range(TURNS):
-            m = i * TURNS + n
+        done = []
+        for n in range(TURNS // 2):
+            m = i * (TURNS // 2) + n
             to_east = None
             to_west = None
             for q in range(SEATS):
@@ -272,18 +273,20 @@
                 left = jnp.where(lane < HALF, first, second)
                 right = jnp.where(lane < HALF, second, first)
                 row = jnp.where(place < STRIP, pltpu.roll(left, STEPS, 1), pltpu.roll(right, HALF - STEPS, 1))
-                strips[row_at(q * span + m), :] = row
+                done.append((strips, q * span + m, row))
                 right = pltpu.roll(right, SEAT * q + SEAT, 1)
                 if q:
                     left = pltpu.roll(left, SEAT * q, 1)
                 mine = place // SEAT == q
                 to_east = right if q == 0 else jnp.where(mine, right, to_east)
                 to_west = left if q == 0 else jnp.where(mine, left, to_west)
-            east[row_at(m), :] = to_east
-            west[row_at(m), :] = to_west
-        return carry
-
-    lax.fori_loop(0, span // TURNS, body, 0)
+            done.append((east, m, to_east))
+            done.append((west, m, to_west))
+        for ref, m, value in done:
+            ref[row_at(m), :] = value
+        return carry
+
+    lax.fori_loop(0, span // (TURNS // 2), body, 0)
 
 
 def build_strips(win, strips, from_west, from_east):
@@ -671,7 +674,7 @@
         )(loc, recv, low, high)
 
     observed = [scatter(0, LARGE), scatter(1, SMALL)]
-    pieces.append(tile_exchange(1, pieces[0], observed[0], own_coef, coef_strips))
+    pieces.append(tile_exchange(1, pieces[0], observed[0], own_coef, coef_west, coef_east))
     shift_space = pltpu.VMEM((2 * LANES, 2 * LANES), jnp.bfloat16)
     smoothed = None
     sampled = []
@@ -706,6 +709,8 @@
                 "strip_coef",
                 scratch_shapes=[pltpu.VMEM(((win_rows + SUB) * SUB, LANES), f32)],
             )(after(coef_strips, mid, *observed[1:]), coef_west, coef_east)
+        if chunk + 1 < len(CHUNKS):
+            pieces[chunk + 1] = after(pieces[chunk + 1], mid)
         operands = [loc, strips, from_west, from_east, strip_coef, mid, low, high, norm_factor]
         specs = [smem] + [vmem] * 7 + [hbm]
         aliases = {}
@@ -738,8 +743,6 @@
         )(*operands, *earlier)
         sampled.append(part)
         first += groups
-        if not last:
-            pieces[chunk + 1] = after(pieces[chunk + 1], part)
 
     back = sampled[-1]
     returned = lax.all_to_all(

time: 199 us -> 189 us (0.950)
  Pallas kernels: 105 us -> 90.9 us
  waiting for transfers between devices: 17.3 us -> 27.5 us
  blocking collectives: 18 us -> 12.4 us
  starting transfers between devices: 42.5 us -> 40.3 us
    pallas_call x3, Pallas kernels: 23.7 us -> 9.4 us  [halo(): call(edges_kernel, arrays((ext_rows * SUB, LANES), (span * SUB, LANES), (...]
    all_to_all x2, waiting for transfers between devices: 0.01 us -> 13.9 us  [tile_exchange(): return lax.all_to_all(piece, 'lon', split_axis=0, concat_axis=0, tiled=True)]
    all_to_all x1, blocking collectives: 18 us -> 12.4 us  [on_device(): lax.all_to_all(back.reshape(devices, rows // devices, LANES), both, split...]
    ppermute x6, waiting for transfers between devices: 9.44 us -> 6.03 us  [exchange_rows(): return (lax.ppermute(up, 'lat', pairs), lax.ppermute(down, 'lat', back))]
    ppermute x6, starting transfers between devices: 15.6 us -> 12.4 us  [exchange_rows(): return (lax.ppermute(up, 'lat', pairs), lax.ppermute(down, 'lat', back))]
    unnamed x58 -> x70, local copies, waits for them, and re-layouts: 11.3 us -> 13.2 us
  transfers between devices with their start and end apart: 15 -> 15, of which waited for: 6 -> 7; matrix products, arithmetic and copies ran while one was open for 1% -> 1% of each run, Pallas kernels for 39% -> 38%
where the time goes in v1:
time: 189 us; the launch traced here: 188 us
  Pallas kernels  90.9 us (48%)
  starting transfers between devices  40.3 us (21%)
  waiting for transfers between devices  27.5 us (15%)
  local copies, waits for them, and re-layouts  15.9 us (8%)
  blocking collectives  12.4 us (7%)
    pallas_call x2, Pallas kernels, on_device(): call(functools.partial(strip_kernel, sizes, begin, len(aliases), len(earl...  27.5 us
    pallas_call x2, Pallas kernels, on_device(): call(own_kernel, arrays(mid_shape)[0], 6 * groups, 'own', scratch_shapes=...  27.5 us
    all_to_all x2, waiting for transfers between devices, tile_exchange(): return lax.all_to_all(piece, 'lon', split_axis=0, concat_axis=0, tiled=True)  13.9 us
    pallas_call x2, Pallas kernels, scatter(): call(functools.partial(scatter_kernel, first), arrays((CHUNKS[chunk], lat...  13.3 us
    unnamed x70, local copies, waits for them, and re-layouts  13.2 us
    all_to_all x1, blocking collectives, on_device(): lax.all_to_all(back.reshape(devices, rows // devices, LANES), both, split...  12.4 us
    ppermute x6, starting transfers between devices, exchange_rows(): return (lax.ppermute(up, 'lat', pairs), lax.ppermute(down, 'lat', back))  12.4 us
    ppermute x6, starting transfers between devices, exchange_columns(): return (lax.ppermute(east, 'lon', pairs), lax.ppermute(west, 'lon', back))  10.7 us
  transfers between devices with their start and end apart: 15, of which 7 were waited for; matrix products, arithmetic and copies ran while one was open for 1% of the time, Pallas kernels for 38%

profile of v1, /device:TPU:0, one launch (start us, length us, event | category | flops | bytes accessed | tf_op | source)
XLA Modules:
  0.0 188.0 jit_solution(10392404581724024181)
XLA Ops:
  3.1 7.3 %all-to-all-start = ((f32[32,8,128]{2,1,0:T(8,128)}), f32[32,8,128]{2,1,0:T(8,128)S(1)}, u32[]{:S(2)}, u32[]{:S(2)}) async-start(f32[32,8,128]{2,1,0:T(8,128)} %bitcast.25), calls=%async_computation | async-start | bytes 262144 | tf_op jit(solution)/shard_map/all_to_all | solution.py:646
  11.9 6.7 %all-to-all-done = f32[32,8,128]{2,1,0:T(8,128)S(1)} async-done(((f32[32,8,128]{2,1,0:T(8,128)}), f32[32,8,128]{2,1,0:T(8,128)S(1)}, u32[]{:S(2)}, u32[]{:S(2)}) %all-to-all-start) | async-done | bytes 131104 | tf_op jit(solution)/shard_map/all_to_all | solution.py:646
  18.6 3.6 %all-to-all-start.1 = ((f32[8,9,4,8,128]{4,3,2,1,0:T(8,128)}), f32[8,9,4,8,128]{4,3,2,1,0:T(8,128)S(1)}, u32[]{:S(2)}, u32[]{:S(2)}) async-start(f32[8,9,4,8,128]{4,3,2,1,0:T(8,128)} %bitcast.24), calls=%async_computation.1 | async-start | bytes 2359296 | tf_op jit(solution)/shard_map/all_to_all | solution.py:602
  22.1 2.8 %collective-permute-start = (f32[1,80,128]{2,1,0:T(8,128)S(1)}, f32[1,80,128]{2,1,0:T(8,128)S(1)}, u32[]{:S(2)}, u32[]{:S(2)}) collective-permute-start(f32[1,80,128]{2,1,0:T(8,128)S(1)} %get-tuple-element.41), channel_id=1, source_target_pairs={{0,8},{8,16},{16,24},{1,9},{9,17},{17,25},{2,10},{10,18},{18,26},{... | collective-permute-start | bytes 122888 | tf_op jit(solution)/shard_map/ppermute | solution.py:537
  26.6 4.2 %collective-permute-done.1.below = f32[1,80,128]{2,1,0:T(8,128)S(1)} collective-permute-done((f32[1,80,128]{2,1,0:T(8,128)S(1)}, f32[1,80,128]{2,1,0:T(8,128)S(1)}, u32[]{:S(2)}, u32[]{:S(2)}) %collective-permute-start.1) | collective-permute-done | bytes 40992 | tf_op jit(solution)/shard_map/ppermute | solution.py:537
  30.8 3.1 %edges.3 = (f32[2240,128]{1,0:T(8,128)S(1)}, f32[560,128]{1,0:T(8,128)S(1)}, f32[560,128]{1,0:T(8,128)S(1)}) custom-call(f32[1,2048,128]{2,1,0:T(8,128)S(1)} %get-tuple-element.37.field, f32[1,80,128]{2,1,0:T(8,128)S(1)} %collective-permute-done.above, f32[1,80,128]{2,1,0:T(8,128)S(1)} %collective-permute-done.1.below), custom_call_target="tpu_custom_call" | custom-call | bytes 10800000 | tf_op jit(solution)/shard_map/edges/pallas_call | solution.py:606
  34.0 3.5 %collective-permute-start.3 = (f32[560,128]{1,0:T(8,128)S(1)}, f32[560,128]{1,0:T(8,128)S(1)}, u32[]{:S(2)}, u32[]{:S(2)}) collective-permute-start(f32[560,128]{1,0:T(8,128)S(1)} %get-tuple-element.44), channel_id=1, source_target_pairs={{1,0},{2,1},{3,2},{4,3},{5,4},{6,5},{7,6},{0,7},{9,8},{10,9},{11,1... | collective-permute-start | bytes 860168 | tf_op jit(solution)/shard_map/ppermute | solution.py:543
  40.5 2.8 %place.1 = (f32[1024,128]{1,0:T(8,128)}, f32[1024,128]{1,0:T(8,128)}, s32[8,256]{1,0:T(8,128)}) custom-call(f32[256,128]{1,0:T(8,128)} %bitcast.16), custom_call_target="tpu_custom_call" | custom-call | bytes 7200000 | tf_op jit(solution)/shard_map/place/pallas_call | solution.py:655
  43.3 7.6 %scatter.2.obs = f32[2,2048,128]{2,1,0:T(8,128)} custom-call(s32[8,256]{1,0:T(8,128)} %get-tuple-element.36.loc.refs_0_, f32[256,128]{1,0:T(8,128)} %bitcast.17, f32[1024,128]{1,0:T(8,128)} %get-tuple-element.39.low.refs_6_, f32[1024,128]{1,0:T(8,128)} %get-tuple-element.40.high.refs_7_), custom_call_target="tpu_custom_call" | custom-call | bytes 32400000 | tf_op jit(solution)/shard_map/scatter/pallas_call | solution.py:666
  55.6 6.4 %all-to-all-start.2 = ((f32[8,16,4,8,128]{4,3,2,1,0:T(8,128)}), f32[8,16,4,8,128]{4,3,2,1,0:T(8,128)}, u32[]{:S(2)}, u32[]{:S(2)}) async-start(f32[8,16,4,8,128]{4,3,2,1,0:T(8,128)} %bitcast.21), calls=%async_computation.2 | async-start | bytes 4194304 | tf_op jit(solution)/shard_map/all_to_all | solution.py:602
  66.5 2.7 %collective-permute-start.4 = (f32[2,80,128]{2,1,0:T(8,128)S(1)}, f32[2,80,128]{2,1,0:T(8,128)S(1)}, u32[]{:S(2)}, u32[]{:S(2)}) collective-permute-start(f32[2,80,128]{2,1,0:T(8,128)S(1)} %get-tuple-element.47), channel_id=1, source_target_pairs={{0,8},{8,16},{16,24},{1,9},{9,17},{17,25},{2,10},{10,18},{18,26},{... | collective-permute-start | bytes 245768 | tf_op jit(solution)/shard_map/ppermute | solution.py:537
  70.7 5.7 %scatter.3.obs = f32[2,2048,128]{2,1,0:T(8,128)S(1)} custom-call(s32[8,256]{1,0:T(8,128)S(1)} %copy-done.21, f32[256,128]{1,0:T(8,128)S(1)} %bitcast.18, f32[1024,128]{1,0:T(8,128)S(1)} %copy-done.6, f32[1024,128]{1,0:T(8,128)S(1)} %copy-done.8), custom_call_target="tpu_custom_call" | custom-call | bytes 32400000 | tf_op jit(solution)/shard_map/scatter/pallas_call | solution.py:666
  77.8 3.2 %edges.4 = (f32[2240,128]{1,0:T(8,128)S(1)}, f32[560,128]{1,0:T(8,128)S(1)}, f32[560,128]{1,0:T(8,128)S(1)}) custom-call(f32[2,2048,128]{2,1,0:T(8,128)S(1)} %get-tuple-element.50.field, f32[2,80,128]{2,1,0:T(8,128)S(1)} %collective-permute-done.4.above, f32[2,80,128]{2,1,0:T(8,128)S(1)} %collective-permute-done.5.below), custom_call_target="tpu_custom_call" | custom-call | bytes 10800000 | tf_op jit(solution)/shard_map/edges/pallas_call | solution.py:606
  83.4 13.7 %own.2.refs_5_ = f32[2,2048,128]{2,1,0:T(8,128)S(1)} custom-call(f32[2,2048,128]{2,1,0:T(8,128)S(1)} %get-tuple-element.50.field, f32[2,80,128]{2,1,0:T(8,128)S(1)} %collective-permute-done.4.above, f32[2,80,128]{2,1,0:T(8,128)S(1)} %collective-permute-done.5.below, f32[5,288,128]{2,1,0:T(8,128)S(1)} %copy-done.11), custom_call_target="tpu_custom_call" | custom-call | bytes 43200000 | tf_op jit(solution)/shard_map/own/pallas_call | solution.py:697
  98.5 12.6 %all-to-all-done.2.tiles = f32[8,16,4,8,128]{4,3,2,1,0:T(8,128)} async-done(((f32[8,16,4,8,128]{4,3,2,1,0:T(8,128)}), f32[8,16,4,8,128]{4,3,2,1,0:T(8,128)}, u32[]{:S(2)}, u32[]{:S(2)}) %all-to-all-start.2) | async-done | bytes 2097184 | tf_op jit(solution)/shard_map/all_to_all | solution.py:602
  112.7 3.0 %field.3 = (f32[2,2048,128]{2,1,0:T(8,128)S(1)}, f32[2,80,128]{2,1,0:T(8,128)S(1)}, f32[2,80,128]{2,1,0:T(8,128)S(1)}) custom-call(s32[8,256]{1,0:T(8,128)S(1)} %copy-done.21, s32[1]{0:T(128)} %bitcast.5.lat, f32[8,16,4,8,128]{4,3,2,1,0:T(8,128)} %all-to-all-done.2.tiles, f32[2,2048,128]{2,1,0:T(8,128)S(1)} %copy-done.4, f32[25,256,128]{2,1,0:T(8,128)S(1)} %copy-done), custom_call_target="tpu_custom_call" | custom-call | bytes 14400000 | tf_op jit(solution)/shard_map/field/pallas_call | solution.py:686
  115.7 2.9 %collective-permute-start.6 = (f32[2,80,128]{2,1,0:T(8,128)S(1)}, f32[2,80,128]{2,1,0:T(8,128)S(1)}, u32[]{:S(2)}, u32[]{:S(2)}) collective-permute-start(f32[2,80,128]{2,1,0:T(8,128)S(1)} %get-tuple-element.53), channel_id=1, source_target_pairs={{0,8},{8,16},{16,24},{1,9},{9,17},{17,25},{2,10},{10,18},{18,26},{... | collective-permute-start | bytes 245768 | tf_op jit(solution)/shard_map/ppermute | solution.py:537
  120.0 3.5 %collective-permute-start.11 = (f32[560,128]{1,0:T(8,128)S(1)}, f32[560,128]{1,0:T(8,128)S(1)}, u32[]{:S(2)}, u32[]{:S(2)}) collective-permute-start(f32[560,128]{1,0:T(8,128)S(1)} %copy-done.32), channel_id=1, source_target_pairs={{1,0},{2,1},{3,2},{4,3},{5,4},{6,5},{7,6},{0,7},{9,8},{10,9},{11,1... | collective-permute-start | bytes 860168 | tf_op jit(solution)/shard_map/ppermute | solution.py:543
  125.0 3.2 %edges.5 = (f32[2240,128]{1,0:T(8,128)S(1)}, f32[560,128]{1,0:T(8,128)S(1)}, f32[560,128]{1,0:T(8,128)S(1)}) custom-call(f32[2,2048,128]{2,1,0:T(8,128)S(1)} %get-tuple-element.60.field, f32[2,80,128]{2,1,0:T(8,128)S(1)} %collective-permute-done.6.above, f32[2,80,128]{2,1,0:T(8,128)S(1)} %collective-permute-done.7.below), custom_call_target="tpu_custom_call" | custom-call | bytes 10800000 | tf_op jit(solution)/shard_map/edges/pallas_call | solution.py:606
  128.2 3.5 %collective-permute-start.9 = (f32[560,128]{1,0:T(8,128)S(1)}, f32[560,128]{1,0:T(8,128)S(1)}, u32[]{:S(2)}, u32[]{:S(2)}) collective-permute-start(f32[560,128]{1,0:T(8,128)S(1)} %get-tuple-element.57), channel_id=1, source_target_pairs={{1,0},{2,1},{3,2},{4,3},{5,4},{6,5},{7,6},{0,7},{9,8},{10,9},{11,1... | collective-permute-start | bytes 860168 | tf_op jit(solution)/shard_map/ppermute | solution.py:543
  133.4 13.6 %strips.2 = (f32[25,256,128]{2,1,0:T(8,128)}, f32[2,2,32,128]{3,2,1,0:T(8,128)S(1)}) custom-call(s32[8,256]{1,0:T(8,128)S(1)} %copy-done.21, f32[2240,128]{1,0:T(8,128)S(1)} %copy-done.18, f32[560,128]{1,0:T(8,128)S(1)} %collective-permute-done.10.refs_2_, f32[560,128]{1,0:T(8,128)S(1)} %collective-permute-done.11.refs_3_, ...), custom_call_target="tpu_custom_call" | custom-call | bytes 43200000 | tf_op jit(solution)/shard_map/strips/pallas_call | solution.py:725
  147.0 13.7 %own.3.refs_5_ = f32[2,2048,128]{2,1,0:T(8,128)S(1)} custom-call(f32[2,2048,128]{2,1,0:T(8,128)S(1)} %get-tuple-element.60.field, f32[2,80,128]{2,1,0:T(8,128)S(1)} %collective-permute-done.6.above, f32[2,80,128]{2,1,0:T(8,128)S(1)} %collective-permute-done.7.below, f32[5,288,128]{2,1,0:T(8,128)S(1)} %copy-done.12), custom_call_target="tpu_custom_call" | custom-call | bytes 43200000 | tf_op jit(solution)/shard_map/own/pallas_call | solution.py:697
  160.7 13.9 %strips.3 = (f32[25,256,128]{2,1,0:T(8,128)}, f32[256,128]{1,0:T(8,128)S(1)}) custom-call(s32[8,256]{1,0:T(8,128)S(1)} %copy-done.21, f32[2240,128]{1,0:T(8,128)S(1)} %get-tuple-element.55.refs_1_, f32[560,128]{1,0:T(8,128)S(1)} %collective-permute-done.8.refs_2_, f32[560,128]{1,0:T(8,128)S(1)} %collective-permute-done.9.refs_3_, ...), custom_call_target="tpu_custom_call", output_to_operand_aliasing={{0}: (9, {})} | custom-call | bytes 43200000 | tf_op jit(solution)/shard_map/strips/pallas_call | solution.py:725
  174.7 12.4 %all_to_all.20 = f32[32,8,128]{2,1,0:T(8,128)S(1)} all-to-all(f32[32,8,128]{2,1,0:T(8,128)S(1)} %bitcast.20), channel_id=1, replica_groups=mesh['lat'=4,'lon'=8] {'lat','lon'}, dimensions={0} | all-to-all | bytes 262144 | tf_op jit(solution)/shard_map/all_to_all | solution.py:748
  (100 shorter events, 31.5 us)
Async XLA Ops:
  0.6 9.8 %slice-start = ((f32[25,32,8,128]{3,2,1,0:T(8,128)}), f32[9,32,8,128]{3,2,1,0:T(8,128)S(1)}, s32[]{:S(2)}) async-start(f32[25,32,8,128]{3,2,1,0:T(8,128)} %param.17), calls=%async_computation.4 | async-start | bytes 2359296 | tf_op jit(solution)/shard_map/slice | solution.py:598
  3.1 15.5 %all-to-all-start = ((f32[32,8,128]{2,1,0:T(8,128)}), f32[32,8,128]{2,1,0:T(8,128)S(1)}, u32[]{:S(2)}, u32[]{:S(2)}) async-start(f32[32,8,128]{2,1,0:T(8,128)} %bitcast.25), calls=%async_computation | async-start | bytes 262144 | tf_op jit(solution)/shard_map/all_to_all | solution.py:646
  18.6 18.9 %copy-start.15 = (f32[32,8,128]{2,1,0:T(8,128)}, f32[32,8,128]{2,1,0:T(8,128)S(1)}, u32[]{:S(2)}) copy-start(f32[32,8,128]{2,1,0:T(8,128)S(1)} %all-to-all-done) | copy-start | bytes 393220
  18.6 36.0 %all-to-all-start.1 = ((f32[8,9,4,8,128]{4,3,2,1,0:T(8,128)}), f32[8,9,4,8,128]{4,3,2,1,0:T(8,128)S(1)}, u32[]{:S(2)}, u32[]{:S(2)}) async-start(f32[8,9,4,8,128]{4,3,2,1,0:T(8,128)} %bitcast.24), calls=%async_computation.1 | async-start | bytes 2359296 | tf_op jit(solution)/shard_map/all_to_all | solution.py:602
  22.1 4.4 %collective-permute-start = (f32[1,80,128]{2,1,0:T(8,128)S(1)}, f32[1,80,128]{2,1,0:T(8,128)S(1)}, u32[]{:S(2)}, u32[]{:S(2)}) collective-permute-start(f32[1,80,128]{2,1,0:T(8,128)S(1)} %get-tuple-element.41), channel_id=1, source_target_pairs={{0,8},{8,16},{16,24},{1,9},{9,17},{17,25},{2,10},{10,18},{18,26},{... | collective-permute-start | bytes 122888 | tf_op jit(solution)/shard_map/ppermute | solution.py:537
  24.9 5.9 %collective-permute-start.1 = (f32[1,80,128]{2,1,0:T(8,128)S(1)}, f32[1,80,128]{2,1,0:T(8,128)S(1)}, u32[]{:S(2)}, u32[]{:S(2)}) collective-permute-start(f32[1,80,128]{2,1,0:T(8,128)S(1)} %get-tuple-element.42), channel_id=1, source_target_pairs={{8,0},{16,8},{24,16},{9,1},{17,9},{25,17},{10,2},{18,10},{26,18},{... | collective-permute-start | bytes 122888 | tf_op jit(solution)/shard_map/ppermute | solution.py:537
  33.9 17.9 %collective-permute-start.2 = (f32[560,128]{1,0:T(8,128)S(1)}, f32[560,128]{1,0:T(8,128)S(1)}, u32[]{:S(2)}, u32[]{:S(2)}) collective-permute-start(f32[560,128]{1,0:T(8,128)S(1)} %get-tuple-element.43), channel_id=1, source_target_pairs={{0,1},{1,2},{2,3},{3,4},{4,5},{5,6},{6,7},{7,0},{8,9},{9,10},{10,1... | collective-permute-start | bytes 860168 | tf_op jit(solution)/shard_map/ppermute | solution.py:543
  34.0 18.5 %collective-permute-start.3 = (f32[560,128]{1,0:T(8,128)S(1)}, f32[560,128]{1,0:T(8,128)S(1)}, u32[]{:S(2)}, u32[]{:S(2)}) collective-permute-start(f32[560,128]{1,0:T(8,128)S(1)} %get-tuple-element.44), channel_id=1, source_target_pairs={{1,0},{2,1},{3,2},{4,3},{5,4},{6,5},{7,6},{0,7},{9,8},{10,9},{11,1... | collective-permute-start | bytes 860168 | tf_op jit(solution)/shard_map/ppermute | solution.py:543
  55.6 55.5 %all-to-all-start.2 = ((f32[8,16,4,8,128]{4,3,2,1,0:T(8,128)}), f32[8,16,4,8,128]{4,3,2,1,0:T(8,128)}, u32[]{:S(2)}, u32[]{:S(2)}) async-start(f32[8,16,4,8,128]{4,3,2,1,0:T(8,128)} %bitcast.21), calls=%async_computation.2 | async-start | bytes 4194304 | tf_op jit(solution)/shard_map/all_to_all | solution.py:602
  66.5 11.3 %collective-permute-start.4 = (f32[2,80,128]{2,1,0:T(8,128)S(1)}, f32[2,80,128]{2,1,0:T(8,128)S(1)}, u32[]{:S(2)}, u32[]{:S(2)}) collective-permute-start(f32[2,80,128]{2,1,0:T(8,128)S(1)} %get-tuple-element.47), channel_id=1, source_target_pairs={{0,8},{8,16},{16,24},{1,9},{9,17},{17,25},{2,10},{10,18},{18,26},{... | collective-permute-start | bytes 245768 | tf_op jit(solution)/shard_map/ppermute | solution.py:537
  69.2 14.2 %copy-start.11 = (f32[5,288,128]{2,1,0:T(8,128)S(1)}, f32[5,288,128]{2,1,0:T(8,128)}, u32[]{:S(2)}) copy-start(f32[5,288,128]{2,1,0:T(8,128)} %copy-done.10) | copy-start | bytes 2211844
  69.3 8.5 %collective-permute-start.5 = (f32[2,80,128]{2,1,0:T(8,128)S(1)}, f32[2,80,128]{2,1,0:T(8,128)S(1)}, u32[]{:S(2)}, u32[]{:S(2)}) collective-permute-start(f32[2,80,128]{2,1,0:T(8,128)S(1)} %get-tuple-element.48), channel_id=1, source_target_pairs={{8,0},{16,8},{24,16},{9,1},{17,9},{25,17},{10,2},{18,10},{26,18},{... | collective-permute-start | bytes 245768 | tf_op jit(solution)/shard_map/ppermute | solution.py:537
  112.7 19.0 %copy-start.20 = (f32[2240,128]{1,0:T(8,128)S(1)}, f32[2240,128]{1,0:T(8,128)}, u32[]{:S(2)}) copy-start(f32[2240,128]{1,0:T(8,128)} %copy-done.19) | copy-start | bytes 3440644
  112.7 19.0 %copy-start.25 = (f32[560,128]{1,0:T(8,128)S(1)}, f32[560,128]{1,0:T(8,128)}, u32[]{:S(2)}) copy-start(f32[560,128]{1,0:T(8,128)} %copy-done.24) | copy-start | bytes 860164
  115.7 16.0 %copy-start.23 = (f32[560,128]{1,0:T(8,128)S(1)}, f32[560,128]{1,0:T(8,128)}, u32[]{:S(2)}) copy-start(f32[560,128]{1,0:T(8,128)} %copy-done.22) | copy-start | bytes 860164
  115.7 7.8 %collective-permute-start.6 = (f32[2,80,128]{2,1,0:T(8,128)S(1)}, f32[2,80,128]{2,1,0:T(8,128)S(1)}, u32[]{:S(2)}, u32[]{:S(2)}) collective-permute-start(f32[2,80,128]{2,1,0:T(8,128)S(1)} %get-tuple-element.53), channel_id=1, source_target_pairs={{0,8},{8,16},{16,24},{1,9},{9,17},{17,25},{2,10},{10,18},{18,26},{... | collective-permute-start | bytes 245768 | tf_op jit(solution)/shard_map/ppermute | solution.py:537
  118.6 6.3 %collective-permute-start.7 = (f32[2,80,128]{2,1,0:T(8,128)S(1)}, f32[2,80,128]{2,1,0:T(8,128)S(1)}, u32[]{:S(2)}, u32[]{:S(2)}) collective-permute-start(f32[2,80,128]{2,1,0:T(8,128)S(1)} %get-tuple-element.54), channel_id=1, source_target_pairs={{8,0},{16,8},{24,16},{9,1},{17,9},{25,17},{10,2},{18,10},{26,18},{... | collective-permute-start | bytes 245768 | tf_op jit(solution)/shard_map/ppermute | solution.py:537
  119.9 13.4 %collective-permute-start.10 = (f32[560,128]{1,0:T(8,128)S(1)}, f32[560,128]{1,0:T(8,128)S(1)}, u32[]{:S(2)}, u32[]{:S(2)}) collective-permute-start(f32[560,128]{1,0:T(8,128)S(1)} %copy-done.34), channel_id=1, source_target_pairs={{0,1},{1,2},{2,3},{3,4},{4,5},{5,6},{6,7},{7,0},{8,9},{9,10},{10,1... | collective-permute-start | bytes 860168 | tf_op jit(solution)/shard_map/ppermute | solution.py:543
  120.0 13.4 %collective-permute-start.11 = (f32[560,128]{1,0:T(8,128)S(1)}, f32[560,128]{1,0:T(8,128)S(1)}, u32[]{:S(2)}, u32[]{:S(2)}) collective-permute-start(f32[560,128]{1,0:T(8,128)S(1)} %copy-done.32), channel_id=1, source_target_pairs={{1,0},{2,1},{3,2},{4,3},{5,4},{6,5},{7,6},{0,7},{9,8},{10,9},{11,1... | collective-permute-start | bytes 860168 | tf_op jit(solution)/shard_map/ppermute | solution.py:543
  124.9 8.4 %copy-start.18 = (f32[2240,128]{1,0:T(8,128)S(1)}, f32[2240,128]{1,0:T(8,128)}, u32[]{:S(2)}) copy-start(f32[2240,128]{1,0:T(8,128)} %copy-done.17) | copy-start | bytes 3440644
  128.1 32.6 %collective-permute-start.8 = (f32[560,128]{1,0:T(8,128)S(1)}, f32[560,128]{1,0:T(8,128)S(1)}, u32[]{:S(2)}, u32[]{:S(2)}) collective-permute-start(f32[560,128]{1,0:T(8,128)S(1)} %get-tuple-element.56), channel_id=1, source_target_pairs={{0,1},{1,2},{2,3},{3,4},{4,5},{5,6},{6,7},{7,0},{8,9},{9,10},{10,1... | collective-permute-start | bytes 860168 | tf_op jit(solution)/shard_map/ppermute | solution.py:543
  128.2 32.5 %collective-permute-start.9 = (f32[560,128]{1,0:T(8,128)S(1)}, f32[560,128]{1,0:T(8,128)S(1)}, u32[]{:S(2)}, u32[]{:S(2)}) collective-permute-start(f32[560,128]{1,0:T(8,128)S(1)} %get-tuple-element.57), channel_id=1, source_target_pairs={{1,0},{2,1},{3,2},{4,3},{5,4},{6,5},{7,6},{0,7},{9,8},{10,9},{11,1... | collective-permute-start | bytes 860168 | tf_op jit(solution)/shard_map/ppermute | solution.py:543
  133.3 13.6 %copy-start.12 = (f32[5,288,128]{2,1,0:T(8,128)S(1)}, f32[5,288,128]{2,1,0:T(8,128)}, u32[]{:S(2)}) copy-start(f32[5,288,128]{2,1,0:T(8,128)} %copy-done.10) | copy-start | bytes 2211844
  160.7 26.3 %copy-start.30 = (s32[1,512]{1,0:T(1,128)S(1)}, s32[1,512]{1,0:T(1,128)}, u32[]{:S(2)}) copy-start(s32[1,512]{1,0:T(1,128)} %get-tuple-element.67.slot) | copy-start | bytes 6148
  (28 other events, 95.1 us)

commit v2 on v1

--- a/solution.py
+++ b/solution.py
@@ -13,6 +13,7 @@
 PER_ROW = LANES // FEATS
 GROUPS = (5, 4, 8, 8)
 CHUNKS = (2, 2)
+EXCHANGES = ((0, 1), (2,), (3,))
 WEIGHT_ROWS = (5, 6, 12, 13)
 LOC_ROW = 7
 ID_ROW = 15
@@ -34,7 +35,7 @@
 
 
 def cost(micros):
-    return pl.CostEstimate(flops=0, bytes_accessed=int(micros * 3.6e6), transcendentals=0)
+    return pl.CostEstimate(flops=0, bytes_accessed=int(micros * 2e5), transcendentals=0)
 
 
 def iota(shape, dim):
@@ -189,7 +190,9 @@
         down[g] = field[g, :edge, :]
 
 
-def field_kernel(begin, sizes, n_lon, group, cap, loc, lat, tiles, obs, norm_h, field, up, down, norm, sem):
+def field_kernel(begin, sizes, places, n_lon, group, cap, loc, lat, obs, norm_h, *refs):
+    tiles = refs[:-5]
+    field, up, down, norm, sem = refs[-5:]
     copy = pltpu.make_async_copy(norm_h.at[pl.ds(begin, sum(sizes))], norm, sem)
     copy.start()
     field[...] = jnp.zeros_like(field)
@@ -203,9 +206,11 @@
             own = pl.ds(pl.multiple_of(t * SUB, SUB), SUB)
             level = 0
             for g, size in enumerate(sizes):
+                source, offset = places[g]
                 for l in range(size):
                     at = pl.ds(t * (SUB * SUB) + l, SUB, stride=SUB)
-                    done.append((g, at, norm[level, own, :] * (obs[g, at, :] + tiles[j, level, c])))
+                    cells = tiles[source][j, offset + l, c]
+                    done.append((g, at, norm[level, own, :] * (obs[g, at, :] + cells)))
                     level += 1
         for g, at, value in done:
             field[g, at, :] = value
@@ -591,10 +596,10 @@
     def after(value, *others):
         return lax.optimization_barrier((value,) + others)[0]
 
-    def tile_exchange(chunk, *others):
-        first = sum(CHUNKS[:chunk])
-        begin = starts[first]
-        size = sum(GROUPS[first : first + CHUNKS[chunk]])
+    def tile_exchange(number, *others):
+        members = EXCHANGES[number]
+        begin = starts[members[0]]
+        size = sum(GROUPS[index] for index in members)
         piece = model_tiles[begin : begin + size].reshape(size, n_lon, group, SUB, LANES)
         piece = jnp.transpose(piece, (1, 0, 2, 3, 4))
         if others:
@@ -674,7 +679,7 @@
         )(loc, recv, low, high)
 
     observed = [scatter(0, LARGE), scatter(1, SMALL)]
-    pieces.append(tile_exchange(1, pieces[0], observed[0], own_coef, coef_west, coef_east))
+    pieces.append(tile_exchange(1, pieces[0], observed[0], own_coef))
     shift_space = pltpu.VMEM((2 * LANES, 2 * LANES), jnp.bfloat16)
     smoothed = None
     sampled = []
@@ -683,14 +688,24 @@
         sizes = GROUPS[first : first + groups]
         begin = starts[first]
         own_levels = (sum(sizes), lat_cells, LANES)
+        used = []
+        places = []
+        for index in range(first, first + groups):
+            number = [index in members for members in EXCHANGES].index(True)
+            if number not in used:
+                used.append(number)
+            places.append((used.index(number), starts[index] - starts[EXCHANGES[number][0]]))
+        arrived = [pieces[number] for number in used]
+        if chunk:
+            arrived[-1] = after(arrived[-1], sampled[-1])
         field = call(
-            functools.partial(field_kernel, begin, sizes, n_lon, group, cap),
+            functools.partial(field_kernel, begin, sizes, places, n_lon, group, cap),
             field_shapes(groups),
             4,
             "field",
-            in_specs=[smem, smem, vmem, vmem, hbm],
+            in_specs=[smem, smem, vmem, hbm] + [vmem] * len(arrived),
             scratch_shapes=[pltpu.VMEM(own_levels, f32), pltpu.SemaphoreType.DMA],
-        )(loc, lat, pieces[chunk], observed[chunk], norm_factor)
+        )(loc, lat, observed[chunk], norm_factor, *arrived)
         field, above, below, strips, from_west, from_east = halo(*field, groups)
         mid_shape = (groups, lat_cells * SUB, LANES)
         win_shape = (groups, win_rows * SUB, LANES)
@@ -709,8 +724,8 @@
                 "strip_coef",
                 scratch_shapes=[pltpu.VMEM(((win_rows + SUB) * SUB, LANES), f32)],
             )(after(coef_strips, mid, *observed[1:]), coef_west, coef_east)
-        if chunk + 1 < len(CHUNKS):
-            pieces[chunk + 1] = after(pieces[chunk + 1], mid)
+        if chunk == 0:
+            pieces.append(tile_exchange(2, pieces[1], from_west, from_east, coef_west, coef_east))
         operands = [loc, strips, from_west, from_east, strip_coef, mid, low, high, norm_factor]
         specs = [smem] + [vmem] * 7 + [hbm]
         aliases = {}

time: 189 us -> 199 us (1.053)
  starting transfers between devices: 40.3 us -> 45.7 us
  local copies, waits for them, and re-layouts: 15.9 us -> 18.6 us
  waiting for transfers between devices: 27.5 us -> 29.5 us
    ppermute x6, waiting for transfers between devices: 0.86 us -> 8.26 us  [exchange_columns(): return (lax.ppermute(east, 'lon', pairs), lax.ppermute(west, 'lon', back))]
    all_to_all x2 -> x3, starting transfers between devices: 9.93 us -> 15.2 us  [tile_exchange(): return lax.all_to_all(piece, 'lon', split_axis=0, concat_axis=0, tiled=True)]
    all_to_all x2 -> x3, waiting for transfers between devices: 13.9 us -> 8.69 us  [tile_exchange(): return lax.all_to_all(piece, 'lon', split_axis=0, concat_axis=0, tiled=True)]
    slice x4 -> x3, local copies, waits for them, and re-layouts: 0.02 us -> 2.81 us  [tile_exchange(): model_tiles[begin:begin + size].reshape(size, n_lon, group, SUB, LANES)]
    unnamed x70 -> x88, local copies, waits for them, and re-layouts: 13.2 us -> 12.5 us
  transfers between devices with their start and end apart: 15 -> 16, of which waited for: 7 -> 7; matrix products, arithmetic and copies ran while one was open for 1% -> 3% of each run, Pallas kernels for 38% -> 34%
where the time goes in v2:
time: 199 us
  Pallas kernels  91.5 us (46%)
  starting transfers between devices  45.7 us (23%)
  waiting for transfers between devices  29.5 us (15%)
  local copies, waits for them, and re-layouts  18.6 us (9%)
  blocking collectives  12 us (6%)
    pallas_call x2, Pallas kernels, on_device(): call(functools.partial(strip_kernel, sizes, begin, len(aliases), len(earl...  27.5 us
    pallas_call x2, Pallas kernels, on_device(): call(own_kernel, arrays(mid_shape)[0], 6 * groups, 'own', scratch_shapes=...  27.5 us
    all_to_all x3, starting transfers between devices, tile_exchange(): return lax.all_to_all(piece, 'lon', split_axis=0, concat_axis=0, tiled=True)  15.2 us
    pallas_call x2, Pallas kernels, scatter(): call(functools.partial(scatter_kernel, first), arrays((CHUNKS[chunk], lat...  13.5 us
    unnamed x88, local copies, waits for them, and re-layouts  12.5 us
    ppermute x6, starting transfers between devices, exchange_rows(): return (lax.ppermute(up, 'lat', pairs), lax.ppermute(down, 'lat', back))  12.5 us
    all_to_all x1, blocking collectives, on_device(): lax.all_to_all(back.reshape(devices, rows // devices, LANES), both, split...  12 us
    ppermute x6, starting transfers between devices, exchange_columns(): return (lax.ppermute(east, 'lon', pairs), lax.ppermute(west, 'lon', back))  10.7 us
  transfers between devices with their start and end apart: 16, of which 7 were waited for; matrix products, arithmetic and copies ran while one was open for 3% of the time, Pallas kernels for 34%

profile of v2, /device:TPU:0, one launch (start us, length us, event | category | flops | bytes accessed | tf_op | source)
XLA Modules:
  0.0 198.6 jit_solution(6057195104019353494)
XLA Ops:
  3.1 7.3 %all-to-all-start = ((f32[32,8,128]{2,1,0:T(8,128)}), f32[32,8,128]{2,1,0:T(8,128)S(1)}, u32[]{:S(2)}, u32[]{:S(2)}) async-start(f32[32,8,128]{2,1,0:T(8,128)} %bitcast.30), calls=%async_computation | async-start | bytes 262144 | tf_op jit(solution)/shard_map/all_to_all | solution.py:651
  11.9 6.7 %all-to-all-done = f32[32,8,128]{2,1,0:T(8,128)S(1)} async-done(((f32[32,8,128]{2,1,0:T(8,128)}), f32[32,8,128]{2,1,0:T(8,128)S(1)}, u32[]{:S(2)}, u32[]{:S(2)}) %all-to-all-start) | async-done | bytes 131104 | tf_op jit(solution)/shard_map/all_to_all | solution.py:651
  18.6 4.2 %all-to-all-start.1 = ((f32[8,9,4,8,128]{4,3,2,1,0:T(8,128)}), f32[8,9,4,8,128]{4,3,2,1,0:T(8,128)}, u32[]{:S(2)}, u32[]{:S(2)}) async-start(f32[8,9,4,8,128]{4,3,2,1,0:T(8,128)} %bitcast.17), calls=%async_computation.1 | async-start | bytes 2359296 | tf_op jit(solution)/shard_map/all_to_all | solution.py:607
  35.8 7.8 %scatter.3.obs = f32[2,2048,128]{2,1,0:T(8,128)} custom-call(s32[8,256]{1,0:T(8,128)} %get-tuple-element.37.loc.refs_0_, f32[256,128]{1,0:T(8,128)} %bitcast.21, f32[1024,128]{1,0:T(8,128)} %get-tuple-element.38.low.refs_6_, f32[1024,128]{1,0:T(8,128)} %get-tuple-element.39.high.refs_7_), custom_call_target="tpu_custom_call" | custom-call | bytes 1800000 | tf_op jit(solution)/shard_map/scatter/pallas_call | solution.py:671
  43.5 8.7 %all-to-all-done.1.refs_0_ = f32[8,9,4,8,128]{4,3,2,1,0:T(8,128)} async-done(((f32[8,9,4,8,128]{4,3,2,1,0:T(8,128)}), f32[8,9,4,8,128]{4,3,2,1,0:T(8,128)}, u32[]{:S(2)}, u32[]{:S(2)}) %all-to-all-start.1) | async-done | bytes 1179680 | tf_op jit(solution)/shard_map/all_to_all | solution.py:607
  52.2 4.2 %all-to-all-start.2 = ((f32[8,8,4,8,128]{4,3,2,1,0:T(8,128)}), f32[8,8,4,8,128]{4,3,2,1,0:T(8,128)}, u32[]{:S(2)}, u32[]{:S(2)}) async-start(f32[8,8,4,8,128]{4,3,2,1,0:T(8,128)} %bitcast.26), calls=%async_computation.2 | async-start | bytes 2097152 | tf_op jit(solution)/shard_map/all_to_all | solution.py:607
  60.5 3.0 %collective-permute-start.2 = (f32[2,80,128]{2,1,0:T(8,128)S(1)}, f32[2,80,128]{2,1,0:T(8,128)S(1)}, u32[]{:S(2)}, u32[]{:S(2)}) collective-permute-start(f32[2,80,128]{2,1,0:T(8,128)S(1)} %get-tuple-element.46), channel_id=1, source_target_pairs={{0,8},{8,16},{16,24},{1,9},{9,17},{17,25},{2,10},{10,18},{18,26},{... | collective-permute-start | bytes 245768 | tf_op jit(solution)/shard_map/ppermute | solution.py:542
  64.8 3.1 %edges.4 = (f32[2240,128]{1,0:T(8,128)S(1)}, f32[560,128]{1,0:T(8,128)S(1)}, f32[560,128]{1,0:T(8,128)S(1)}) custom-call(f32[1,2048,128]{2,1,0:T(8,128)S(1)} %copy-done.18, f32[1,80,128]{2,1,0:T(8,128)S(1)} %collective-permute-done.above, f32[1,80,128]{2,1,0:T(8,128)S(1)} %copy-done.37), custom_call_target="tpu_custom_call" | custom-call | bytes 600000 | tf_op jit(solution)/shard_map/edges/pallas_call | solution.py:611
  69.0 3.5 %collective-permute-start.7 = (f32[560,128]{1,0:T(8,128)S(1)}, f32[560,128]{1,0:T(8,128)S(1)}, u32[]{:S(2)}, u32[]{:S(2)}) collective-permute-start(f32[560,128]{1,0:T(8,128)S(1)} %get-tuple-element.51), channel_id=1, source_target_pairs={{1,0},{2,1},{3,2},{4,3},{5,4},{6,5},{7,6},{0,7},{9,8},{10,9},{11,1... | collective-permute-start | bytes 860168 | tf_op jit(solution)/shard_map/ppermute | solution.py:548
  72.5 3.2 %edges.3 = (f32[2240,128]{1,0:T(8,128)S(1)}, f32[560,128]{1,0:T(8,128)S(1)}, f32[560,128]{1,0:T(8,128)S(1)}) custom-call(f32[2,2048,128]{2,1,0:T(8,128)S(1)} %get-tuple-element.55.field, f32[2,80,128]{2,1,0:T(8,128)S(1)} %collective-permute-done.2.above, f32[2,80,128]{2,1,0:T(8,128)S(1)} %collective-permute-done.3.below), custom_call_target="tpu_custom_call" | custom-call | bytes 600000 | tf_op jit(solution)/shard_map/edges/pallas_call | solution.py:611
  75.8 3.5 %collective-permute-start.5 = (f32[560,128]{1,0:T(8,128)S(1)}, f32[560,128]{1,0:T(8,128)S(1)}, u32[]{:S(2)}, u32[]{:S(2)}) collective-permute-start(f32[560,128]{1,0:T(8,128)S(1)} %get-tuple-element.49), channel_id=1, source_target_pairs={{1,0},{2,1},{3,2},{4,3},{5,4},{6,5},{7,6},{0,7},{9,8},{10,9},{11,1... | collective-permute-start | bytes 860168 | tf_op jit(solution)/shard_map/ppermute | solution.py:548
  80.4 3.6 %collective-permute-done.6.from_west = f32[560,128]{1,0:T(8,128)S(1)} collective-permute-done((f32[560,128]{1,0:T(8,128)S(1)}, f32[560,128]{1,0:T(8,128)S(1)}, u32[]{:S(2)}, u32[]{:S(2)}) %collective-permute-start.6) | collective-permute-done | bytes 286752 | tf_op jit(solution)/shard_map/ppermute | solution.py:548
  85.5 4.7 %collective-permute-done.4.refs_2_ = f32[560,128]{1,0:T(8,128)S(1)} collective-permute-done((f32[560,128]{1,0:T(8,128)S(1)}, f32[560,128]{1,0:T(8,128)S(1)}, u32[]{:S(2)}, u32[]{:S(2)}) %collective-permute-start.4) | collective-permute-done | bytes 286752 | tf_op jit(solution)/shard_map/ppermute | solution.py:548
  91.6 6.7 %all-to-all-start.3 = ((f32[8,8,4,8,128]{4,3,2,1,0:T(8,128)}), f32[8,8,4,8,128]{4,3,2,1,0:T(8,128)}, u32[]{:S(2)}, u32[]{:S(2)}) async-start(f32[8,8,4,8,128]{4,3,2,1,0:T(8,128)} %bitcast.27), calls=%async_computation.3 | async-start | bytes 2097152 | tf_op jit(solution)/shard_map/all_to_all | solution.py:607
  100.4 5.7 %scatter.2.obs = f32[2,2048,128]{2,1,0:T(8,128)S(1)} custom-call(s32[8,256]{1,0:T(8,128)S(1)} %copy-done.27, f32[256,128]{1,0:T(8,128)S(1)} %bitcast.22, f32[1024,128]{1,0:T(8,128)S(1)} %copy-done.6, f32[1024,128]{1,0:T(8,128)S(1)} %copy-done.9), custom_call_target="tpu_custom_call" | custom-call | bytes 1800000 | tf_op jit(solution)/shard_map/scatter/pallas_call | solution.py:671
  107.5 13.7 %own.2.refs_5_ = f32[2,2048,128]{2,1,0:T(8,128)S(1)} custom-call(f32[2,2048,128]{2,1,0:T(8,128)S(1)} %copy-done.4, f32[2,80,128]{2,1,0:T(8,128)S(1)} %collective-permute-done.2.above, f32[2,80,128]{2,1,0:T(8,128)S(1)} %copy-done.26, f32[5,288,128]{2,1,0:T(8,128)S(1)} %copy-done.13), custom_call_target="tpu_custom_call" | custom-call | bytes 2400000 | tf_op jit(solution)/shard_map/own/pallas_call | solution.py:712
  122.9 13.6 %strips.2 = (f32[25,256,128]{2,1,0:T(8,128)}, f32[2,2,32,128]{3,2,1,0:T(8,128)S(1)}) custom-call(s32[8,256]{1,0:T(8,128)S(1)} %copy-done.27, f32[2240,128]{1,0:T(8,128)S(1)} %copy-done.22, f32[560,128]{1,0:T(8,128)S(1)} %copy-done.33, f32[560,128]{1,0:T(8,128)S(1)} %copy-done.35, f32[5,288,128]{2,1,0:T(8,128)S(1)} %strip_coef.1.refs_4_, ...), custom_call_target="tpu_custom_call" | custom-call | bytes 2400000 | tf_op jit(solution)/shard_map/strips/pallas_call | solution.py:740
  141.8 2.8 %collective-permute-start.8 = (f32[2,80,128]{2,1,0:T(8,128)S(1)}, f32[2,80,128]{2,1,0:T(8,128)S(1)}, u32[]{:S(2)}, u32[]{:S(2)}) collective-permute-start(f32[2,80,128]{2,1,0:T(8,128)S(1)} %get-tuple-element.60), channel_id=1, source_target_pairs={{0,8},{8,16},{16,24},{1,9},{9,17},{17,25},{2,10},{10,18},{18,26},{... | collective-permute-start | bytes 245768 | tf_op jit(solution)/shard_map/ppermute | solution.py:542
  147.0 4.1 %collective-permute-done.9.below = f32[2,80,128]{2,1,0:T(8,128)S(1)} collective-permute-done((f32[2,80,128]{2,1,0:T(8,128)S(1)}, f32[2,80,128]{2,1,0:T(8,128)S(1)}, u32[]{:S(2)}, u32[]{:S(2)}) %collective-permute-start.9) | collective-permute-done | bytes 81952 | tf_op jit(solution)/shard_map/ppermute | solution.py:542
  151.1 3.2 %edges.5 = (f32[2240,128]{1,0:T(8,128)S(1)}, f32[560,128]{1,0:T(8,128)S(1)}, f32[560,128]{1,0:T(8,128)S(1)}) custom-call(f32[2,2048,128]{2,1,0:T(8,128)S(1)} %get-tuple-element.65.field, f32[2,80,128]{2,1,0:T(8,128)S(1)} %collective-permute-done.8.above, f32[2,80,128]{2,1,0:T(8,128)S(1)} %collective-permute-done.9.below), custom_call_target="tpu_custom_call" | custom-call | bytes 600000 | tf_op jit(solution)/shard_map/edges/pallas_call | solution.py:611
  154.4 3.5 %collective-permute-start.11 = (f32[560,128]{1,0:T(8,128)S(1)}, f32[560,128]{1,0:T(8,128)S(1)}, u32[]{:S(2)}, u32[]{:S(2)}) collective-permute-start(f32[560,128]{1,0:T(8,128)S(1)} %get-tuple-element.64), channel_id=1, source_target_pairs={{1,0},{2,1},{3,2},{4,3},{5,4},{6,5},{7,6},{0,7},{9,8},{10,9},{11,1... | collective-permute-start | bytes 860168 | tf_op jit(solution)/shard_map/ppermute | solution.py:548
  157.9 13.7 %own.3.refs_5_ = f32[2,2048,128]{2,1,0:T(8,128)S(1)} custom-call(f32[2,2048,128]{2,1,0:T(8,128)S(1)} %get-tuple-element.65.field, f32[2,80,128]{2,1,0:T(8,128)S(1)} %collective-permute-done.8.above, f32[2,80,128]{2,1,0:T(8,128)S(1)} %collective-permute-done.9.below, f32[5,288,128]{2,1,0:T(8,128)S(1)} %copy-done.14), custom_call_target="tpu_custom_call" | custom-call | bytes 2400000 | tf_op jit(solution)/shard_map/own/pallas_call | solution.py:712
  171.7 13.9 %strips.3 = (f32[25,256,128]{2,1,0:T(8,128)}, f32[256,128]{1,0:T(8,128)S(1)}) custom-call(s32[8,256]{1,0:T(8,128)S(1)} %copy-done.27, f32[2240,128]{1,0:T(8,128)S(1)} %get-tuple-element.62.refs_1_, f32[560,128]{1,0:T(8,128)S(1)} %collective-permute-done.10.refs_2_, f32[560,128]{1,0:T(8,128)S(1)} %collective-permute-done.11.refs_3_, ...), custom_call_target="tpu_custom_call", output_to_operand_aliasing={{0}: (9, {})} | custom-call | bytes 2400000 | tf_op jit(solution)/shard_map/strips/pallas_call | solution.py:740
  185.6 12.0 %all_to_all.25 = f32[32,8,128]{2,1,0:T(8,128)S(1)} all-to-all(f32[32,8,128]{2,1,0:T(8,128)S(1)} %bitcast.24), channel_id=1, replica_groups=mesh['lat'=4,'lon'=8] {'lat','lon'}, dimensions={0} | all-to-all | bytes 262144 | tf_op jit(solution)/shard_map/all_to_all | solution.py:763
  (120 shorter events, 40.9 us)
Async XLA Ops:
  3.1 15.5 %all-to-all-start = ((f32[32,8,128]{2,1,0:T(8,128)}), f32[32,8,128]{2,1,0:T(8,128)S(1)}, u32[]{:S(2)}, u32[]{:S(2)}) async-start(f32[32,8,128]{2,1,0:T(8,128)} %bitcast.30), calls=%async_computation | async-start | bytes 262144 | tf_op jit(solution)/shard_map/all_to_all | solution.py:651
  11.9 19.6 %copy-start.17 = (f32[1,2048,128]{2,1,0:T(8,128)}, f32[1,2048,128]{2,1,0:T(8,128)S(1)}, u32[]{:S(2)}) copy-start(f32[1,2048,128]{2,1,0:T(8,128)S(1)} %get-tuple-element.40.field) | copy-start | bytes 3145732
  18.6 33.7 %all-to-all-start.1 = ((f32[8,9,4,8,128]{4,3,2,1,0:T(8,128)}), f32[8,9,4,8,128]{4,3,2,1,0:T(8,128)}, u32[]{:S(2)}, u32[]{:S(2)}) async-start(f32[8,9,4,8,128]{4,3,2,1,0:T(8,128)} %bitcast.17), calls=%async_computation.1 | async-start | bytes 2359296 | tf_op jit(solution)/shard_map/all_to_all | solution.py:607
  22.8 7.9 %collective-permute-start = (f32[1,80,128]{2,1,0:T(8,128)S(1)}, f32[1,80,128]{2,1,0:T(8,128)S(1)}, u32[]{:S(2)}, u32[]{:S(2)}) collective-permute-start(f32[1,80,128]{2,1,0:T(8,128)S(1)} %get-tuple-element.42), channel_id=1, source_target_pairs={{0,8},{8,16},{16,24},{1,9},{9,17},{17,25},{2,10},{10,18},{18,26},{... | collective-permute-start | bytes 122888 | tf_op jit(solution)/shard_map/ppermute | solution.py:542
  25.6 5.9 %collective-permute-start.1 = (f32[1,80,128]{2,1,0:T(8,128)S(1)}, f32[1,80,128]{2,1,0:T(8,128)S(1)}, u32[]{:S(2)}, u32[]{:S(2)}) collective-permute-start(f32[1,80,128]{2,1,0:T(8,128)S(1)} %get-tuple-element.43), channel_id=1, source_target_pairs={{8,0},{16,8},{24,16},{9,1},{17,9},{25,17},{10,2},{18,10},{26,18},{... | collective-permute-start | bytes 122888 | tf_op jit(solution)/shard_map/ppermute | solution.py:542
  35.8 20.7 %copy-start = (f32[25,256,128]{2,1,0:T(8,128)S(1)}, f32[25,256,128]{2,1,0:T(8,128)}, u32[]{:S(2)}) copy-start(f32[25,256,128]{2,1,0:T(8,128)} %refs_8_.3) | copy-start | bytes 9830404
  35.8 20.7 %copy-start.27 = (s32[8,256]{1,0:T(8,128)S(1)}, s32[8,256]{1,0:T(8,128)}, u32[]{:S(2)}) copy-start(s32[8,256]{1,0:T(8,128)} %get-tuple-element.37.loc.refs_0_) | copy-start | bytes 24580
  52.2 39.4 %all-to-all-start.2 = ((f32[8,8,4,8,128]{4,3,2,1,0:T(8,128)}), f32[8,8,4,8,128]{4,3,2,1,0:T(8,128)}, u32[]{:S(2)}, u32[]{:S(2)}) async-start(f32[8,8,4,8,128]{4,3,2,1,0:T(8,128)} %bitcast.26), calls=%async_computation.2 | async-start | bytes 2097152 | tf_op jit(solution)/shard_map/all_to_all | solution.py:607
  60.5 20.0 %copy-start.3 = (f32[2,2048,128]{2,1,0:T(8,128)}, f32[2,2048,128]{2,1,0:T(8,128)S(1)}, u32[]{:S(2)}) copy-start(f32[2,2048,128]{2,1,0:T(8,128)S(1)} %get-tuple-element.55.field) | copy-start | bytes 6291460
  60.5 18.8 %copy-start.43 = (f32[8,32,8,128]{3,2,1,0:T(8,128)S(1)}, f32[8,32,8,128]{3,2,1,0:T(8,128)}, u32[]{:S(2)}) copy-start(f32[8,32,8,128]{3,2,1,0:T(8,128)} %get-tuple-element.70) | copy-start | bytes 3145732
  60.5 12.0 %collective-permute-start.2 = (f32[2,80,128]{2,1,0:T(8,128)S(1)}, f32[2,80,128]{2,1,0:T(8,128)S(1)}, u32[]{:S(2)}, u32[]{:S(2)}) collective-permute-start(f32[2,80,128]{2,1,0:T(8,128)S(1)} %get-tuple-element.46), channel_id=1, source_target_pairs={{0,8},{8,16},{16,24},{1,9},{9,17},{17,25},{2,10},{10,18},{18,26},{... | collective-permute-start | bytes 245768 | tf_op jit(solution)/shard_map/ppermute | solution.py:542
  63.5 9.0 %collective-permute-start.3 = (f32[2,80,128]{2,1,0:T(8,128)S(1)}, f32[2,80,128]{2,1,0:T(8,128)S(1)}, u32[]{:S(2)}, u32[]{:S(2)}) collective-permute-start(f32[2,80,128]{2,1,0:T(8,128)S(1)} %get-tuple-element.47), channel_id=1, source_target_pairs={{8,0},{16,8},{24,16},{9,1},{17,9},{25,17},{10,2},{18,10},{26,18},{... | collective-permute-start | bytes 245768 | tf_op jit(solution)/shard_map/ppermute | solution.py:542
  69.0 15.1 %collective-permute-start.6 = (f32[560,128]{1,0:T(8,128)S(1)}, f32[560,128]{1,0:T(8,128)S(1)}, u32[]{:S(2)}, u32[]{:S(2)}) collective-permute-start(f32[560,128]{1,0:T(8,128)S(1)} %get-tuple-element.50), channel_id=1, source_target_pairs={{0,1},{1,2},{2,3},{3,4},{4,5},{5,6},{6,7},{7,0},{8,9},{9,10},{10,1... | collective-permute-start | bytes 860168 | tf_op jit(solution)/shard_map/ppermute | solution.py:548
  69.0 15.7 %collective-permute-start.7 = (f32[560,128]{1,0:T(8,128)S(1)}, f32[560,128]{1,0:T(8,128)S(1)}, u32[]{:S(2)}, u32[]{:S(2)}) collective-permute-start(f32[560,128]{1,0:T(8,128)S(1)} %get-tuple-element.51), channel_id=1, source_target_pairs={{1,0},{2,1},{3,2},{4,3},{5,4},{6,5},{7,6},{0,7},{9,8},{10,9},{11,1... | collective-permute-start | bytes 860168 | tf_op jit(solution)/shard_map/ppermute | solution.py:548
  75.7 14.4 %collective-permute-start.4 = (f32[560,128]{1,0:T(8,128)S(1)}, f32[560,128]{1,0:T(8,128)S(1)}, u32[]{:S(2)}, u32[]{:S(2)}) collective-permute-start(f32[560,128]{1,0:T(8,128)S(1)} %get-tuple-element.48), channel_id=1, source_target_pairs={{0,1},{1,2},{2,3},{3,4},{4,5},{5,6},{6,7},{7,0},{8,9},{9,10},{10,1... | collective-permute-start | bytes 860168 | tf_op jit(solution)/shard_map/ppermute | solution.py:548
  75.8 15.1 %collective-permute-start.5 = (f32[560,128]{1,0:T(8,128)S(1)}, f32[560,128]{1,0:T(8,128)S(1)}, u32[]{:S(2)}, u32[]{:S(2)}) collective-permute-start(f32[560,128]{1,0:T(8,128)S(1)} %get-tuple-element.49), channel_id=1, source_target_pairs={{1,0},{2,1},{3,2},{4,3},{5,4},{6,5},{7,6},{0,7},{9,8},{10,9},{11,1... | collective-permute-start | bytes 860168 | tf_op jit(solution)/shard_map/ppermute | solution.py:548
  79.3 19.0 %copy-start.20 = (f32[32,8,128]{2,1,0:T(8,128)S(1)}, f32[32,8,128]{2,1,0:T(8,128)}, u32[]{:S(2)}) copy-start(f32[32,8,128]{2,1,0:T(8,128)} %copy-done.19) | copy-start | bytes 393220
  91.6 45.8 %all-to-all-start.3 = ((f32[8,8,4,8,128]{4,3,2,1,0:T(8,128)}), f32[8,8,4,8,128]{4,3,2,1,0:T(8,128)}, u32[]{:S(2)}, u32[]{:S(2)}) async-start(f32[8,8,4,8,128]{4,3,2,1,0:T(8,128)} %bitcast.27), calls=%async_computation.3 | async-start | bytes 2097152 | tf_op jit(solution)/shard_map/all_to_all | solution.py:607
  141.8 16.1 %copy-start.14 = (f32[5,288,128]{2,1,0:T(8,128)S(1)}, f32[5,288,128]{2,1,0:T(8,128)}, u32[]{:S(2)}) copy-start(f32[5,288,128]{2,1,0:T(8,128)} %copy-done.12) | copy-start | bytes 2211844
  141.8 5.2 %collective-permute-start.8 = (f32[2,80,128]{2,1,0:T(8,128)S(1)}, f32[2,80,128]{2,1,0:T(8,128)S(1)}, u32[]{:S(2)}, u32[]{:S(2)}) collective-permute-start(f32[2,80,128]{2,1,0:T(8,128)S(1)} %get-tuple-element.60), channel_id=1, source_target_pairs={{0,8},{8,16},{16,24},{1,9},{9,17},{17,25},{2,10},{10,18},{18,26},{... | collective-permute-start | bytes 245768 | tf_op jit(solution)/shard_map/ppermute | solution.py:542
  144.6 6.5 %collective-permute-start.9 = (f32[2,80,128]{2,1,0:T(8,128)S(1)}, f32[2,80,128]{2,1,0:T(8,128)S(1)}, u32[]{:S(2)}, u32[]{:S(2)}) collective-permute-start(f32[2,80,128]{2,1,0:T(8,128)S(1)} %get-tuple-element.61), channel_id=1, source_target_pairs={{8,0},{16,8},{24,16},{9,1},{17,9},{25,17},{10,2},{18,10},{26,18},{... | collective-permute-start | bytes 245768 | tf_op jit(solution)/shard_map/ppermute | solution.py:542
  154.3 17.4 %collective-permute-start.10 = (f32[560,128]{1,0:T(8,128)S(1)}, f32[560,128]{1,0:T(8,128)S(1)}, u32[]{:S(2)}, u32[]{:S(2)}) collective-permute-start(f32[560,128]{1,0:T(8,128)S(1)} %get-tuple-element.63), channel_id=1, source_target_pairs={{0,1},{1,2},{2,3},{3,4},{4,5},{5,6},{6,7},{7,0},{8,9},{9,10},{10,1... | collective-permute-start | bytes 860168 | tf_op jit(solution)/shard_map/ppermute | solution.py:548
  154.4 17.3 %collective-permute-start.11 = (f32[560,128]{1,0:T(8,128)S(1)}, f32[560,128]{1,0:T(8,128)S(1)}, u32[]{:S(2)}, u32[]{:S(2)}) collective-permute-start(f32[560,128]{1,0:T(8,128)S(1)} %get-tuple-element.64), channel_id=1, source_target_pairs={{1,0},{2,1},{3,2},{4,3},{5,4},{6,5},{7,6},{0,7},{9,8},{10,9},{11,1... | collective-permute-start | bytes 860168 | tf_op jit(solution)/shard_map/ppermute | solution.py:548
  171.7 26.0 %copy-start.42 = (s32[1,512]{1,0:T(1,128)S(1)}, s32[1,512]{1,0:T(1,128)}, u32[]{:S(2)}) copy-start(s32[1,512]{1,0:T(1,128)} %get-tuple-element.69.slot) | copy-start | bytes 6148
  (37 other events, 218.4 us)

commit v3 on v2

--- a/solution.py
+++ b/solution.py
@@ -725,7 +725,7 @@
                 scratch_shapes=[pltpu.VMEM(((win_rows + SUB) * SUB, LANES), f32)],
             )(after(coef_strips, mid, *observed[1:]), coef_west, coef_east)
         if chunk == 0:
-            pieces.append(tile_exchange(2, pieces[1], from_west, from_east, coef_west, coef_east))
+            pieces.append(tile_exchange(2, pieces[1], mid, from_west, from_east, coef_west, coef_east))
         operands = [loc, strips, from_west, from_east, strip_coef, mid, low, high, norm_factor]
         specs = [smem] + [vmem] * 7 + [hbm]
         aliases = {}

time: 199 us -> 196 us (0.985)
  waiting for transfers between devices: 29.5 us -> 21.8 us
  local copies, waits for them, and re-layouts: 18.6 us -> 23.1 us
    ppermute x6, waiting for transfers between devices: 8.26 us -> 0.02 us  [exchange_columns(): return (lax.ppermute(east, 'lon', pairs), lax.ppermute(west, 'lon', back))]
    unnamed x88 -> x80, local copies, waits for them, and re-layouts: 12.5 us -> 17 us
    all_to_all x3, starting transfers between devices: 15.2 us -> 12.8 us  [tile_exchange(): return lax.all_to_all(piece, 'lon', split_axis=0, concat_axis=0, tiled=True)]
  transfers between devices with their start and end apart: 16 -> 16, of which waited for: 7 -> 5; matrix products, arithmetic and copies ran while one was open for 3% -> 3% of each run, Pallas kernels for 34% -> 35%
where the time goes in v3:
time: 196 us; the launch traced here: 195 us
  Pallas kernels  91.8 us (47%)
  starting transfers between devices  45 us (23%)
  local copies, waits for them, and re-layouts  23.1 us (12%)
  waiting for transfers between devices  21.8 us (11%)
  blocking collectives  12.4 us (6%)
    pallas_call x2, Pallas kernels, on_device(): call(own_kernel, arrays(mid_shape)[0], 6 * groups, 'own', scratch_shapes=...  27.8 us
    pallas_call x2, Pallas kernels, on_device(): call(functools.partial(strip_kernel, sizes, begin, len(aliases), len(earl...  27.5 us
    unnamed x80, local copies, waits for them, and re-layouts  17 us
    ppermute x6, starting transfers between devices, exchange_rows(): return (lax.ppermute(up, 'lat', pairs), lax.ppermute(down, 'lat', back))  14.2 us
    pallas_call x2, Pallas kernels, scatter(): call(functools.partial(scatter_kernel, first), arrays((CHUNKS[chunk], lat...  13.5 us
    all_to_all x3, starting transfers between devices, tile_exchange(): return lax.all_to_all(piece, 'lon', split_axis=0, concat_axis=0, tiled=True)  12.8 us
    all_to_all x1, blocking collectives, on_device(): lax.all_to_all(back.reshape(devices, rows // devices, LANES), both, split...  12.4 us
    ppermute x6, starting transfers between devices, exchange_columns(): return (lax.ppermute(east, 'lon', pairs), lax.ppermute(west, 'lon', back))  10.7 us
  transfers between devices with their start and end apart: 16, of which 5 were waited for; matrix products, arithmetic and copies ran while one was open for 3% of the time, Pallas kernels for 35%

profile of v3, /device:TPU:0, one launch (start us, length us, event | category | flops | bytes accessed | tf_op | source)
XLA Modules:
  0.0 195.1 jit_solution(12532755076369428466)
XLA Ops:
  3.1 7.3 %all-to-all-start = ((f32[32,8,128]{2,1,0:T(8,128)}), f32[32,8,128]{2,1,0:T(8,128)S(1)}, u32[]{:S(2)}, u32[]{:S(2)}) async-start(f32[32,8,128]{2,1,0:T(8,128)} %bitcast.30), calls=%async_computation | async-start | bytes 262144 | tf_op jit(solution)/shard_map/all_to_all | solution.py:651
  11.9 6.7 %all-to-all-done = f32[32,8,128]{2,1,0:T(8,128)S(1)} async-done(((f32[32,8,128]{2,1,0:T(8,128)}), f32[32,8,128]{2,1,0:T(8,128)S(1)}, u32[]{:S(2)}, u32[]{:S(2)}) %all-to-all-start) | async-done | bytes 131104 | tf_op jit(solution)/shard_map/all_to_all | solution.py:651
  18.6 4.3 %all-to-all-start.1 = ((f32[8,9,4,8,128]{4,3,2,1,0:T(8,128)}), f32[8,9,4,8,128]{4,3,2,1,0:T(8,128)}, u32[]{:S(2)}, u32[]{:S(2)}) async-start(f32[8,9,4,8,128]{4,3,2,1,0:T(8,128)} %bitcast.17), calls=%async_computation.1 | async-start | bytes 2359296 | tf_op jit(solution)/shard_map/all_to_all | solution.py:607
  26.9 2.8 %fusion = (f32[8,32,8,128]{3,2,1,0:T(8,128)}, f32[8,32,8,128]{3,2,1,0:T(8,128)S(1)}) fusion(f32[25,32,8,128]{3,2,1,0:T(8,128)} %param.17), kind=kLoop, calls=%fused_computation.3 | loop fusion | bytes 4194304 | tf_op jit(solution)/shard_map/slice | solution.py:603
  35.8 7.8 %scatter.3.obs = f32[2,2048,128]{2,1,0:T(8,128)} custom-call(s32[8,256]{1,0:T(8,128)} %get-tuple-element.37.loc.refs_0_, f32[256,128]{1,0:T(8,128)} %bitcast.21, f32[1024,128]{1,0:T(8,128)} %get-tuple-element.38.low.refs_6_, f32[1024,128]{1,0:T(8,128)} %get-tuple-element.39.high.refs_7_), custom_call_target="tpu_custom_call" | custom-call | bytes 1800000 | tf_op jit(solution)/shard_map/scatter/pallas_call | solution.py:671
  43.6 8.7 %all-to-all-done.1.refs_0_ = f32[8,9,4,8,128]{4,3,2,1,0:T(8,128)} async-done(((f32[8,9,4,8,128]{4,3,2,1,0:T(8,128)}), f32[8,9,4,8,128]{4,3,2,1,0:T(8,128)}, u32[]{:S(2)}, u32[]{:S(2)}) %all-to-all-start.1) | async-done | bytes 1179680 | tf_op jit(solution)/shard_map/all_to_all | solution.py:607
  52.2 4.2 %all-to-all-start.2 = ((f32[8,8,4,8,128]{4,3,2,1,0:T(8,128)}), f32[8,8,4,8,128]{4,3,2,1,0:T(8,128)}, u32[]{:S(2)}, u32[]{:S(2)}) async-start(f32[8,8,4,8,128]{4,3,2,1,0:T(8,128)} %bitcast.26), calls=%async_computation.2 | async-start | bytes 2097152 | tf_op jit(solution)/shard_map/all_to_all | solution.py:607
  60.5 2.9 %collective-permute-start.2 = (f32[2,80,128]{2,1,0:T(8,128)S(1)}, f32[2,80,128]{2,1,0:T(8,128)S(1)}, u32[]{:S(2)}, u32[]{:S(2)}) collective-permute-start(f32[2,80,128]{2,1,0:T(8,128)S(1)} %get-tuple-element.46), channel_id=1, source_target_pairs={{0,8},{8,16},{16,24},{1,9},{9,17},{17,25},{2,10},{10,18},{18,26},{... | collective-permute-start | bytes 245768 | tf_op jit(solution)/shard_map/ppermute | solution.py:542
  64.7 3.1 %edges.4 = (f32[2240,128]{1,0:T(8,128)S(1)}, f32[560,128]{1,0:T(8,128)S(1)}, f32[560,128]{1,0:T(8,128)S(1)}) custom-call(f32[1,2048,128]{2,1,0:T(8,128)S(1)} %copy-done.18, f32[1,80,128]{2,1,0:T(8,128)S(1)} %collective-permute-done.above, f32[1,80,128]{2,1,0:T(8,128)S(1)} %collective-permute-done.1.below), custom_call_target="tpu_custom_call" | custom-call | bytes 600000 | tf_op jit(solution)/shard_map/edges/pallas_call | solution.py:611
  68.9 3.5 %collective-permute-start.7 = (f32[560,128]{1,0:T(8,128)S(1)}, f32[560,128]{1,0:T(8,128)S(1)}, u32[]{:S(2)}, u32[]{:S(2)}) collective-permute-start(f32[560,128]{1,0:T(8,128)S(1)} %get-tuple-element.53), channel_id=1, source_target_pairs={{1,0},{2,1},{3,2},{4,3},{5,4},{6,5},{7,6},{0,7},{9,8},{10,9},{11,1... | collective-permute-start | bytes 860168 | tf_op jit(solution)/shard_map/ppermute | solution.py:548
  72.3 3.2 %edges.3 = (f32[2240,128]{1,0:T(8,128)S(1)}, f32[560,128]{1,0:T(8,128)S(1)}, f32[560,128]{1,0:T(8,128)S(1)}) custom-call(f32[2,2048,128]{2,1,0:T(8,128)S(1)} %get-tuple-element.49.field, f32[2,80,128]{2,1,0:T(8,128)S(1)} %collective-permute-done.2.above, f32[2,80,128]{2,1,0:T(8,128)S(1)} %collective-permute-done.3.below), custom_call_target="tpu_custom_call" | custom-call | bytes 600000 | tf_op jit(solution)/shard_map/edges/pallas_call | solution.py:611
  75.6 3.5 %collective-permute-start.5 = (f32[560,128]{1,0:T(8,128)S(1)}, f32[560,128]{1,0:T(8,128)S(1)}, u32[]{:S(2)}, u32[]{:S(2)}) collective-permute-start(f32[560,128]{1,0:T(8,128)S(1)} %get-tuple-element.51), channel_id=1, source_target_pairs={{1,0},{2,1},{3,2},{4,3},{5,4},{6,5},{7,6},{0,7},{9,8},{10,9},{11,1... | collective-permute-start | bytes 860168 | tf_op jit(solution)/shard_map/ppermute | solution.py:548
  80.3 14.0 %own.2.refs_5_ = f32[2,2048,128]{2,1,0:T(8,128)S(1)} custom-call(f32[2,2048,128]{2,1,0:T(8,128)S(1)} %get-tuple-element.49.field, f32[2,80,128]{2,1,0:T(8,128)S(1)} %collective-permute-done.2.above, f32[2,80,128]{2,1,0:T(8,128)S(1)} %collective-permute-done.3.below, f32[5,288,128]{2,1,0:T(8,128)S(1)} %copy-done.13), custom_call_target="tpu_custom_call" | custom-call | bytes 2400000 | tf_op jit(solution)/shard_map/own/pallas_call | solution.py:712
  98.5 4.3 %all-to-all-start.3 = ((f32[8,8,4,8,128]{4,3,2,1,0:T(8,128)}), f32[8,8,4,8,128]{4,3,2,1,0:T(8,128)}, u32[]{:S(2)}, u32[]{:S(2)}) async-start(f32[8,8,4,8,128]{4,3,2,1,0:T(8,128)} %bitcast.27), calls=%async_computation.3 | async-start | bytes 2097152 | tf_op jit(solution)/shard_map/all_to_all | solution.py:607
  104.9 5.7 %scatter.2.obs = f32[2,2048,128]{2,1,0:T(8,128)S(1)} custom-call(s32[8,256]{1,0:T(8,128)S(1)} %copy-done.25, f32[256,128]{1,0:T(8,128)S(1)} %bitcast.22, f32[1024,128]{1,0:T(8,128)S(1)} %copy-done.6, f32[1024,128]{1,0:T(8,128)S(1)} %copy-done.9), custom_call_target="tpu_custom_call" | custom-call | bytes 1800000 | tf_op jit(solution)/shard_map/scatter/pallas_call | solution.py:671
  116.8 13.6 %strips.2 = (f32[25,256,128]{2,1,0:T(8,128)}, f32[2,2,32,128]{3,2,1,0:T(8,128)S(1)}) custom-call(s32[8,256]{1,0:T(8,128)S(1)} %copy-done.25, f32[2240,128]{1,0:T(8,128)S(1)} %copy-done.22, f32[560,128]{1,0:T(8,128)S(1)} %copy-done.31, f32[560,128]{1,0:T(8,128)S(1)} %copy-done.33, f32[5,288,128]{2,1,0:T(8,128)S(1)} %strip_coef.1.refs_4_, ...), custom_call_target="tpu_custom_call" | custom-call | bytes 2400000 | tf_op jit(solution)/shard_map/strips/pallas_call | solution.py:740
  132.8 2.8 %field.3 = (f32[2,2048,128]{2,1,0:T(8,128)S(1)}, f32[2,80,128]{2,1,0:T(8,128)S(1)}, f32[2,80,128]{2,1,0:T(8,128)S(1)}) custom-call(s32[8,256]{1,0:T(8,128)S(1)} %copy-done.25, s32[1]{0:T(128)} %bitcast.5.lat, f32[2,2048,128]{2,1,0:T(8,128)S(1)} %copy-done.4, f32[25,256,128]{2,1,0:T(8,128)S(1)} %copy-done, f32[8,8,4,8,128]{4,3,2,1,0:T(8,128)} %all-to-all-done.2.refs_0_, ...), custom_call_target="tpu_custom_call" | custom-call | bytes 800000 | tf_op jit(solution)/shard_map/field/pallas_call | solution.py:701
  135.6 4.7 %collective-permute-start.8 = (f32[2,80,128]{2,1,0:T(8,128)S(1)}, f32[2,80,128]{2,1,0:T(8,128)S(1)}, u32[]{:S(2)}, u32[]{:S(2)}) collective-permute-start(f32[2,80,128]{2,1,0:T(8,128)S(1)} %get-tuple-element.60), channel_id=1, source_target_pairs={{0,8},{8,16},{16,24},{1,9},{9,17},{17,25},{2,10},{10,18},{18,26},{... | collective-permute-start | bytes 245768 | tf_op jit(solution)/shard_map/ppermute | solution.py:542
  142.5 4.8 %collective-permute-done.9.below = f32[2,80,128]{2,1,0:T(8,128)S(1)} collective-permute-done((f32[2,80,128]{2,1,0:T(8,128)S(1)}, f32[2,80,128]{2,1,0:T(8,128)S(1)}, u32[]{:S(2)}, u32[]{:S(2)}) %collective-permute-start.9) | collective-permute-done | bytes 81952 | tf_op jit(solution)/shard_map/ppermute | solution.py:542
  147.3 3.2 %edges.5 = (f32[2240,128]{1,0:T(8,128)S(1)}, f32[560,128]{1,0:T(8,128)S(1)}, f32[560,128]{1,0:T(8,128)S(1)}) custom-call(f32[2,2048,128]{2,1,0:T(8,128)S(1)} %get-tuple-element.65.field, f32[2,80,128]{2,1,0:T(8,128)S(1)} %collective-permute-done.8.above, f32[2,80,128]{2,1,0:T(8,128)S(1)} %collective-permute-done.9.below), custom_call_target="tpu_custom_call" | custom-call | bytes 600000 | tf_op jit(solution)/shard_map/edges/pallas_call | solution.py:611
  150.5 3.5 %collective-permute-start.11 = (f32[560,128]{1,0:T(8,128)S(1)}, f32[560,128]{1,0:T(8,128)S(1)}, u32[]{:S(2)}, u32[]{:S(2)}) collective-permute-start(f32[560,128]{1,0:T(8,128)S(1)} %get-tuple-element.64), channel_id=1, source_target_pairs={{1,0},{2,1},{3,2},{4,3},{5,4},{6,5},{7,6},{0,7},{9,8},{10,9},{11,1... | collective-permute-start | bytes 860168 | tf_op jit(solution)/shard_map/ppermute | solution.py:548
  154.0 13.7 %own.3.refs_5_ = f32[2,2048,128]{2,1,0:T(8,128)S(1)} custom-call(f32[2,2048,128]{2,1,0:T(8,128)S(1)} %get-tuple-element.65.field, f32[2,80,128]{2,1,0:T(8,128)S(1)} %collective-permute-done.8.above, f32[2,80,128]{2,1,0:T(8,128)S(1)} %collective-permute-done.9.below, f32[5,288,128]{2,1,0:T(8,128)S(1)} %copy-done.14), custom_call_target="tpu_custom_call" | custom-call | bytes 2400000 | tf_op jit(solution)/shard_map/own/pallas_call | solution.py:712
  167.8 13.9 %strips.3 = (f32[25,256,128]{2,1,0:T(8,128)}, f32[256,128]{1,0:T(8,128)S(1)}) custom-call(s32[8,256]{1,0:T(8,128)S(1)} %copy-done.25, f32[2240,128]{1,0:T(8,128)S(1)} %get-tuple-element.62.refs_1_, f32[560,128]{1,0:T(8,128)S(1)} %collective-permute-done.10.refs_2_, f32[560,128]{1,0:T(8,128)S(1)} %collective-permute-done.11.refs_3_, ...), custom_call_target="tpu_custom_call", output_to_operand_aliasing={{0}: (9, {})} | custom-call | bytes 2400000 | tf_op jit(solution)/shard_map/strips/pallas_call | solution.py:740
  181.7 12.4 %all_to_all.25 = f32[32,8,128]{2,1,0:T(8,128)S(1)} all-to-all(f32[32,8,128]{2,1,0:T(8,128)S(1)} %bitcast.24), channel_id=1, replica_groups=mesh['lat'=4,'lon'=8] {'lat','lon'}, dimensions={0} | all-to-all | bytes 262144 | tf_op jit(solution)/shard_map/all_to_all | solution.py:763
  (112 shorter events, 39.6 us)
Async XLA Ops:
  3.1 15.5 %all-to-all-start = ((f32[32,8,128]{2,1,0:T(8,128)}), f32[32,8,128]{2,1,0:T(8,128)S(1)}, u32[]{:S(2)}, u32[]{:S(2)}) async-start(f32[32,8,128]{2,1,0:T(8,128)} %bitcast.30), calls=%async_computation | async-start | bytes 262144 | tf_op jit(solution)/shard_map/all_to_all | solution.py:651
  11.9 19.6 %copy-start.17 = (f32[1,2048,128]{2,1,0:T(8,128)}, f32[1,2048,128]{2,1,0:T(8,128)S(1)}, u32[]{:S(2)}) copy-start(f32[1,2048,128]{2,1,0:T(8,128)S(1)} %get-tuple-element.40.field) | copy-start | bytes 3145732
  18.6 33.7 %all-to-all-start.1 = ((f32[8,9,4,8,128]{4,3,2,1,0:T(8,128)}), f32[8,9,4,8,128]{4,3,2,1,0:T(8,128)}, u32[]{:S(2)}, u32[]{:S(2)}) async-start(f32[8,9,4,8,128]{4,3,2,1,0:T(8,128)} %bitcast.17), calls=%async_computation.1 | async-start | bytes 2359296 | tf_op jit(solution)/shard_map/all_to_all | solution.py:607
  22.8 7.9 %collective-permute-start = (f32[1,80,128]{2,1,0:T(8,128)S(1)}, f32[1,80,128]{2,1,0:T(8,128)S(1)}, u32[]{:S(2)}, u32[]{:S(2)}) collective-permute-start(f32[1,80,128]{2,1,0:T(8,128)S(1)} %get-tuple-element.42), channel_id=1, source_target_pairs={{0,8},{8,16},{16,24},{1,9},{9,17},{17,25},{2,10},{10,18},{18,26},{... | collective-permute-start | bytes 122888 | tf_op jit(solution)/shard_map/ppermute | solution.py:542
  25.6 5.9 %collective-permute-start.1 = (f32[1,80,128]{2,1,0:T(8,128)S(1)}, f32[1,80,128]{2,1,0:T(8,128)S(1)}, u32[]{:S(2)}, u32[]{:S(2)}) collective-permute-start(f32[1,80,128]{2,1,0:T(8,128)S(1)} %get-tuple-element.43), channel_id=1, source_target_pairs={{8,0},{16,8},{24,16},{9,1},{17,9},{25,17},{10,2},{18,10},{26,18},{... | collective-permute-start | bytes 122888 | tf_op jit(solution)/shard_map/ppermute | solution.py:542
  35.8 20.7 %copy-start = (f32[25,256,128]{2,1,0:T(8,128)S(1)}, f32[25,256,128]{2,1,0:T(8,128)}, u32[]{:S(2)}) copy-start(f32[25,256,128]{2,1,0:T(8,128)} %refs_8_.3) | copy-start | bytes 9830404
  35.8 20.7 %copy-start.25 = (s32[8,256]{1,0:T(8,128)S(1)}, s32[8,256]{1,0:T(8,128)}, u32[]{:S(2)}) copy-start(s32[8,256]{1,0:T(8,128)} %get-tuple-element.37.loc.refs_0_) | copy-start | bytes 24580
  52.2 46.3 %all-to-all-start.2 = ((f32[8,8,4,8,128]{4,3,2,1,0:T(8,128)}), f32[8,8,4,8,128]{4,3,2,1,0:T(8,128)}, u32[]{:S(2)}, u32[]{:S(2)}) async-start(f32[8,8,4,8,128]{4,3,2,1,0:T(8,128)} %bitcast.26), calls=%async_computation.2 | async-start | bytes 2097152 | tf_op jit(solution)/shard_map/all_to_all | solution.py:607
  60.5 18.6 %copy-start.39 = (f32[8,32,8,128]{3,2,1,0:T(8,128)S(1)}, f32[8,32,8,128]{3,2,1,0:T(8,128)}, u32[]{:S(2)}) copy-start(f32[8,32,8,128]{3,2,1,0:T(8,128)} %get-tuple-element.70) | copy-start | bytes 3145732
  60.5 11.8 %collective-permute-start.2 = (f32[2,80,128]{2,1,0:T(8,128)S(1)}, f32[2,80,128]{2,1,0:T(8,128)S(1)}, u32[]{:S(2)}, u32[]{:S(2)}) collective-permute-start(f32[2,80,128]{2,1,0:T(8,128)S(1)} %get-tuple-element.46), channel_id=1, source_target_pairs={{0,8},{8,16},{16,24},{1,9},{9,17},{17,25},{2,10},{10,18},{18,26},{... | collective-permute-start | bytes 245768 | tf_op jit(solution)/shard_map/ppermute | solution.py:542
  63.4 9.0 %collective-permute-start.3 = (f32[2,80,128]{2,1,0:T(8,128)S(1)}, f32[2,80,128]{2,1,0:T(8,128)S(1)}, u32[]{:S(2)}, u32[]{:S(2)}) collective-permute-start(f32[2,80,128]{2,1,0:T(8,128)S(1)} %get-tuple-element.47), channel_id=1, source_target_pairs={{8,0},{16,8},{24,16},{9,1},{17,9},{25,17},{10,2},{18,10},{26,18},{... | collective-permute-start | bytes 245768 | tf_op jit(solution)/shard_map/ppermute | solution.py:542
  68.8 26.8 %collective-permute-start.6 = (f32[560,128]{1,0:T(8,128)S(1)}, f32[560,128]{1,0:T(8,128)S(1)}, u32[]{:S(2)}, u32[]{:S(2)}) collective-permute-start(f32[560,128]{1,0:T(8,128)S(1)} %get-tuple-element.52), channel_id=1, source_target_pairs={{0,1},{1,2},{2,3},{3,4},{4,5},{5,6},{6,7},{7,0},{8,9},{9,10},{10,1... | collective-permute-start | bytes 860168 | tf_op jit(solution)/shard_map/ppermute | solution.py:548
  68.9 27.5 %collective-permute-start.7 = (f32[560,128]{1,0:T(8,128)S(1)}, f32[560,128]{1,0:T(8,128)S(1)}, u32[]{:S(2)}, u32[]{:S(2)}) collective-permute-start(f32[560,128]{1,0:T(8,128)S(1)} %get-tuple-element.53), channel_id=1, source_target_pairs={{1,0},{2,1},{3,2},{4,3},{5,4},{6,5},{7,6},{0,7},{9,8},{10,9},{11,1... | collective-permute-start | bytes 860168 | tf_op jit(solution)/shard_map/ppermute | solution.py:548
  75.5 21.5 %collective-permute-start.4 = (f32[560,128]{1,0:T(8,128)S(1)}, f32[560,128]{1,0:T(8,128)S(1)}, u32[]{:S(2)}, u32[]{:S(2)}) collective-permute-start(f32[560,128]{1,0:T(8,128)S(1)} %get-tuple-element.50), channel_id=1, source_target_pairs={{0,1},{1,2},{2,3},{3,4},{4,5},{5,6},{6,7},{7,0},{8,9},{9,10},{10,1... | collective-permute-start | bytes 860168 | tf_op jit(solution)/shard_map/ppermute | solution.py:548
  75.6 22.2 %collective-permute-start.5 = (f32[560,128]{1,0:T(8,128)S(1)}, f32[560,128]{1,0:T(8,128)S(1)}, u32[]{:S(2)}, u32[]{:S(2)}) collective-permute-start(f32[560,128]{1,0:T(8,128)S(1)} %get-tuple-element.51), channel_id=1, source_target_pairs={{1,0},{2,1},{3,2},{4,3},{5,4},{6,5},{7,6},{0,7},{9,8},{10,9},{11,1... | collective-permute-start | bytes 860168 | tf_op jit(solution)/shard_map/ppermute | solution.py:548
  98.5 32.7 %all-to-all-start.3 = ((f32[8,8,4,8,128]{4,3,2,1,0:T(8,128)}), f32[8,8,4,8,128]{4,3,2,1,0:T(8,128)}, u32[]{:S(2)}, u32[]{:S(2)}) async-start(f32[8,8,4,8,128]{4,3,2,1,0:T(8,128)} %bitcast.27), calls=%async_computation.3 | async-start | bytes 2097152 | tf_op jit(solution)/shard_map/all_to_all | solution.py:607
  135.6 18.4 %copy-start.14 = (f32[5,288,128]{2,1,0:T(8,128)S(1)}, f32[5,288,128]{2,1,0:T(8,128)}, u32[]{:S(2)}) copy-start(f32[5,288,128]{2,1,0:T(8,128)} %copy-done.12) | copy-start | bytes 2211844
  135.6 6.9 %collective-permute-start.8 = (f32[2,80,128]{2,1,0:T(8,128)S(1)}, f32[2,80,128]{2,1,0:T(8,128)S(1)}, u32[]{:S(2)}, u32[]{:S(2)}) collective-permute-start(f32[2,80,128]{2,1,0:T(8,128)S(1)} %get-tuple-element.60), channel_id=1, source_target_pairs={{0,8},{8,16},{16,24},{1,9},{9,17},{17,25},{2,10},{10,18},{18,26},{... | collective-permute-start | bytes 245768 | tf_op jit(solution)/shard_map/ppermute | solution.py:542
  140.3 7.0 %collective-permute-start.9 = (f32[2,80,128]{2,1,0:T(8,128)S(1)}, f32[2,80,128]{2,1,0:T(8,128)S(1)}, u32[]{:S(2)}, u32[]{:S(2)}) collective-permute-start(f32[2,80,128]{2,1,0:T(8,128)S(1)} %get-tuple-element.61), channel_id=1, source_target_pairs={{8,0},{16,8},{24,16},{9,1},{17,9},{25,17},{10,2},{18,10},{26,18},{... | collective-permute-start | bytes 245768 | tf_op jit(solution)/shard_map/ppermute | solution.py:542
  150.4 17.4 %collective-permute-start.10 = (f32[560,128]{1,0:T(8,128)S(1)}, f32[560,128]{1,0:T(8,128)S(1)}, u32[]{:S(2)}, u32[]{:S(2)}) collective-permute-start(f32[560,128]{1,0:T(8,128)S(1)} %get-tuple-element.63), channel_id=1, source_target_pairs={{0,1},{1,2},{2,3},{3,4},{4,5},{5,6},{6,7},{7,0},{8,9},{9,10},{10,1... | collective-permute-start | bytes 860168 | tf_op jit(solution)/shard_map/ppermute | solution.py:548
  150.5 17.3 %collective-permute-start.11 = (f32[560,128]{1,0:T(8,128)S(1)}, f32[560,128]{1,0:T(8,128)S(1)}, u32[]{:S(2)}, u32[]{:S(2)}) collective-permute-start(f32[560,128]{1,0:T(8,128)S(1)} %get-tuple-element.64), channel_id=1, source_target_pairs={{1,0},{2,1},{3,2},{4,3},{5,4},{6,5},{7,6},{0,7},{9,8},{10,9},{11,1... | collective-permute-start | bytes 860168 | tf_op jit(solution)/shard_map/ppermute | solution.py:548
  154.0 13.8 %copy-start.11 = (f32[1024,128]{1,0:T(8,128)S(1)}, f32[1024,128]{1,0:T(8,128)}, u32[]{:S(2)}) copy-start(f32[1024,128]{1,0:T(8,128)} %get-tuple-element.39.high.refs_7_) | copy-start | bytes 1572868
  154.0 13.8 %copy-start.16 = (f32[5,288,128]{2,1,0:T(8,128)S(1)}, f32[5,288,128]{2,1,0:T(8,128)}, u32[]{:S(2)}) copy-start(f32[5,288,128]{2,1,0:T(8,128)} %copy-done.15) | copy-start | bytes 2211844
  167.8 26.3 %copy-start.38 = (s32[1,512]{1,0:T(1,128)S(1)}, s32[1,512]{1,0:T(1,128)}, u32[]{:S(2)}) copy-start(s32[1,512]{1,0:T(1,128)} %get-tuple-element.69.slot) | copy-start | bytes 6148
  (33 other events, 133.3 us)

commit v4 on v1

--- a/solution.py
+++ b/solution.py
@@ -34,7 +34,7 @@
 
 
 def cost(micros):
-    return pl.CostEstimate(flops=0, bytes_accessed=int(micros * 3.6e6), transcendentals=0)
+    return pl.CostEstimate(flops=0, bytes_accessed=int(micros * 2e5), transcendentals=0)
 
 
 def iota(shape, dim):
@@ -674,8 +674,21 @@
         )(loc, recv, low, high)
 
     observed = [scatter(0, LARGE), scatter(1, SMALL)]
-    pieces.append(tile_exchange(1, pieces[0], observed[0], own_coef, coef_west, coef_east))
+    pieces.append(tile_exchange(1, pieces[0], observed[0], own_coef))
     shift_space = pltpu.VMEM((2 * LANES, 2 * LANES), jnp.bfloat16)
+    def first_field(chunk, piece):
+        first = sum(CHUNKS[:chunk])
+        sizes = GROUPS[first : first + CHUNKS[chunk]]
+        return call(
+            functools.partial(field_kernel, starts[first], sizes, n_lon, group, cap),
+            field_shapes(CHUNKS[chunk]),
+            4,
+            "field",
+            in_specs=[smem, smem, vmem, vmem, hbm],
+            scratch_shapes=[pltpu.VMEM((sum(sizes), lat_cells, LANES), f32), pltpu.SemaphoreType.DMA],
+        )(loc, lat, piece, observed[chunk], norm_factor)
+
+    fields = [first_field(0, pieces[0])]
     smoothed = None
     sampled = []
     first = 0
@@ -683,14 +696,7 @@
         sizes = GROUPS[first : first + groups]
         begin = starts[first]
         own_levels = (sum(sizes), lat_cells, LANES)
-        field = call(
-            functools.partial(field_kernel, begin, sizes, n_lon, group, cap),
-            field_shapes(groups),
-            4,
-            "field",
-            in_specs=[smem, smem, vmem, vmem, hbm],
-            scratch_shapes=[pltpu.VMEM(own_levels, f32), pltpu.SemaphoreType.DMA],
-        )(loc, lat, pieces[chunk], observed[chunk], norm_factor)
+        field = fields[chunk]
         field, above, below, strips, from_west, from_east = halo(*field, groups)
         mid_shape = (groups, lat_cells * SUB, LANES)
         win_shape = (groups, win_rows * SUB, LANES)
@@ -702,15 +708,14 @@
             scratch_shapes=[pltpu.VMEM(win_shape, f32), pltpu.VMEM(win_shape, f32), shift_space],
         )(after(field, strips), above, below, own_coef)
         if chunk == 0:
+            fields.append(first_field(1, after(pieces[1], mid)))
             strip_coef = call(
                 strip_coef_kernel,
                 arrays((5, win_rows, LANES))[0],
                 3,
                 "strip_coef",
                 scratch_shapes=[pltpu.VMEM(((win_rows + SUB) * SUB, LANES), f32)],
-            )(after(coef_strips, mid, *observed[1:]), coef_west, coef_east)
-        if chunk + 1 < len(CHUNKS):
-            pieces[chunk + 1] = after(pieces[chunk + 1], mid)
+            )(after(coef_strips, mid, fields[1][1]), coef_west, coef_east)
         operands = [loc, strips, from_west, from_east, strip_coef, mid, low, high, norm_factor]
         specs = [smem] + [vmem] * 7 + [hbm]
         aliases = {}

time: 189 us -> 192 us (1.016)
  starting transfers between devices: 40.3 us -> 35.3 us
  Pallas kernels: 90.9 us -> 95.3 us
    ppermute x6, starting transfers between devices: 10.7 us -> 7.45 us  [exchange_columns(): return (lax.ppermute(east, 'lon', pairs), lax.ppermute(west, 'lon', back))]
    all_to_all x2, waiting for transfers between devices: 13.9 us -> 16.6 us  [tile_exchange(): return lax.all_to_all(piece, 'lon', split_axis=0, concat_axis=0, tiled=True)]
    pallas_call x2, Pallas kernels: 27.5 us -> 29.5 us  [on_device(): call(functools.partial(strip_kernel, sizes, begin, len(aliases), len(earl...]
  transfers between devices with their start and end apart: 15 -> 15, of which waited for: 7 -> 6; matrix products, arithmetic and copies ran while one was open for 1% -> 1% of each run, Pallas kernels for 38% -> 40%
where the time goes in v4:
time: 192 us; the launch traced here: 191 us
  Pallas kernels  95.3 us (50%)
  starting transfers between devices  35.3 us (18%)
  waiting for transfers between devices  27.7 us (14%)
  local copies, waits for them, and re-layouts  17.6 us (9%)
  blocking collectives  13.9 us (7%)
    pallas_call x2, Pallas kernels, on_device(): call(functools.partial(strip_kernel, sizes, begin, len(aliases), len(earl...  29.5 us
    pallas_call x2, Pallas kernels, on_device(): call(own_kernel, arrays(mid_shape)[0], 6 * groups, 'own', scratch_shapes=...  28.3 us
    all_to_all x2, waiting for transfers between devices, tile_exchange(): return lax.all_to_all(piece, 'lon', split_axis=0, concat_axis=0, tiled=True)  16.6 us
    unnamed x70, local copies, waits for them, and re-layouts  14.8 us
    all_to_all x1, blocking collectives, on_device(): lax.all_to_all(back.reshape(devices, rows // devices, LANES), both, split...  13.9 us
    pallas_call x2, Pallas kernels, scatter(): call(functools.partial(scatter_kernel, first), arrays((CHUNKS[chunk], lat...  13.3 us
    ppermute x6, starting transfers between devices, exchange_rows(): return (lax.ppermute(up, 'lat', pairs), lax.ppermute(down, 'lat', back))  12.3 us
    pallas_call x3, Pallas kernels, halo(): call(edges_kernel, arrays((ext_rows * SUB, LANES), (span * SUB, LANES), (...  10.1 us
  transfers between devices with their start and end apart: 15, of which 6 were waited for; matrix products, arithmetic and copies ran while one was open for 1% of the time, Pallas kernels for 40%

profile of v4, /device:TPU:0, one launch (start us, length us, event | category | flops | bytes accessed | tf_op | source)
XLA Modules:
  0.0 190.9 jit_solution(5888070878118295783)
XLA Ops:
  3.1 7.3 %all-to-all-start = ((f32[32,8,128]{2,1,0:T(8,128)}), f32[32,8,128]{2,1,0:T(8,128)S(1)}, u32[]{:S(2)}, u32[]{:S(2)}) async-start(f32[32,8,128]{2,1,0:T(8,128)} %bitcast.25), calls=%async_computation | async-start | bytes 262144 | tf_op jit(solution)/shard_map/all_to_all | solution.py:646
  11.9 6.6 %all-to-all-done = f32[32,8,128]{2,1,0:T(8,128)S(1)} async-done(((f32[32,8,128]{2,1,0:T(8,128)}), f32[32,8,128]{2,1,0:T(8,128)S(1)}, u32[]{:S(2)}, u32[]{:S(2)}) %all-to-all-start) | async-done | bytes 131104 | tf_op jit(solution)/shard_map/all_to_all | solution.py:646
  18.6 3.6 %all-to-all-start.1 = ((f32[8,9,4,8,128]{4,3,2,1,0:T(8,128)}), f32[8,9,4,8,128]{4,3,2,1,0:T(8,128)S(1)}, u32[]{:S(2)}, u32[]{:S(2)}) async-start(f32[8,9,4,8,128]{4,3,2,1,0:T(8,128)} %bitcast.24), calls=%async_computation.1 | async-start | bytes 2359296 | tf_op jit(solution)/shard_map/all_to_all | solution.py:602
  22.1 2.8 %collective-permute-start = (f32[1,80,128]{2,1,0:T(8,128)S(1)}, f32[1,80,128]{2,1,0:T(8,128)S(1)}, u32[]{:S(2)}, u32[]{:S(2)}) collective-permute-start(f32[1,80,128]{2,1,0:T(8,128)S(1)} %get-tuple-element.41), channel_id=1, source_target_pairs={{0,8},{8,16},{16,24},{1,9},{9,17},{17,25},{2,10},{10,18},{18,26},{... | collective-permute-start | bytes 122888 | tf_op jit(solution)/shard_map/ppermute | solution.py:537
  28.0 2.9 %collective-permute-done.1.below = f32[1,80,128]{2,1,0:T(8,128)S(1)} collective-permute-done((f32[1,80,128]{2,1,0:T(8,128)S(1)}, f32[1,80,128]{2,1,0:T(8,128)S(1)}, u32[]{:S(2)}, u32[]{:S(2)}) %collective-permute-start.1) | collective-permute-done | bytes 40992 | tf_op jit(solution)/shard_map/ppermute | solution.py:537
  32.4 2.8 %place.1 = (f32[1024,128]{1,0:T(8,128)}, f32[1024,128]{1,0:T(8,128)}, s32[8,256]{1,0:T(8,128)}) custom-call(f32[256,128]{1,0:T(8,128)} %bitcast.16), custom_call_target="tpu_custom_call" | custom-call | bytes 400000 | tf_op jit(solution)/shard_map/place/pallas_call | solution.py:655
  35.2 7.6 %scatter.2.obs = f32[2,2048,128]{2,1,0:T(8,128)} custom-call(s32[8,256]{1,0:T(8,128)} %get-tuple-element.36.loc.refs_0_, f32[256,128]{1,0:T(8,128)} %bitcast.17, f32[1024,128]{1,0:T(8,128)} %get-tuple-element.39.low.refs_6_, f32[1024,128]{1,0:T(8,128)} %get-tuple-element.40.high.refs_7_), custom_call_target="tpu_custom_call" | custom-call | bytes 1800000 | tf_op jit(solution)/shard_map/scatter/pallas_call | solution.py:666
  42.8 8.6 %all-to-all-done.1.tiles = f32[8,9,4,8,128]{4,3,2,1,0:T(8,128)S(1)} async-done(((f32[8,9,4,8,128]{4,3,2,1,0:T(8,128)}), f32[8,9,4,8,128]{4,3,2,1,0:T(8,128)S(1)}, u32[]{:S(2)}, u32[]{:S(2)}) %all-to-all-start.1) | async-done | bytes 1179680 | tf_op jit(solution)/shard_map/all_to_all | solution.py:602
  52.5 4.6 %all-to-all-start.2 = ((f32[8,16,4,8,128]{4,3,2,1,0:T(8,128)}), f32[8,16,4,8,128]{4,3,2,1,0:T(8,128)}, u32[]{:S(2)}, u32[]{:S(2)}) async-start(f32[8,16,4,8,128]{4,3,2,1,0:T(8,128)} %bitcast.21), calls=%async_computation.2 | async-start | bytes 4194304 | tf_op jit(solution)/shard_map/all_to_all | solution.py:602
  58.4 3.8 %edges.5 = (f32[2240,128]{1,0:T(8,128)S(1)}, f32[560,128]{1,0:T(8,128)}, f32[560,128]{1,0:T(8,128)S(1)}) custom-call(f32[1,2048,128]{2,1,0:T(8,128)S(1)} %copy-done.16, f32[1,80,128]{2,1,0:T(8,128)S(1)} %collective-permute-done.above, f32[1,80,128]{2,1,0:T(8,128)S(1)} %collective-permute-done.1.below), custom_call_target="tpu_custom_call" | custom-call | bytes 600000 | tf_op jit(solution)/shard_map/edges/pallas_call | solution.py:606
  68.8 2.7 %collective-permute-start.2 = (f32[2,80,128]{2,1,0:T(8,128)S(1)}, f32[2,80,128]{2,1,0:T(8,128)S(1)}, u32[]{:S(2)}, u32[]{:S(2)}) collective-permute-start(f32[2,80,128]{2,1,0:T(8,128)S(1)} %get-tuple-element.45), channel_id=1, source_target_pairs={{0,8},{8,16},{16,24},{1,9},{9,17},{17,25},{2,10},{10,18},{18,26},{... | collective-permute-start | bytes 245768 | tf_op jit(solution)/shard_map/ppermute | solution.py:537
  73.0 5.7 %scatter.3.obs = f32[2,2048,128]{2,1,0:T(8,128)S(1)} custom-call(s32[8,256]{1,0:T(8,128)S(1)} %copy-done.23, f32[256,128]{1,0:T(8,128)S(1)} %bitcast.18, f32[1024,128]{1,0:T(8,128)S(1)} %copy-done.6, f32[1024,128]{1,0:T(8,128)S(1)} %copy-done.8), custom_call_target="tpu_custom_call" | custom-call | bytes 1800000 | tf_op jit(solution)/shard_map/scatter/pallas_call | solution.py:666
  80.1 3.2 %edges.3 = (f32[2240,128]{1,0:T(8,128)S(1)}, f32[560,128]{1,0:T(8,128)S(1)}, f32[560,128]{1,0:T(8,128)S(1)}) custom-call(f32[2,2048,128]{2,1,0:T(8,128)S(1)} %get-tuple-element.48.field, f32[2,80,128]{2,1,0:T(8,128)S(1)} %collective-permute-done.2.above, f32[2,80,128]{2,1,0:T(8,128)S(1)} %collective-permute-done.3.below), custom_call_target="tpu_custom_call" | custom-call | bytes 600000 | tf_op jit(solution)/shard_map/edges/pallas_call | solution.py:606
  85.8 14.1 %own.2.refs_5_ = f32[2,2048,128]{2,1,0:T(8,128)S(1)} custom-call(f32[2,2048,128]{2,1,0:T(8,128)S(1)} %get-tuple-element.48.field, f32[2,80,128]{2,1,0:T(8,128)S(1)} %collective-permute-done.2.above, f32[2,80,128]{2,1,0:T(8,128)S(1)} %collective-permute-done.3.below, f32[5,288,128]{2,1,0:T(8,128)S(1)} %copy-done.11), custom_call_target="tpu_custom_call" | custom-call | bytes 2400000 | tf_op jit(solution)/shard_map/own/pallas_call | solution.py:703
  101.3 8.0 %all-to-all-done.2.tiles = f32[8,16,4,8,128]{4,3,2,1,0:T(8,128)} async-done(((f32[8,16,4,8,128]{4,3,2,1,0:T(8,128)}), f32[8,16,4,8,128]{4,3,2,1,0:T(8,128)}, u32[]{:S(2)}, u32[]{:S(2)}) %all-to-all-start.2) | async-done | bytes 2097184 | tf_op jit(solution)/shard_map/all_to_all | solution.py:602
  110.9 3.0 %field.3 = (f32[2,2048,128]{2,1,0:T(8,128)S(1)}, f32[2,80,128]{2,1,0:T(8,128)S(1)}, f32[2,80,128]{2,1,0:T(8,128)S(1)}) custom-call(s32[8,256]{1,0:T(8,128)S(1)} %copy-done.23, s32[1]{0:T(128)} %bitcast.5.lat, f32[8,16,4,8,128]{4,3,2,1,0:T(8,128)} %all-to-all-done.2.tiles, f32[2,2048,128]{2,1,0:T(8,128)S(1)} %copy-done.4, f32[25,256,128]{2,1,0:T(8,128)S(1)} %copy-done), custom_call_target="tpu_custom_call" | custom-call | bytes 800000 | tf_op jit(solution)/shard_map/field/pallas_call | solution.py:682
  113.9 2.7 %collective-permute-start.4 = (f32[2,80,128]{2,1,0:T(8,128)S(1)}, f32[2,80,128]{2,1,0:T(8,128)S(1)}, u32[]{:S(2)}, u32[]{:S(2)}) collective-permute-start(f32[2,80,128]{2,1,0:T(8,128)S(1)} %get-tuple-element.51), channel_id=1, source_target_pairs={{0,8},{8,16},{16,24},{1,9},{9,17},{17,25},{2,10},{10,18},{18,26},{... | collective-permute-start | bytes 245768 | tf_op jit(solution)/shard_map/ppermute | solution.py:537
  118.7 2.9 %collective-permute-start.11 = (f32[560,128]{1,0:T(8,128)S(1)}, f32[560,128]{1,0:T(8,128)S(1)}, u32[]{:S(2)}, u32[]{:S(2)}) collective-permute-start(f32[560,128]{1,0:T(8,128)S(1)} %copy-done.32), channel_id=1, source_target_pairs={{1,0},{2,1},{3,2},{4,3},{5,4},{6,5},{7,6},{0,7},{9,8},{10,9},{11,1... | collective-permute-start | bytes 860168 | tf_op jit(solution)/shard_map/ppermute | solution.py:543
  123.0 3.2 %edges.4 = (f32[2240,128]{1,0:T(8,128)S(1)}, f32[560,128]{1,0:T(8,128)S(1)}, f32[560,128]{1,0:T(8,128)S(1)}) custom-call(f32[2,2048,128]{2,1,0:T(8,128)S(1)} %get-tuple-element.60.field, f32[2,80,128]{2,1,0:T(8,128)S(1)} %collective-permute-done.4.above, f32[2,80,128]{2,1,0:T(8,128)S(1)} %collective-permute-done.5.below), custom_call_target="tpu_custom_call" | custom-call | bytes 600000 | tf_op jit(solution)/shard_map/edges/pallas_call | solution.py:606
  126.2 3.5 %collective-permute-start.7 = (f32[560,128]{1,0:T(8,128)S(1)}, f32[560,128]{1,0:T(8,128)S(1)}, u32[]{:S(2)}, u32[]{:S(2)}) collective-permute-start(f32[560,128]{1,0:T(8,128)S(1)} %get-tuple-element.55), channel_id=1, source_target_pairs={{1,0},{2,1},{3,2},{4,3},{5,4},{6,5},{7,6},{0,7},{9,8},{10,9},{11,1... | collective-permute-start | bytes 860168 | tf_op jit(solution)/shard_map/ppermute | solution.py:543
  132.3 14.6 %strips.2 = (f32[25,256,128]{2,1,0:T(8,128)}, f32[2,2,32,128]{3,2,1,0:T(8,128)S(1)}) custom-call(s32[8,256]{1,0:T(8,128)S(1)} %copy-done.23, f32[2240,128]{1,0:T(8,128)S(1)} %copy-done.20, f32[560,128]{1,0:T(8,128)S(1)} %collective-permute-done.10.refs_2_, f32[560,128]{1,0:T(8,128)S(1)} %collective-permute-done.11.refs_3_, ...), custom_call_target="tpu_custom_call" | custom-call | bytes 2400000 | tf_op jit(solution)/shard_map/strips/pallas_call | solution.py:730
  146.9 14.1 %own.3.refs_5_ = f32[2,2048,128]{2,1,0:T(8,128)S(1)} custom-call(f32[2,2048,128]{2,1,0:T(8,128)S(1)} %get-tuple-element.60.field, f32[2,80,128]{2,1,0:T(8,128)S(1)} %collective-permute-done.4.above, f32[2,80,128]{2,1,0:T(8,128)S(1)} %collective-permute-done.5.below, f32[5,288,128]{2,1,0:T(8,128)S(1)} %copy-done.12), custom_call_target="tpu_custom_call" | custom-call | bytes 2400000 | tf_op jit(solution)/shard_map/own/pallas_call | solution.py:703
  161.1 14.9 %strips.3 = (f32[25,256,128]{2,1,0:T(8,128)}, f32[256,128]{1,0:T(8,128)S(1)}) custom-call(s32[8,256]{1,0:T(8,128)S(1)} %copy-done.23, f32[2240,128]{1,0:T(8,128)S(1)} %get-tuple-element.53.refs_1_, f32[560,128]{1,0:T(8,128)S(1)} %collective-permute-done.6.refs_2_, f32[560,128]{1,0:T(8,128)S(1)} %collective-permute-done.7.refs_3_, ...), custom_call_target="tpu_custom_call", output_to_operand_aliasing={{0}: (9, {})} | custom-call | bytes 2400000 | tf_op jit(solution)/shard_map/strips/pallas_call | solution.py:730
  176.0 13.9 %all_to_all.20 = f32[32,8,128]{2,1,0:T(8,128)S(1)} all-to-all(f32[32,8,128]{2,1,0:T(8,128)S(1)} %bitcast.20), channel_id=1, replica_groups=mesh['lat'=4,'lon'=8] {'lat','lon'}, dimensions={0} | all-to-all | bytes 262144 | tf_op jit(solution)/shard_map/all_to_all | solution.py:753
  (100 shorter events, 32.6 us)
Async XLA Ops:
  0.6 9.8 %slice-start = ((f32[25,32,8,128]{3,2,1,0:T(8,128)}), f32[9,32,8,128]{3,2,1,0:T(8,128)S(1)}, s32[]{:S(2)}) async-start(f32[25,32,8,128]{3,2,1,0:T(8,128)} %param.17), calls=%async_computation.4 | async-start | bytes 2359296 | tf_op jit(solution)/shard_map/slice | solution.py:598
  3.1 15.5 %all-to-all-start = ((f32[32,8,128]{2,1,0:T(8,128)}), f32[32,8,128]{2,1,0:T(8,128)S(1)}, u32[]{:S(2)}, u32[]{:S(2)}) async-start(f32[32,8,128]{2,1,0:T(8,128)} %bitcast.25), calls=%async_computation | async-start | bytes 262144 | tf_op jit(solution)/shard_map/all_to_all | solution.py:646
  11.9 19.0 %copy-start.15 = (f32[1,2048,128]{2,1,0:T(8,128)}, f32[1,2048,128]{2,1,0:T(8,128)S(1)}, u32[]{:S(2)}) copy-start(f32[1,2048,128]{2,1,0:T(8,128)S(1)} %get-tuple-element.37.field) | copy-start | bytes 3145732
  18.6 32.9 %all-to-all-start.1 = ((f32[8,9,4,8,128]{4,3,2,1,0:T(8,128)}), f32[8,9,4,8,128]{4,3,2,1,0:T(8,128)S(1)}, u32[]{:S(2)}, u32[]{:S(2)}) async-start(f32[8,9,4,8,128]{4,3,2,1,0:T(8,128)} %bitcast.24), calls=%async_computation.1 | async-start | bytes 2359296 | tf_op jit(solution)/shard_map/all_to_all | solution.py:602
  22.1 5.9 %collective-permute-start = (f32[1,80,128]{2,1,0:T(8,128)S(1)}, f32[1,80,128]{2,1,0:T(8,128)S(1)}, u32[]{:S(2)}, u32[]{:S(2)}) collective-permute-start(f32[1,80,128]{2,1,0:T(8,128)S(1)} %get-tuple-element.41), channel_id=1, source_target_pairs={{0,8},{8,16},{16,24},{1,9},{9,17},{17,25},{2,10},{10,18},{18,26},{... | collective-permute-start | bytes 122888 | tf_op jit(solution)/shard_map/ppermute | solution.py:537
  24.9 6.0 %collective-permute-start.1 = (f32[1,80,128]{2,1,0:T(8,128)S(1)}, f32[1,80,128]{2,1,0:T(8,128)S(1)}, u32[]{:S(2)}, u32[]{:S(2)}) collective-permute-start(f32[1,80,128]{2,1,0:T(8,128)S(1)} %get-tuple-element.42), channel_id=1, source_target_pairs={{8,0},{16,8},{24,16},{9,1},{17,9},{25,17},{10,2},{18,10},{26,18},{... | collective-permute-start | bytes 122888 | tf_op jit(solution)/shard_map/ppermute | solution.py:537
  52.5 11.8 %copy-start = (f32[25,256,128]{2,1,0:T(8,128)S(1)}, f32[25,256,128]{2,1,0:T(8,128)}, u32[]{:S(2)}) copy-start(f32[25,256,128]{2,1,0:T(8,128)} %refs_8_.3) | copy-start | bytes 9830404
  52.5 11.8 %copy-start.23 = (s32[8,256]{1,0:T(8,128)S(1)}, s32[8,256]{1,0:T(8,128)}, u32[]{:S(2)}) copy-start(s32[8,256]{1,0:T(8,128)} %get-tuple-element.36.loc.refs_0_) | copy-start | bytes 24580
  52.5 56.8 %all-to-all-start.2 = ((f32[8,16,4,8,128]{4,3,2,1,0:T(8,128)}), f32[8,16,4,8,128]{4,3,2,1,0:T(8,128)}, u32[]{:S(2)}, u32[]{:S(2)}) async-start(f32[8,16,4,8,128]{4,3,2,1,0:T(8,128)} %bitcast.21), calls=%async_computation.2 | async-start | bytes 4194304 | tf_op jit(solution)/shard_map/all_to_all | solution.py:602
  63.9 62.3 %collective-permute-start.8 = (f32[560,128]{1,0:T(8,128)}, f32[560,128]{1,0:T(8,128)}, u32[]{:S(2)}, u32[]{:S(2)}) collective-permute-start(f32[560,128]{1,0:T(8,128)} %get-tuple-element.58), channel_id=1, source_target_pairs={{0,1},{1,2},{2,3},{3,4},{4,5},{5,6},{6,7},{7,0},{8,9},{9,10},{10,1... | collective-permute-start | bytes 860168 | tf_op jit(solution)/shard_map/ppermute | solution.py:543
  68.8 11.3 %collective-permute-start.2 = (f32[2,80,128]{2,1,0:T(8,128)S(1)}, f32[2,80,128]{2,1,0:T(8,128)S(1)}, u32[]{:S(2)}, u32[]{:S(2)}) collective-permute-start(f32[2,80,128]{2,1,0:T(8,128)S(1)} %get-tuple-element.45), channel_id=1, source_target_pairs={{0,8},{8,16},{16,24},{1,9},{9,17},{17,25},{2,10},{10,18},{18,26},{... | collective-permute-start | bytes 245768 | tf_op jit(solution)/shard_map/ppermute | solution.py:537
  71.6 14.2 %copy-start.11 = (f32[5,288,128]{2,1,0:T(8,128)S(1)}, f32[5,288,128]{2,1,0:T(8,128)}, u32[]{:S(2)}) copy-start(f32[5,288,128]{2,1,0:T(8,128)} %copy-done.10) | copy-start | bytes 2211844
  71.6 8.5 %collective-permute-start.3 = (f32[2,80,128]{2,1,0:T(8,128)S(1)}, f32[2,80,128]{2,1,0:T(8,128)S(1)}, u32[]{:S(2)}, u32[]{:S(2)}) collective-permute-start(f32[2,80,128]{2,1,0:T(8,128)S(1)} %get-tuple-element.46), channel_id=1, source_target_pairs={{8,0},{16,8},{24,16},{9,1},{17,9},{25,17},{10,2},{18,10},{26,18},{... | collective-permute-start | bytes 245768 | tf_op jit(solution)/shard_map/ppermute | solution.py:537
  110.9 18.9 %copy-start.22 = (f32[2240,128]{1,0:T(8,128)S(1)}, f32[2240,128]{1,0:T(8,128)}, u32[]{:S(2)}) copy-start(f32[2240,128]{1,0:T(8,128)} %copy-done.21) | copy-start | bytes 3440644
  113.9 4.8 %collective-permute-start.4 = (f32[2,80,128]{2,1,0:T(8,128)S(1)}, f32[2,80,128]{2,1,0:T(8,128)S(1)}, u32[]{:S(2)}, u32[]{:S(2)}) collective-permute-start(f32[2,80,128]{2,1,0:T(8,128)S(1)} %get-tuple-element.51), channel_id=1, source_target_pairs={{0,8},{8,16},{16,24},{1,9},{9,17},{17,25},{2,10},{10,18},{18,26},{... | collective-permute-start | bytes 245768 | tf_op jit(solution)/shard_map/ppermute | solution.py:537
  116.6 6.3 %collective-permute-start.5 = (f32[2,80,128]{2,1,0:T(8,128)S(1)}, f32[2,80,128]{2,1,0:T(8,128)S(1)}, u32[]{:S(2)}, u32[]{:S(2)}) collective-permute-start(f32[2,80,128]{2,1,0:T(8,128)S(1)} %get-tuple-element.52), channel_id=1, source_target_pairs={{8,0},{16,8},{24,16},{9,1},{17,9},{25,17},{10,2},{18,10},{26,18},{... | collective-permute-start | bytes 245768 | tf_op jit(solution)/shard_map/ppermute | solution.py:537
  117.9 11.8 %collective-permute-start.9 = (f32[560,128]{1,0:T(8,128)S(1)}, f32[560,128]{1,0:T(8,128)S(1)}, u32[]{:S(2)}, u32[]{:S(2)}) collective-permute-start(f32[560,128]{1,0:T(8,128)S(1)} %copy-done.30), channel_id=1, source_target_pairs={{1,0},{2,1},{3,2},{4,3},{5,4},{6,5},{7,6},{0,7},{9,8},{10,9},{11,1... | collective-permute-start | bytes 860168 | tf_op jit(solution)/shard_map/ppermute | solution.py:543
  118.0 14.3 %collective-permute-start.10 = (f32[560,128]{1,0:T(8,128)S(1)}, f32[560,128]{1,0:T(8,128)S(1)}, u32[]{:S(2)}, u32[]{:S(2)}) collective-permute-start(f32[560,128]{1,0:T(8,128)S(1)} %copy-done.34), channel_id=1, source_target_pairs={{0,1},{1,2},{2,3},{3,4},{4,5},{5,6},{6,7},{7,0},{8,9},{9,10},{10,1... | collective-permute-start | bytes 860168 | tf_op jit(solution)/shard_map/ppermute | solution.py:543
  118.7 13.6 %collective-permute-start.11 = (f32[560,128]{1,0:T(8,128)S(1)}, f32[560,128]{1,0:T(8,128)S(1)}, u32[]{:S(2)}, u32[]{:S(2)}) collective-permute-start(f32[560,128]{1,0:T(8,128)S(1)} %copy-done.32), channel_id=1, source_target_pairs={{1,0},{2,1},{3,2},{4,3},{5,4},{6,5},{7,6},{0,7},{9,8},{10,9},{11,1... | collective-permute-start | bytes 860168 | tf_op jit(solution)/shard_map/ppermute | solution.py:543
  123.0 9.4 %copy-start.20 = (f32[2240,128]{1,0:T(8,128)S(1)}, f32[2240,128]{1,0:T(8,128)}, u32[]{:S(2)}) copy-start(f32[2240,128]{1,0:T(8,128)} %copy-done.19) | copy-start | bytes 3440644
  126.1 35.0 %collective-permute-start.6 = (f32[560,128]{1,0:T(8,128)S(1)}, f32[560,128]{1,0:T(8,128)S(1)}, u32[]{:S(2)}, u32[]{:S(2)}) collective-permute-start(f32[560,128]{1,0:T(8,128)S(1)} %get-tuple-element.54), channel_id=1, source_target_pairs={{0,1},{1,2},{2,3},{3,4},{4,5},{5,6},{6,7},{7,0},{8,9},{9,10},{10,1... | collective-permute-start | bytes 860168 | tf_op jit(solution)/shard_map/ppermute | solution.py:543
  126.2 34.9 %collective-permute-start.7 = (f32[560,128]{1,0:T(8,128)S(1)}, f32[560,128]{1,0:T(8,128)S(1)}, u32[]{:S(2)}, u32[]{:S(2)}) collective-permute-start(f32[560,128]{1,0:T(8,128)S(1)} %get-tuple-element.55), channel_id=1, source_target_pairs={{1,0},{2,1},{3,2},{4,3},{5,4},{6,5},{7,6},{0,7},{9,8},{10,9},{11,1... | collective-permute-start | bytes 860168 | tf_op jit(solution)/shard_map/ppermute | solution.py:543
  132.3 14.7 %copy-start.12 = (f32[5,288,128]{2,1,0:T(8,128)S(1)}, f32[5,288,128]{2,1,0:T(8,128)}, u32[]{:S(2)}) copy-start(f32[5,288,128]{2,1,0:T(8,128)} %copy-done.10) | copy-start | bytes 2211844
  161.1 28.8 %copy-start.28 = (s32[1,512]{1,0:T(1,128)S(1)}, s32[1,512]{1,0:T(1,128)}, u32[]{:S(2)}) copy-start(s32[1,512]{1,0:T(1,128)} %get-tuple-element.67.slot) | copy-start | bytes 6148
  (28 other events, 96.5 us)

commit v5 on v1

--- a/solution.py
+++ b/solution.py
@@ -710,7 +710,7 @@
                 scratch_shapes=[pltpu.VMEM(((win_rows + SUB) * SUB, LANES), f32)],
             )(after(coef_strips, mid, *observed[1:]), coef_west, coef_east)
         if chunk + 1 < len(CHUNKS):
-            pieces[chunk + 1] = after(pieces[chunk + 1], mid)
+            pieces[chunk + 1] = after(pieces[chunk + 1], mid, strip_coef)
         operands = [loc, strips, from_west, from_east, strip_coef, mid, low, high, norm_factor]
         specs = [smem] + [vmem] * 7 + [hbm]
         aliases = {}

time: 189 us -> 189 us (level)
    unnamed x70 -> x74, local copies, waits for them, and re-layouts: 13.2 us -> 12.6 us
where the time goes in v5:
time: 189 us; the launch traced here: 188 us
  Pallas kernels  90.9 us (48%)
  starting transfers between devices  40.3 us (21%)
  waiting for transfers between devices  26.3 us (14%)
  local copies, waits for them, and re-layouts  15.3 us (8%)
  blocking collectives  14 us (7%)
    pallas_call x2, Pallas kernels, on_device(): call(functools.partial(strip_kernel, sizes, begin, len(aliases), len(earl...  27.5 us
    pallas_call x2, Pallas kernels, on_device(): call(own_kernel, arrays(mid_shape)[0], 6 * groups, 'own', scratch_shapes=...  27.5 us
    all_to_all x1, blocking collectives, on_device(): lax.all_to_all(back.reshape(devices, rows // devices, LANES), both, split...  14 us
    pallas_call x2, Pallas kernels, scatter(): call(functools.partial(scatter_kernel, first), arrays((CHUNKS[chunk], lat...  13.3 us
    all_to_all x2, waiting for transfers between devices, tile_exchange(): return lax.all_to_all(piece, 'lon', split_axis=0, concat_axis=0, tiled=True)  12.8 us
    unnamed x74, local copies, waits for them, and re-layouts  12.6 us
    ppermute x6, starting transfers between devices, exchange_rows(): return (lax.ppermute(up, 'lat', pairs), lax.ppermute(down, 'lat', back))  12.4 us
    ppermute x6, starting transfers between devices, exchange_columns(): return (lax.ppermute(east, 'lon', pairs), lax.ppermute(west, 'lon', back))  10.7 us
  transfers between devices with their start and end apart: 15, of which 7 were waited for; matrix products, arithmetic and copies ran while one was open for 1% of the time, Pallas kernels for 38%

profile of v5, /device:TPU:0, one launch (start us, length us, event | category | flops | bytes accessed | tf_op | source)
XLA Modules:
  0.0 188.0 jit_solution(9235802540303173035)
XLA Ops:
  3.1 7.3 %all-to-all-start = ((f32[32,8,128]{2,1,0:T(8,128)}), f32[32,8,128]{2,1,0:T(8,128)S(1)}, u32[]{:S(2)}, u32[]{:S(2)}) async-start(f32[32,8,128]{2,1,0:T(8,128)} %bitcast.25), calls=%async_computation | async-start | bytes 262144 | tf_op jit(solution)/shard_map/all_to_all | solution.py:646
  11.9 6.7 %all-to-all-done = f32[32,8,128]{2,1,0:T(8,128)S(1)} async-done(((f32[32,8,128]{2,1,0:T(8,128)}), f32[32,8,128]{2,1,0:T(8,128)S(1)}, u32[]{:S(2)}, u32[]{:S(2)}) %all-to-all-start) | async-done | bytes 131104 | tf_op jit(solution)/shard_map/all_to_all | solution.py:646
  18.6 3.6 %all-to-all-start.1 = ((f32[8,9,4,8,128]{4,3,2,1,0:T(8,128)}), f32[8,9,4,8,128]{4,3,2,1,0:T(8,128)S(1)}, u32[]{:S(2)}, u32[]{:S(2)}) async-start(f32[8,9,4,8,128]{4,3,2,1,0:T(8,128)} %bitcast.24), calls=%async_computation.1 | async-start | bytes 2359296 | tf_op jit(solution)/shard_map/all_to_all | solution.py:602
  22.1 2.8 %collective-permute-start = (f32[1,80,128]{2,1,0:T(8,128)S(1)}, f32[1,80,128]{2,1,0:T(8,128)S(1)}, u32[]{:S(2)}, u32[]{:S(2)}) collective-permute-start(f32[1,80,128]{2,1,0:T(8,128)S(1)} %get-tuple-element.41), channel_id=1, source_target_pairs={{0,8},{8,16},{16,24},{1,9},{9,17},{17,25},{2,10},{10,18},{18,26},{... | collective-permute-start | bytes 122888 | tf_op jit(solution)/shard_map/ppermute | solution.py:537
  26.6 4.2 %collective-permute-done.1.below = f32[1,80,128]{2,1,0:T(8,128)S(1)} collective-permute-done((f32[1,80,128]{2,1,0:T(8,128)S(1)}, f32[1,80,128]{2,1,0:T(8,128)S(1)}, u32[]{:S(2)}, u32[]{:S(2)}) %collective-permute-start.1) | collective-permute-done | bytes 40992 | tf_op jit(solution)/shard_map/ppermute | solution.py:537
  30.8 3.1 %edges.3 = (f32[2240,128]{1,0:T(8,128)S(1)}, f32[560,128]{1,0:T(8,128)S(1)}, f32[560,128]{1,0:T(8,128)S(1)}) custom-call(f32[1,2048,128]{2,1,0:T(8,128)S(1)} %get-tuple-element.37.field, f32[1,80,128]{2,1,0:T(8,128)S(1)} %collective-permute-done.above, f32[1,80,128]{2,1,0:T(8,128)S(1)} %collective-permute-done.1.below), custom_call_target="tpu_custom_call" | custom-call | bytes 10800000 | tf_op jit(solution)/shard_map/edges/pallas_call | solution.py:606
  34.0 3.5 %collective-permute-start.3 = (f32[560,128]{1,0:T(8,128)S(1)}, f32[560,128]{1,0:T(8,128)S(1)}, u32[]{:S(2)}, u32[]{:S(2)}) collective-permute-start(f32[560,128]{1,0:T(8,128)S(1)} %get-tuple-element.44), channel_id=1, source_target_pairs={{1,0},{2,1},{3,2},{4,3},{5,4},{6,5},{7,6},{0,7},{9,8},{10,9},{11,1... | collective-permute-start | bytes 860168 | tf_op jit(solution)/shard_map/ppermute | solution.py:543
  40.5 2.8 %place.1 = (f32[1024,128]{1,0:T(8,128)}, f32[1024,128]{1,0:T(8,128)}, s32[8,256]{1,0:T(8,128)}) custom-call(f32[256,128]{1,0:T(8,128)} %bitcast.16), custom_call_target="tpu_custom_call" | custom-call | bytes 7200000 | tf_op jit(solution)/shard_map/place/pallas_call | solution.py:655
  43.3 7.6 %scatter.2.obs = f32[2,2048,128]{2,1,0:T(8,128)} custom-call(s32[8,256]{1,0:T(8,128)} %get-tuple-element.36.loc.refs_0_, f32[256,128]{1,0:T(8,128)} %bitcast.17, f32[1024,128]{1,0:T(8,128)} %get-tuple-element.39.low.refs_6_, f32[1024,128]{1,0:T(8,128)} %get-tuple-element.40.high.refs_7_), custom_call_target="tpu_custom_call" | custom-call | bytes 32400000 | tf_op jit(solution)/shard_map/scatter/pallas_call | solution.py:666
  55.6 6.4 %all-to-all-start.2 = ((f32[8,16,4,8,128]{4,3,2,1,0:T(8,128)}), f32[8,16,4,8,128]{4,3,2,1,0:T(8,128)}, u32[]{:S(2)}, u32[]{:S(2)}) async-start(f32[8,16,4,8,128]{4,3,2,1,0:T(8,128)} %bitcast.21), calls=%async_computation.2 | async-start | bytes 4194304 | tf_op jit(solution)/shard_map/all_to_all | solution.py:602
  66.5 2.7 %collective-permute-start.4 = (f32[2,80,128]{2,1,0:T(8,128)S(1)}, f32[2,80,128]{2,1,0:T(8,128)S(1)}, u32[]{:S(2)}, u32[]{:S(2)}) collective-permute-start(f32[2,80,128]{2,1,0:T(8,128)S(1)} %get-tuple-element.47), channel_id=1, source_target_pairs={{0,8},{8,16},{16,24},{1,9},{9,17},{17,25},{2,10},{10,18},{18,26},{... | collective-permute-start | bytes 245768 | tf_op jit(solution)/shard_map/ppermute | solution.py:537
  70.7 5.7 %scatter.3.obs = f32[2,2048,128]{2,1,0:T(8,128)S(1)} custom-call(s32[8,256]{1,0:T(8,128)S(1)} %copy-done.23, f32[256,128]{1,0:T(8,128)S(1)} %bitcast.18, f32[1024,128]{1,0:T(8,128)S(1)} %copy-done.6, f32[1024,128]{1,0:T(8,128)S(1)} %copy-done.8), custom_call_target="tpu_custom_call" | custom-call | bytes 32400000 | tf_op jit(solution)/shard_map/scatter/pallas_call | solution.py:666
  77.8 3.2 %edges.4 = (f32[2240,128]{1,0:T(8,128)S(1)}, f32[560,128]{1,0:T(8,128)S(1)}, f32[560,128]{1,0:T(8,128)S(1)}) custom-call(f32[2,2048,128]{2,1,0:T(8,128)S(1)} %get-tuple-element.50.field, f32[2,80,128]{2,1,0:T(8,128)S(1)} %collective-permute-done.4.above, f32[2,80,128]{2,1,0:T(8,128)S(1)} %collective-permute-done.5.below), custom_call_target="tpu_custom_call" | custom-call | bytes 10800000 | tf_op jit(solution)/shard_map/edges/pallas_call | solution.py:606
  82.1 13.7 %own.2.refs_5_ = f32[2,2048,128]{2,1,0:T(8,128)S(1)} custom-call(f32[2,2048,128]{2,1,0:T(8,128)S(1)} %get-tuple-element.50.field, f32[2,80,128]{2,1,0:T(8,128)S(1)} %collective-permute-done.4.above, f32[2,80,128]{2,1,0:T(8,128)S(1)} %collective-permute-done.5.below, f32[5,288,128]{2,1,0:T(8,128)S(1)} %copy-done.11), custom_call_target="tpu_custom_call" | custom-call | bytes 43200000 | tf_op jit(solution)/shard_map/own/pallas_call | solution.py:697
  99.6 11.5 %all-to-all-done.2.tiles = f32[8,16,4,8,128]{4,3,2,1,0:T(8,128)} async-done(((f32[8,16,4,8,128]{4,3,2,1,0:T(8,128)}), f32[8,16,4,8,128]{4,3,2,1,0:T(8,128)}, u32[]{:S(2)}, u32[]{:S(2)}) %all-to-all-start.2) | async-done | bytes 2097184 | tf_op jit(solution)/shard_map/all_to_all | solution.py:602
  112.7 3.0 %field.3 = (f32[2,2048,128]{2,1,0:T(8,128)S(1)}, f32[2,80,128]{2,1,0:T(8,128)S(1)}, f32[2,80,128]{2,1,0:T(8,128)S(1)}) custom-call(s32[8,256]{1,0:T(8,128)S(1)} %copy-done.23, s32[1]{0:T(128)} %bitcast.5.lat, f32[8,16,4,8,128]{4,3,2,1,0:T(8,128)} %all-to-all-done.2.tiles, f32[2,2048,128]{2,1,0:T(8,128)S(1)} %copy-done.4, f32[25,256,128]{2,1,0:T(8,128)S(1)} %copy-done), custom_call_target="tpu_custom_call" | custom-call | bytes 14400000 | tf_op jit(solution)/shard_map/field/pallas_call | solution.py:686
  115.7 2.9 %collective-permute-start.6 = (f32[2,80,128]{2,1,0:T(8,128)S(1)}, f32[2,80,128]{2,1,0:T(8,128)S(1)}, u32[]{:S(2)}, u32[]{:S(2)}) collective-permute-start(f32[2,80,128]{2,1,0:T(8,128)S(1)} %get-tuple-element.55), channel_id=1, source_target_pairs={{0,8},{8,16},{16,24},{1,9},{9,17},{17,25},{2,10},{10,18},{18,26},{... | collective-permute-start | bytes 245768 | tf_op jit(solution)/shard_map/ppermute | solution.py:537
  120.0 3.5 %collective-permute-start.11 = (f32[560,128]{1,0:T(8,128)S(1)}, f32[560,128]{1,0:T(8,128)S(1)}, u32[]{:S(2)}, u32[]{:S(2)}) collective-permute-start(f32[560,128]{1,0:T(8,128)S(1)} %copy-done.34), channel_id=1, source_target_pairs={{1,0},{2,1},{3,2},{4,3},{5,4},{6,5},{7,6},{0,7},{9,8},{10,9},{11,1... | collective-permute-start | bytes 860168 | tf_op jit(solution)/shard_map/ppermute | solution.py:543
  125.0 3.2 %edges.5 = (f32[2240,128]{1,0:T(8,128)S(1)}, f32[560,128]{1,0:T(8,128)S(1)}, f32[560,128]{1,0:T(8,128)S(1)}) custom-call(f32[2,2048,128]{2,1,0:T(8,128)S(1)} %get-tuple-element.60.field, f32[2,80,128]{2,1,0:T(8,128)S(1)} %collective-permute-done.6.above, f32[2,80,128]{2,1,0:T(8,128)S(1)} %collective-permute-done.7.below), custom_call_target="tpu_custom_call" | custom-call | bytes 10800000 | tf_op jit(solution)/shard_map/edges/pallas_call | solution.py:606
  128.2 3.5 %collective-permute-start.9 = (f32[560,128]{1,0:T(8,128)S(1)}, f32[560,128]{1,0:T(8,128)S(1)}, u32[]{:S(2)}, u32[]{:S(2)}) collective-permute-start(f32[560,128]{1,0:T(8,128)S(1)} %get-tuple-element.59), channel_id=1, source_target_pairs={{1,0},{2,1},{3,2},{4,3},{5,4},{6,5},{7,6},{0,7},{9,8},{10,9},{11,1... | collective-permute-start | bytes 860168 | tf_op jit(solution)/shard_map/ppermute | solution.py:543
  131.8 13.6 %strips.2 = (f32[25,256,128]{2,1,0:T(8,128)}, f32[2,2,32,128]{3,2,1,0:T(8,128)S(1)}) custom-call(s32[8,256]{1,0:T(8,128)S(1)} %copy-done.23, f32[2240,128]{1,0:T(8,128)S(1)} %copy-done.20, f32[560,128]{1,0:T(8,128)S(1)} %collective-permute-done.10.refs_2_, f32[560,128]{1,0:T(8,128)S(1)} %collective-permute-done.11.refs_3_, f32[5,288,128]{2,1,0:T(8,128)S(1)} %copy-done.14, ...), custom_call_target="tpu_custom_call" | custom-call | bytes 43200000 | tf_op jit(solution)/shard_map/strips/pallas_call | solution.py:725
  145.4 13.7 %own.3.refs_5_ = f32[2,2048,128]{2,1,0:T(8,128)S(1)} custom-call(f32[2,2048,128]{2,1,0:T(8,128)S(1)} %get-tuple-element.60.field, f32[2,80,128]{2,1,0:T(8,128)S(1)} %collective-permute-done.6.above, f32[2,80,128]{2,1,0:T(8,128)S(1)} %collective-permute-done.7.below, f32[5,288,128]{2,1,0:T(8,128)S(1)} %copy-done.12), custom_call_target="tpu_custom_call" | custom-call | bytes 43200000 | tf_op jit(solution)/shard_map/own/pallas_call | solution.py:697
  159.1 13.9 %strips.3 = (f32[25,256,128]{2,1,0:T(8,128)}, f32[256,128]{1,0:T(8,128)S(1)}) custom-call(s32[8,256]{1,0:T(8,128)S(1)} %copy-done.23, f32[2240,128]{1,0:T(8,128)S(1)} %get-tuple-element.57.refs_1_, f32[560,128]{1,0:T(8,128)S(1)} %collective-permute-done.8.refs_2_, f32[560,128]{1,0:T(8,128)S(1)} %collective-permute-done.9.refs_3_, ...), custom_call_target="tpu_custom_call", output_to_operand_aliasing={{0}: (9, {})} | custom-call | bytes 43200000 | tf_op jit(solution)/shard_map/strips/pallas_call | solution.py:725
  173.0 14.0 %all_to_all.20 = f32[32,8,128]{2,1,0:T(8,128)S(1)} all-to-all(f32[32,8,128]{2,1,0:T(8,128)S(1)} %bitcast.20), channel_id=1, replica_groups=mesh['lat'=4,'lon'=8] {'lat','lon'}, dimensions={0} | all-to-all | bytes 262144 | tf_op jit(solution)/shard_map/all_to_all | solution.py:748
  (104 shorter events, 30.9 us)
Async XLA Ops:
  3.1 15.5 %all-to-all-start = ((f32[32,8,128]{2,1,0:T(8,128)}), f32[32,8,128]{2,1,0:T(8,128)S(1)}, u32[]{:S(2)}, u32[]{:S(2)}) async-start(f32[32,8,128]{2,1,0:T(8,128)} %bitcast.25), calls=%async_computation | async-start | bytes 262144 | tf_op jit(solution)/shard_map/all_to_all | solution.py:646
  18.6 18.9 %copy-start.17 = (f32[32,8,128]{2,1,0:T(8,128)}, f32[32,8,128]{2,1,0:T(8,128)S(1)}, u32[]{:S(2)}) copy-start(f32[32,8,128]{2,1,0:T(8,128)S(1)} %all-to-all-done) | copy-start | bytes 393220
  18.6 36.0 %all-to-all-start.1 = ((f32[8,9,4,8,128]{4,3,2,1,0:T(8,128)}), f32[8,9,4,8,128]{4,3,2,1,0:T(8,128)S(1)}, u32[]{:S(2)}, u32[]{:S(2)}) async-start(f32[8,9,4,8,128]{4,3,2,1,0:T(8,128)} %bitcast.24), calls=%async_computation.1 | async-start | bytes 2359296 | tf_op jit(solution)/shard_map/all_to_all | solution.py:602
  22.1 4.4 %collective-permute-start = (f32[1,80,128]{2,1,0:T(8,128)S(1)}, f32[1,80,128]{2,1,0:T(8,128)S(1)}, u32[]{:S(2)}, u32[]{:S(2)}) collective-permute-start(f32[1,80,128]{2,1,0:T(8,128)S(1)} %get-tuple-element.41), channel_id=1, source_target_pairs={{0,8},{8,16},{16,24},{1,9},{9,17},{17,25},{2,10},{10,18},{18,26},{... | collective-permute-start | bytes 122888 | tf_op jit(solution)/shard_map/ppermute | solution.py:537
  24.9 5.9 %collective-permute-start.1 = (f32[1,80,128]{2,1,0:T(8,128)S(1)}, f32[1,80,128]{2,1,0:T(8,128)S(1)}, u32[]{:S(2)}, u32[]{:S(2)}) collective-permute-start(f32[1,80,128]{2,1,0:T(8,128)S(1)} %get-tuple-element.42), channel_id=1, source_target_pairs={{8,0},{16,8},{24,16},{9,1},{17,9},{25,17},{10,2},{18,10},{26,18},{... | collective-permute-start | bytes 122888 | tf_op jit(solution)/shard_map/ppermute | solution.py:537
  33.9 17.9 %collective-permute-start.2 = (f32[560,128]{1,0:T(8,128)S(1)}, f32[560,128]{1,0:T(8,128)S(1)}, u32[]{:S(2)}, u32[]{:S(2)}) collective-permute-start(f32[560,128]{1,0:T(8,128)S(1)} %get-tuple-element.43), channel_id=1, source_target_pairs={{0,1},{1,2},{2,3},{3,4},{4,5},{5,6},{6,7},{7,0},{8,9},{9,10},{10,1... | collective-permute-start | bytes 860168 | tf_op jit(solution)/shard_map/ppermute | solution.py:543
  34.0 18.5 %collective-permute-start.3 = (f32[560,128]{1,0:T(8,128)S(1)}, f32[560,128]{1,0:T(8,128)S(1)}, u32[]{:S(2)}, u32[]{:S(2)}) collective-permute-start(f32[560,128]{1,0:T(8,128)S(1)} %get-tuple-element.44), channel_id=1, source_target_pairs={{1,0},{2,1},{3,2},{4,3},{5,4},{6,5},{7,6},{0,7},{9,8},{10,9},{11,1... | collective-permute-start | bytes 860168 | tf_op jit(solution)/shard_map/ppermute | solution.py:543
  55.6 55.5 %all-to-all-start.2 = ((f32[8,16,4,8,128]{4,3,2,1,0:T(8,128)}), f32[8,16,4,8,128]{4,3,2,1,0:T(8,128)}, u32[]{:S(2)}, u32[]{:S(2)}) async-start(f32[8,16,4,8,128]{4,3,2,1,0:T(8,128)} %bitcast.21), calls=%async_computation.2 | async-start | bytes 4194304 | tf_op jit(solution)/shard_map/all_to_all | solution.py:602
  66.5 11.3 %collective-permute-start.4 = (f32[2,80,128]{2,1,0:T(8,128)S(1)}, f32[2,80,128]{2,1,0:T(8,128)S(1)}, u32[]{:S(2)}, u32[]{:S(2)}) collective-permute-start(f32[2,80,128]{2,1,0:T(8,128)S(1)} %get-tuple-element.47), channel_id=1, source_target_pairs={{0,8},{8,16},{16,24},{1,9},{9,17},{17,25},{2,10},{10,18},{18,26},{... | collective-permute-start | bytes 245768 | tf_op jit(solution)/shard_map/ppermute | solution.py:537
  69.2 8.5 %collective-permute-start.5 = (f32[2,80,128]{2,1,0:T(8,128)S(1)}, f32[2,80,128]{2,1,0:T(8,128)S(1)}, u32[]{:S(2)}, u32[]{:S(2)}) collective-permute-start(f32[2,80,128]{2,1,0:T(8,128)S(1)} %get-tuple-element.48), channel_id=1, source_target_pairs={{8,0},{16,8},{24,16},{9,1},{17,9},{25,17},{10,2},{18,10},{26,18},{... | collective-permute-start | bytes 245768 | tf_op jit(solution)/shard_map/ppermute | solution.py:537
  82.0 15.1 %copy-start.22 = (f32[2240,128]{1,0:T(8,128)S(1)}, f32[2240,128]{1,0:T(8,128)}, u32[]{:S(2)}) copy-start(f32[2240,128]{1,0:T(8,128)} %copy-done.21) | copy-start | bytes 3440644
  112.7 19.0 %copy-start.7 = (f32[1024,128]{1,0:T(8,128)S(1)}, f32[1024,128]{1,0:T(8,128)}, u32[]{:S(2)}) copy-start(f32[1024,128]{1,0:T(8,128)} %get-tuple-element.39.low.refs_6_) | copy-start | bytes 1572868
  112.7 19.0 %copy-start.9 = (f32[1024,128]{1,0:T(8,128)S(1)}, f32[1024,128]{1,0:T(8,128)}, u32[]{:S(2)}) copy-start(f32[1024,128]{1,0:T(8,128)} %get-tuple-element.40.high.refs_7_) | copy-start | bytes 1572868
  112.7 19.0 %copy-start.14 = (f32[5,288,128]{2,1,0:T(8,128)S(1)}, f32[5,288,128]{2,1,0:T(8,128)}, u32[]{:S(2)}) copy-start(f32[5,288,128]{2,1,0:T(8,128)} %copy-done.13) | copy-start | bytes 2211844
  112.7 19.0 %copy-start.20 = (f32[2240,128]{1,0:T(8,128)S(1)}, f32[2240,128]{1,0:T(8,128)}, u32[]{:S(2)}) copy-start(f32[2240,128]{1,0:T(8,128)} %copy-done.19) | copy-start | bytes 3440644
  115.7 16.0 %copy-start.2 = (f32[2,2048,128]{2,1,0:T(8,128)S(1)}, f32[2,2048,128]{2,1,0:T(8,128)}, u32[]{:S(2)}) copy-start(f32[2,2048,128]{2,1,0:T(8,128)} %copy-done.1) | copy-start | bytes 6291460
  115.7 7.8 %collective-permute-start.6 = (f32[2,80,128]{2,1,0:T(8,128)S(1)}, f32[2,80,128]{2,1,0:T(8,128)S(1)}, u32[]{:S(2)}, u32[]{:S(2)}) collective-permute-start(f32[2,80,128]{2,1,0:T(8,128)S(1)} %get-tuple-element.55), channel_id=1, source_target_pairs={{0,8},{8,16},{16,24},{1,9},{9,17},{17,25},{2,10},{10,18},{18,26},{... | collective-permute-start | bytes 245768 | tf_op jit(solution)/shard_map/ppermute | solution.py:537
  118.6 6.3 %collective-permute-start.7 = (f32[2,80,128]{2,1,0:T(8,128)S(1)}, f32[2,80,128]{2,1,0:T(8,128)S(1)}, u32[]{:S(2)}, u32[]{:S(2)}) collective-permute-start(f32[2,80,128]{2,1,0:T(8,128)S(1)} %get-tuple-element.56), channel_id=1, source_target_pairs={{8,0},{16,8},{24,16},{9,1},{17,9},{25,17},{10,2},{18,10},{26,18},{... | collective-permute-start | bytes 245768 | tf_op jit(solution)/shard_map/ppermute | solution.py:537
  119.9 11.8 %collective-permute-start.10 = (f32[560,128]{1,0:T(8,128)S(1)}, f32[560,128]{1,0:T(8,128)S(1)}, u32[]{:S(2)}, u32[]{:S(2)}) collective-permute-start(f32[560,128]{1,0:T(8,128)S(1)} %copy-done.36), channel_id=1, source_target_pairs={{0,1},{1,2},{2,3},{3,4},{4,5},{5,6},{6,7},{7,0},{8,9},{9,10},{10,1... | collective-permute-start | bytes 860168 | tf_op jit(solution)/shard_map/ppermute | solution.py:543
  120.0 11.7 %collective-permute-start.11 = (f32[560,128]{1,0:T(8,128)S(1)}, f32[560,128]{1,0:T(8,128)S(1)}, u32[]{:S(2)}, u32[]{:S(2)}) collective-permute-start(f32[560,128]{1,0:T(8,128)S(1)} %copy-done.34), channel_id=1, source_target_pairs={{1,0},{2,1},{3,2},{4,3},{5,4},{6,5},{7,6},{0,7},{9,8},{10,9},{11,1... | collective-permute-start | bytes 860168 | tf_op jit(solution)/shard_map/ppermute | solution.py:543
  128.1 31.0 %collective-permute-start.8 = (f32[560,128]{1,0:T(8,128)S(1)}, f32[560,128]{1,0:T(8,128)S(1)}, u32[]{:S(2)}, u32[]{:S(2)}) collective-permute-start(f32[560,128]{1,0:T(8,128)S(1)} %get-tuple-element.58), channel_id=1, source_target_pairs={{0,1},{1,2},{2,3},{3,4},{4,5},{5,6},{6,7},{7,0},{8,9},{9,10},{10,1... | collective-permute-start | bytes 860168 | tf_op jit(solution)/shard_map/ppermute | solution.py:543
  128.2 17.2 %copy-start.12 = (f32[5,288,128]{2,1,0:T(8,128)S(1)}, f32[5,288,128]{2,1,0:T(8,128)}, u32[]{:S(2)}) copy-start(f32[5,288,128]{2,1,0:T(8,128)} %copy-done.10) | copy-start | bytes 2211844
  128.2 30.9 %collective-permute-start.9 = (f32[560,128]{1,0:T(8,128)S(1)}, f32[560,128]{1,0:T(8,128)S(1)}, u32[]{:S(2)}, u32[]{:S(2)}) collective-permute-start(f32[560,128]{1,0:T(8,128)S(1)} %get-tuple-element.59), channel_id=1, source_target_pairs={{1,0},{2,1},{3,2},{4,3},{5,4},{6,5},{7,6},{0,7},{9,8},{10,9},{11,1... | collective-permute-start | bytes 860168 | tf_op jit(solution)/shard_map/ppermute | solution.py:543
  159.1 27.9 %copy-start.32 = (s32[1,512]{1,0:T(1,128)S(1)}, s32[1,512]{1,0:T(1,128)}, u32[]{:S(2)}) copy-start(s32[1,512]{1,0:T(1,128)} %get-tuple-element.67.slot) | copy-start | bytes 6148
  (30 other events, 149.8 us)
